TPU v7x, 256 devices: a whole 4x4x8 slice. The times are simulated.
256 devices in a mesh: row: 16 (over z, y_lo), col: 16 (over x, y_hi, core).
Axes of the slice: x: 4, y: 4 (y_hi: 2, y_lo: 2; y = y_hi * 2 + y_lo), z: 8, core: 2. Of those that a mesh axis runs over, the one named last changes fastest.
Arguments:
- pair: bfloat16 [384, 384, 128], P('row', 'col'), may hold values from -6 to 6
- cotangent: bfloat16 [384, 384, 128], P('row', 'col'), may hold values from -6 to 6
- w_in: bfloat16 [128, 640], replicated, may hold values from -0.5 to 0.5
- w_out: bfloat16 [128, 128], replicated, may hold values from -0.5 to 0.5
- norm_params: float32 [4, 128], replicated, may hold values from 0.1 to 1.9
Outputs:
- update: bfloat16 [384, 384, 128], P('row', 'col')
- grad_pair: bfloat16 [384, 384, 128], P('row', 'col')
- grad_w_in: float32 [128, 640], replicated
- grad_w_out: float32 [128, 128], replicated
- grad_norm: float32 [4, 128], replicated
All inputs are finite; a program needn't handle non-finite values.
Results may differ from a plain program's by a relative error of at most 0.012.
Values may be sent and summed in bfloat16 or wider, within the bound.
No kernel may reach another device: no remote copies, remote signals or barrier semaphores. Data moves between devices by JAX's collectives and lax.ppermute only.
A program may use at most 64 MiB of HBM per device.

v0:
```python
import jax
import jax.numpy as jnp
from jax import lax
from jax.sharding import PartitionSpec as P


def norm_fwd(v, gain, bias):
    mu = jnp.mean(v, axis=-1, keepdims=True)
    var = jnp.mean((v - mu) ** 2, axis=-1, keepdims=True)
    rstd = 1.0 / jnp.sqrt(var + 1e-05)
    hat = (v - mu) * rstd
    return (hat * gain + bias, hat, rstd)


def norm_back(dout, hat, rstd, gain):
    inner = dout * gain
    return rstd * (
        inner
        - jnp.mean(inner, axis=-1, keepdims=True)
        - hat * jnp.mean(inner * hat, axis=-1, keepdims=True)
    )


def shards(pair, cotangent, w_in, w_out, norm_params):
    f32 = jnp.float32
    bf16 = jnp.bfloat16
    width = w_out.shape[0]
    n_all = pair.shape[0] * lax.axis_size("row")
    zn_f, hat0, rstd0 = norm_fwd(pair.astype(f32), norm_params[0], norm_params[1])
    zn = zn_f.astype(bf16)
    proj = jnp.einsum("ijc,cd->ijd", zn, w_in, preferred_element_type=f32)
    p0, p1, p2, p3, p4 = [proj[..., m * width : (m + 1) * width] for m in range(5)]
    s1 = jax.nn.sigmoid(p1)
    s3 = jax.nn.sigmoid(p3)
    gate = jax.nn.sigmoid(p4)
    a_val = (s1 * p0).astype(bf16)
    b_val = (s3 * p2).astype(bf16)
    a_full = lax.all_gather(a_val, "col", axis=1, tiled=True)
    b_below = lax.all_gather(b_val, "row", axis=0, tiled=True)
    b_turned = lax.all_to_all(b_below, "col", split_axis=0, concat_axis=1, tiled=True)
    x = jnp.einsum("ikc,jkc->ijc", a_full, b_turned, preferred_element_type=f32)
    xn_f, hat2, rstd2 = norm_fwd(x, norm_params[2], norm_params[3])
    xn = xn_f.astype(bf16)
    y = jnp.einsum("ijc,cd->ijd", xn, w_out, preferred_element_type=f32)
    update = (gate * y).astype(bf16)
    dout = cotangent.astype(f32)
    dy = (dout * gate).astype(bf16)
    dp4 = dout * y * gate * (1.0 - gate)
    local_w_out = jnp.einsum("ijc,ijd->cd", xn, dy, preferred_element_type=f32) / n_all
    dxn = jnp.einsum("ijd,cd->ijc", dy, w_out, preferred_element_type=f32)
    local_mid = jnp.stack([jnp.sum(dxn * hat2, axis=(0, 1)), jnp.sum(dxn, axis=(0, 1))]) / n_all
    grad_w_out, grad_mid = lax.psum((local_w_out, local_mid), ("row", "col"))
    dx = norm_back(dxn, hat2, rstd2, norm_params[2]).astype(bf16)
    da_part = jnp.einsum("ijc,jkc->ikc", dx, b_turned, preferred_element_type=f32)
    da = lax.psum_scatter(
        da_part.astype(jnp.bfloat16), "col", scatter_dimension=1, tiled=True
    ).astype(jnp.float32)
    db_part = jnp.einsum("ijc,ikc->jkc", dx, a_full, preferred_element_type=f32).astype(bf16)
    db_moved = lax.all_to_all(db_part, "col", split_axis=1, concat_axis=0, tiled=True)
    db = lax.psum_scatter(
        db_moved.astype(f32).astype(jnp.bfloat16), "row", scatter_dimension=0, tiled=True
    ).astype(jnp.float32)
    d_all = jnp.concatenate(
        [da * s1, da * p0 * s1 * (1.0 - s1), db * s3, db * p2 * s3 * (1.0 - s3), dp4], axis=-1
    ).astype(bf16)
    local_w_in = jnp.einsum("ijc,ijd->cd", zn, d_all, preferred_element_type=f32) / n_all
    dzn = jnp.einsum("ijd,cd->ijc", d_all, w_in, preferred_element_type=f32)
    grad_pair = norm_back(dzn, hat0, rstd0, norm_params[0]).astype(bf16)
    local_first = jnp.stack([jnp.sum(dzn * hat0, axis=(0, 1)), jnp.sum(dzn, axis=(0, 1))]) / n_all
    grad_w_in, grad_first = lax.psum((local_w_in, local_first), ("row", "col"))
    grad_norm = jnp.concatenate([grad_first, grad_mid], axis=0)
    return (update, grad_pair, grad_w_in, grad_w_out, grad_norm)


def solution(mesh):
    placed = (P("row", "col", None), P("row", "col", None), P(), P(), P())
    return jax.shard_map(
        shards,
        mesh=mesh,
        in_specs=placed,
        out_specs=(P("row", "col", None), P("row", "col", None), P(), P(), P()),
        check_vma=False,
    )
```

profile of v0, /device:TPU:1, one launch (start us, length us, event | category | flops | bytes accessed | tf_op | source)
XLA Modules:
  0.0 682.3 jit_solution(1608786965070010568)
XLA Ops:
  7.2 1.1 convert_reduce_fusion
  8.3 1.2 fusion.15
  10.4 1.4 fusion.40
  11.8 1.1 copy-done.1
  14.6 69.2 %all-gather.3.cloned.1.call-done = bf16[384,24,128]{2,1,0:T(8,128)(2,1)} async-done(((bf16[24,24,128]{2,1,0:T(8,128)(2,1)}), bf16[384,24,128]{2,1,0:T(8,128)(2,1)}) %all-gather.3.cloned.1.call-update) | async-done | bytes 2359312 | tf_op jit(solution)/shard_map/all_gather | solution.py:39
  83.8 15.7 %all-to-all-start = ((bf16[384,24,128]{2,1,0:T(8,128)(2,1)}), bf16[384,24,128]{2,1,0:T(8,128)(2,1)}, u32[]{:S(2)}, u32[]{:S(2)}) async-start(bf16[384,24,128]{2,1,0:T(8,128)(2,1)} %all-gather.3.cloned.1.call-done), calls=%async_computation | async-start | bytes 4718592 | tf_op jit(solution)/shard_map/all_to_all | solution.py:40
  99.6 60.8 %all-gather.5.cloned.1.call-done = bf16[24,384,128]{2,1,0:T(8,128)(2,1)} async-done(((bf16[24,24,128]{2,1,0:T(8,128)(2,1)}), bf16[24,384,128]{2,1,0:T(8,128)(2,1)}) %all-gather.5.cloned.1.call-update) | async-done | bytes 2359312 | tf_op jit(solution)/shard_map/all_gather | solution.py:38
  160.3 3.3 copy.100
  163.7 3.7 copy.98
  167.4 4.5 copy.99
  171.9 4.0 bitcast_reduce_fusion
  175.8 1.9 copy.101
  178.1 1.4 multiply_reduce_fusion
  180.4 4.1 convert_bitcast_fusion.1
  184.4 4.7 copy.120
  189.1 3.7 copy.131
  192.8 2.3 convert_bitcast_fusion
  195.2 3.6 copy.115
  198.8 35.1 %all_to_all.36 = bf16[24,384,128]{2,0,1:T(8,128)(2,1)S(1)} all-to-all(bf16[24,384,128]{2,0,1:T(8,128)(2,1)S(1)} %copy.115), channel_id=1, replica_groups=mesh['row'=16,'col'=16] {'col'}, dimensions={1} | all-to-all | bytes 4718592 | tf_op jit(solution)/shard_map/all_to_all | solution.py:59
  233.9 1.8 copy.117
  236.0 1.1 copy-done.2
  237.2 1.0 fusion.1
  238.2 1.0 multiply_convert_fusion.1
  239.3 30.1 %reduce-scatter.7.cloned.1.call-done = bf16[24,3072]{1,0:T(8,128)(2,1)} async-done(((bf16[384,3072]{1,0:T(8,128)(2,1)}), bf16[24,3072]{1,0:T(8,128)(2,1)}) %reduce-scatter.7.cloned.1.call-update) | async-done | bytes 147472
  270.6 66.4 %reduce-scatter.5.cloned.1.call-done = bf16[24,24,128]{2,1,0:T(8,128)(2,1)} async-done(((bf16[384,24,128]{2,1,0:T(8,128)(2,1)}), bf16[24,24,128]{2,1,0:T(8,128)(2,1)}) %reduce-scatter.5.cloned.1.call-update) | async-done | bytes 147472 | tf_op jit(solution)/shard_map/reduce_scatter | solution.py:60
  338.0 1.0 fusion.42
  339.7 1.3 fusion
  341.0 86.0 %all-reduce = (f32[2,128]{1,0:T(2,128)S(1)}, f32[2,128]{1,0:T(2,128)S(1)}) all-reduce(f32[2,128]{1,0:T(2,128)S(1)} %maximum_multiply_fusion.1, f32[2,128]{1,0:T(2,128)S(1)} %maximum_multiply_fusion), channel_id=1, replica_groups=mesh['row'=16,'col'=16] {'row','col'}, use_global_device_ids=true, to_apply=%region_17.0 | all-reduce | flops 512 | bytes 4096 | tf_op jit(solution)/shard_map/psum | solution.py:52
  427.6 1.0 fusion.13
  428.6 244.0 %all-reduce.4.cloned.1.call-done = (f32[128,640]{1,0:T(8,128)}, f32[128,128]{1,0:T(8,128)}) async-done(((f32[128,640]{1,0:T(8,128)}, f32[128,128]{1,0:T(8,128)}), (f32[128,640]{1,0:T(8,128)}, f32[128,128]{1,0:T(8,128)})) %all-reduce.4.cloned.1.call-update) | async-done | bytes 393232 | tf_op jit(solution)/shard_map/psum | solution.py:70
  672.6 1.7 copy.138
  674.3 1.5 copy.139
  (51 shorter events, 7.5 us)
Async XLA Ops:
  7.2 3.2 copy-start
  7.2 76.6 %all-gather.3.cloned.1.call-start = ((), (), s32[]{:S(2)}) async-start(), calls=%async_computation.4 | async-start | bytes 2506752 | tf_op jit(solution)/shard_map/all_gather | solution.py:39
  11.8 1.1 copy-start.1
  13.8 146.5 %all-gather.5.cloned.1.call-start = ((), (), s32[]{:S(2)}) async-start(), calls=%async_computation.5 | async-start | bytes 2506752 | tf_op jit(solution)/shard_map/all_gather | solution.py:38
  83.8 79.9 %all-to-all-start = ((bf16[384,24,128]{2,1,0:T(8,128)(2,1)}), bf16[384,24,128]{2,1,0:T(8,128)(2,1)}, u32[]{:S(2)}, u32[]{:S(2)}) async-start(bf16[384,24,128]{2,1,0:T(8,128)(2,1)} %all-gather.3.cloned.1.call-done), calls=%async_computation | async-start | bytes 4718592 | tf_op jit(solution)/shard_map/all_to_all | solution.py:40
  99.5 169.9 %reduce-scatter.7.cloned.1.call-start = ((), (), s32[]{:S(2)}) async-start(), calls=%async_computation.7 | async-start | bytes 2506752
  171.9 6.2 copy-start.6
  171.9 6.2 copy-start.8
  177.7 1.8 copy-start.4
  192.8 144.2 %reduce-scatter.5.cloned.1.call-start = ((), (), s32[]{:S(2)}) async-start(), calls=%async_computation.6 | async-start | bytes 2506752 | tf_op jit(solution)/shard_map/reduce_scatter | solution.py:60
  235.7 1.4 copy-start.2
  235.7 1.4 copy-start.5
  235.7 1.4 copy-start.7
  235.7 2.5 copy-start.9
  235.8 436.8 %all-reduce.4.cloned.1.call-start = ((), (), s32[]{:S(2)}) async-start(), calls=%async_computation.8 | async-start | bytes 786432 | tf_op jit(solution)/shard_map/psum | solution.py:70
  239.3 100.0 %copy-start.3 = (bf16[24,24,128]{2,1,0:T(8,128)(2,1)S(1)}, bf16[24,24,128]{2,1,0:T(8,128)(2,1)}, u32[]{:S(2)}) copy-start(bf16[24,24,128]{2,1,0:T(8,128)(2,1)} %param.5) | copy-start | bytes 442372
Sparse Core Ops, SparseCore 0:
  14.0 69.7 all-gather.2
  86.9 73.3 all-gather.4
  192.9 76.4 reduce-scatter.6
  271.8 65.1 reduce-scatter.4
  427.7 244.8 all-reduce.3
where the time goes:
time: 683 us; the launch traced here: 682 us
  waiting for transfers between devices  471 us (69%)
  blocking collectives  121 us (18%)
  local copies, waits for them, and re-layouts  35 us (5%)
  matrix products  17 us (2%)
  starting transfers between devices  16.1 us (2%)
  between operations  14 us (2%)
  other arithmetic  7.89 us (1%)
    psum x1, waiting for transfers between devices, shards(): grad_w_in, grad_first = lax.psum((local_w_in, local_first), ('row', 'col'))  244 us
    psum x1, blocking collectives, shards(): grad_w_out, grad_mid = lax.psum((local_w_out, local_mid), ('row', 'col'))  86 us
    all_gather x1, waiting for transfers between devices, shards(): b_below = lax.all_gather(b_val, 'row', axis=0, tiled=True)  69.2 us
    reduce_scatter x1, waiting for transfers between devices, shards(): lax.psum_scatter(db_moved.astype(f32).astype(jnp.bfloat16), 'row', scatte...  66.4 us
    all_gather x1, waiting for transfers between devices, shards(): a_full = lax.all_gather(a_val, 'col', axis=1, tiled=True)  60.8 us
    all_to_all x1, blocking collectives, shards(): lax.all_to_all(db_part, 'col', split_axis=1, concat_axis=0, tiled=True)  35.1 us
    unnamed x6, waiting for transfers between devices  30.9 us
    all_to_all x1, starting transfers between devices, shards(): lax.all_to_all(b_below, 'col', split_axis=0, concat_axis=1, tiled=True)  15.7 us
  transfers between devices with their start and end apart: 6, of which 5 were waited for; matrix products, arithmetic and copies ran while one was open for 2% of the time, Pallas kernels for 0%

commit v1 on v0

v1 whole, which is shorter than its diff:
```python
import jax
import jax.numpy as jnp
from jax import lax
from jax.experimental import pallas as pl
from jax.experimental.pallas import tpu as pltpu
from jax.sharding import Mesh
from jax.sharding import PartitionSpec as P

F32 = jnp.float32
BF16 = jnp.bfloat16
EPS = 1e-05
ROWS = 16
COLS = 8
CHIPS = 128
TILE = 24
WIDE = 32
TROWS = 6
POS = TILE * WIDE
C = 128


def dot(x, y, cx, cy):
    return lax.dot_general(x, y, (((cx,), (cy,)), ((), ())), preferred_element_type=F32)


def block_turn(parts):
    lane = lax.broadcasted_iota(jnp.int32, parts[0].shape, 1)
    for bit, shift in ((1, 32), (2, 64)):
        low = (lane & shift) == 0
        out = [None] * 4
        for i in range(4):
            if i & bit:
                continue
            x, y = parts[i], parts[i | bit]
            out[i] = jnp.where(low, x, pltpu.roll(y, shift, 1))
            out[i | bit] = jnp.where(low, pltpu.roll(x, 128 - shift, 1), y)
        parts = out
    return parts


def norm_lanes(v):
    mu = jnp.mean(v, axis=-1, keepdims=True)
    d = v - mu
    rstd = 1.0 / jnp.sqrt(jnp.mean(d * d, axis=-1, keepdims=True) + EPS)
    return d * rstd, rstd


def padded(tile):
    wide = jnp.concatenate([tile.astype(F32), jnp.zeros((TILE, WIDE - TILE, C), F32)], axis=1)
    return wide.reshape(POS, C)


def zero_rows(scr, rows, used):
    for t in range(used, rows):
        scr[pl.ds(t, CHIPS, stride=rows), :] = jnp.zeros((CHIPS, 128), F32)


def first_kernel(pair_ref, w_ref, norm_ref, send_ref, zn_ref, scr):
    hat, _ = norm_lanes(pair_ref[...].astype(F32))
    zn = padded(hat * norm_ref[0:1, :][None] + norm_ref[1:2, :][None]).astype(BF16)
    zn_ref[...] = zn
    for m in range(2):
        w = w_ref[:, 2 * m * C : (2 * m + 2) * C]
        p = dot(w, zn, 0, 1)
        val = jax.nn.sigmoid(p[C:]) * p[:C]
        for t in range(TROWS):
            scr[pl.ds(TROWS * m + t, CHIPS, stride=16), :] = val[:, t * 128 : (t + 1) * 128]
    zero_rows(scr, 16, 2 * TROWS)
    send_ref[...] = scr[...].astype(BF16).reshape(CHIPS, 16, 128)


def gather_rows(scr, rows, offset, dst):
    for g in range(2):
        for t in range(TROWS):
            parts = [scr[pl.ds((4 * g + u) * rows + offset + t, ROWS, stride=COLS * rows), :] for u in range(4)]
            for v, o in enumerate(block_turn(parts)):
                dst[pl.ds(16 * (4 * t + v), 16), g * 128 : (g + 1) * 128] = o.astype(BF16)


def scatter_rows(val, scr, rows, offset):
    for g in range(2):
        for t in range(TROWS):
            parts = [val[16 * (4 * t + v) : 16 * (4 * t + v) + 16, g * 128 : (g + 1) * 128] for v in range(4)]
            for u, o in enumerate(block_turn(parts)):
                scr[pl.ds((4 * g + u) * rows + offset + t, ROWS, stride=COLS * rows), :] = o


def second_kernel(core_ref, own_ref, sib_ref, send_ref, a_ref, b_ref, scr, a_sib, bscr, b_sib, sscr):
    core = core_ref[0]
    total = None
    for src, a_dst, b_dst in ((own_ref, a_ref, b_ref), (sib_ref, a_sib, b_sib)):
        scr[...] = src[...].astype(F32).reshape(CHIPS * 16, 128)
        gather_rows(scr, 16, 0, a_dst)
        bscr[...] = jnp.zeros(bscr.shape, F32)
        for g in range(2):
            for t in range(TROWS):
                parts = [scr[pl.ds((4 * g + u) * 16 + TROWS + t, ROWS, stride=COLS * 16), :] for u in range(4)]
                for v, o in enumerate(block_turn(parts)):
                    bscr[pl.ds(512 * g + 4 * t + v, ROWS, stride=WIDE), :] = o
        for g in range(2):
            b_dst[:, :, :, g * 128 : (g + 1) * 128] = bscr[512 * g : 512 * g + 512, :].astype(BF16).reshape(COLS, 2, WIDE, 128)
        part = dot(a_dst[...], b_dst[:, core].reshape(COLS * WIDE, 256), 1, 1)
        total = part if total is None else total + part
    scatter_rows(total, sscr, 8, 0)
    zero_rows(sscr, 8, TROWS)
    send_ref[...] = sscr[...].astype(BF16).reshape(CHIPS, 8, 128)


def column(row):
    return jnp.broadcast_to(row, (C, C)).T[:, :1]


def lane_sums(val):
    part = val[:, :128]
    for t in range(1, TROWS):
        part = part + val[:, t * 128 : (t + 1) * 128]
    return jnp.sum(part.T, axis=0, keepdims=True)


def third_kernel(recv_ref, zn_ref, cot_ref, w4_ref, wo_ref, norm_ref, send_ref, upd_ref, dp4_ref, gwo_ref, mid_ref, scr):
    scr[...] = recv_ref[...].astype(F32).reshape(CHIPS * 8, 128)
    x = jnp.concatenate([scr[pl.ds(t, CHIPS, stride=8), :] for t in range(TROWS)], axis=1)
    gain, bias = column(norm_ref[2:3, :]), column(norm_ref[3:4, :])
    mu = jnp.mean(x, axis=0, keepdims=True)
    d = x - mu
    rstd = 1.0 / jnp.sqrt(jnp.mean(d * d, axis=0, keepdims=True) + EPS)
    hat = d * rstd
    xn = (hat * gain + bias).astype(BF16)
    y = dot(wo_ref[...], xn, 0, 0)
    gate = jax.nn.sigmoid(dot(w4_ref[...], zn_ref[...], 0, 1))
    upd = (gate * y).T.reshape(TILE, WIDE, C)[:, :TILE, :]
    upd_ref[...] = upd.astype(BF16)
    cot = padded(cot_ref[...]).T
    cg = cot * gate
    dy = cg.astype(BF16)
    dp4_ref[...] = (cg * y * (1.0 - gate)).astype(BF16)
    gwo_ref[...] = dot(xn, dy, 1, 1)
    dxn = dot(wo_ref[...], dy, 1, 0)
    mid_ref[0:1, :] = lane_sums(dxn * hat)
    mid_ref[1:2, :] = lane_sums(dxn)
    mid_ref[2:8, :] = jnp.zeros((6, 128), F32)
    e = dxn * gain
    dx = rstd * (e - jnp.mean(e, axis=0, keepdims=True) - hat * jnp.mean(e * hat, axis=0, keepdims=True))
    for t in range(TROWS):
        scr[pl.ds(t, CHIPS, stride=8), :] = dx[:, t * 128 : (t + 1) * 128]
    zero_rows(scr, 8, TROWS)
    send_ref[...] = scr[...].astype(BF16).reshape(CHIPS, 8, 128)


def fourth_kernel(core_ref, own_ref, sib_ref, a_ref, b_ref, send_ref, scr, d_ref, dbscr, sscr):
    core = core_ref[0]
    da = None
    for src, side in ((own_ref, core), (sib_ref, 1 - core)):
        scr[...] = src[...].astype(F32).reshape(CHIPS * 8, 128)
        gather_rows(scr, 8, 0, d_ref)
        dx = d_ref[...]
        part = dot(dx, b_ref[:, side].reshape(COLS * WIDE, 256), 1, 0)
        da = part if da is None else da + part
        db = dot(dx, a_ref[...], 0, 0)
        for g in range(2):
            dbscr[pl.ds(256 * g, 256), :] = db[:, g * 128 : (g + 1) * 128]
        for g in range(2):
            for t in range(TROWS):
                parts = [dbscr[pl.ds(256 * g + 4 * t + v, COLS, stride=WIDE), :] for v in range(4)]
                for u, o in enumerate(block_turn(parts)):
                    sscr[pl.ds(side * 128 + (4 * g + u) * 16 + TROWS + t, COLS, stride=256), :] = o
    scatter_rows(da, sscr, 16, 0)
    zero_rows(sscr, 16, 2 * TROWS)
    send_ref[...] = sscr[...].astype(BF16).reshape(CHIPS, 16, 128)


def fifth_kernel(recv_ref, zn_ref, pair_ref, w_ref, dp4_ref, gwo_ref, mid_ref, norm_ref, gpair_ref, g_ref, scr):
    scr[...] = recv_ref[...].astype(F32).reshape(CHIPS * 16, 128)
    zn = zn_ref[...]
    blocks = []
    for m in range(2):
        grad = jnp.concatenate([scr[pl.ds(TROWS * m + t, CHIPS, stride=16), :] for t in range(TROWS)], axis=1)
        p = dot(w_ref[:, 2 * m * C : (2 * m + 2) * C], zn, 0, 1)
        s = jax.nn.sigmoid(p[C:])
        gs = grad * s
        blocks += [gs.astype(BF16), (gs * p[:C] * (1.0 - s)).astype(BF16)]
    dp = jnp.concatenate(blocks + [dp4_ref[...]], axis=0)
    g_ref[0 : 5 * C, :] = dot(dp, zn, 1, 0)
    g_ref[5 * C : 6 * C, :] = gwo_ref[...]
    dzn = dot(w_ref[...], dp, 1, 0).T
    hat, rstd = norm_lanes(padded(pair_ref[...]))
    e = dzn * norm_ref[0:1, :]
    back = rstd * (e - jnp.mean(e, axis=-1, keepdims=True) - hat * jnp.mean(e * hat, axis=-1, keepdims=True))
    gpair_ref[...] = back.reshape(TILE, WIDE, C)[:, :TILE, :].astype(BF16)
    g_ref[6 * C : 6 * C + 8, :] = mid_ref[...]
    g_ref[6 * C + 2 : 6 * C + 3, :] = jnp.sum(dzn * hat, axis=0, keepdims=True)
    g_ref[6 * C + 3 : 6 * C + 4, :] = jnp.sum(dzn, axis=0, keepdims=True)
    g_ref[6 * C + 8 : 8 * C, :] = jnp.zeros((2 * C - 8, 128), F32)


def call(kernel, outs, scratch, *args, scalars=0):
    vmem = pl.BlockSpec(memory_space=pltpu.VMEM)
    smem = pl.BlockSpec(memory_space=pltpu.SMEM)
    return pl.pallas_call(
        kernel,
        out_shape=[jax.ShapeDtypeStruct(s, t) for s, t in outs],
        in_specs=[smem] * scalars + [vmem] * (len(args) - scalars),
        out_specs=[vmem] * len(outs),
        scratch_shapes=[pltpu.VMEM(s, t) for s, t in scratch],
        compiler_params=pltpu.CompilerParams(vmem_limit_bytes=40 * 1024 * 1024),
    )(*args)


def shards(pair, cotangent, w_in, w_out, norm_params):
    chips = ("row", "q")
    swap = [(0, 1), (1, 0)]

    def turn(x):
        return lax.all_to_all(x, chips, split_axis=0, concat_axis=0, tiled=True)

    core = lax.axis_index("core").astype(jnp.int32).reshape(1)
    send, zn = call(
        first_kernel, [((CHIPS, 16, 128), BF16), ((POS, C), BF16)], [((CHIPS * 16, 128), F32)], pair, w_in, norm_params
    )
    own = turn(send)
    sib = lax.ppermute(own, "core", swap)
    send, a_own, b_own = call(
        second_kernel,
        [((CHIPS, 8, 128), BF16), ((384, 256), BF16), ((COLS, 2, WIDE, 256), BF16)],
        [
            ((CHIPS * 16, 128), F32),
            ((384, 256), BF16),
            ((1024, 128), F32),
            ((COLS, 2, WIDE, 256), BF16),
            ((CHIPS * 8, 128), F32),
        ],
        core,
        own,
        sib,
        scalars=1,
    )
    recv = turn(send)
    send, update, dp4, gwo, mid = call(
        third_kernel,
        [
            ((CHIPS, 8, 128), BF16),
            ((TILE, TILE, C), BF16),
            ((C, POS), BF16),
            ((C, C), F32),
            ((8, 128), F32),
        ],
        [((CHIPS * 8, 128), F32)],
        recv,
        zn,
        cotangent,
        w_in[:, 4 * C :],
        w_out,
        norm_params,
    )
    own = turn(send)
    sib = lax.ppermute(own, "core", swap)
    (send,) = call(
        fourth_kernel,
        [((CHIPS, 16, 128), BF16)],
        [((CHIPS * 8, 128), F32), ((384, 256), BF16), ((512, 128), F32), ((CHIPS * 16, 128), F32)],
        core,
        own,
        sib,
        a_own,
        b_own,
        scalars=1,
    )
    recv = turn(send)
    grad_pair, grads = call(
        fifth_kernel,
        [((TILE, TILE, C), BF16), ((8 * C, 128), F32)],
        [((CHIPS * 16, 128), F32)],
        recv,
        zn,
        pair,
        w_in,
        dp4,
        gwo,
        mid,
        norm_params,
    )
    mine = jnp.sum(turn(grads.reshape(CHIPS, 8, 128)), axis=0)
    mine = (mine + lax.ppermute(mine, "core", swap)) / 384.0
    full = turn(jnp.broadcast_to(mine[None], (CHIPS, 8, 128))).reshape(8 * C, 128)
    grad_w_in = full[: 5 * C].T
    grad_w_out = full[5 * C : 6 * C]
    norms = full[6 * C : 6 * C + 4]
    grad_norm = jnp.concatenate([norms[2:4], norms[0:2]], axis=0)
    return (update, grad_pair, grad_w_in, grad_w_out, grad_norm)


def solution(mesh):
    fine = Mesh(mesh.devices.reshape(ROWS, COLS, 2), ("row", "q", "core"))
    placed = (P("row", ("q", "core"), None), P("row", ("q", "core"), None), P(), P(), P())
    return jax.shard_map(shards, mesh=fine, in_specs=placed, out_specs=placed, check_vma=False)
```

time: 683 us -> 176 us (0.26)
  waiting for transfers between devices: 471 us -> 15.5 us
  local copies, waits for them, and re-layouts: 35 us -> 4.12 us
  matrix products: 17 us -> 0 us
  between operations: 14 us -> 0.73 us
  Pallas kernels: 0 us -> 12.4 us
  other arithmetic: 7.89 us -> 0.72 us
    psum x1 -> x0, waiting for transfers between devices: 244 us -> none  [shards(): grad_w_in, grad_first = lax.psum((local_w_in, local_first), ('row', 'col'))]
    all_gather x2 -> x0, waiting for transfers between devices: 130 us -> none  [the longest x1 69.2 us: shards(): b_below = lax.all_gather(b_val, 'row', axis=0, tiled=True)]
    psum x1 -> x0, blocking collectives: 86 us -> none  [shards(): grad_w_out, grad_mid = lax.psum((local_w_out, local_mid), ('row', 'col'))]
    all_to_all x1 -> x5, blocking collectives: 35.1 us -> 121 us  [turn(): return lax.all_to_all(x, chips, split_axis=0, concat_axis=0, tiled=True)]
    reduce_scatter x1 -> x0, waiting for transfers between devices: 66.4 us -> none  [shards(): lax.psum_scatter(db_moved.astype(f32).astype(jnp.bfloat16), 'row', scatte...]
    unnamed x6 -> x0, waiting for transfers between devices: 30.9 us -> none
    dot_general x9 -> x0, matrix products: 17 us -> none  [the longest x1 4.08 us: shards(): jnp.einsum('ijc,jkc->ikc', dx, b_turned, preferred_element_type=f32)]
    pallas_call x0 -> x5, Pallas kernels: none -> 12.4 us  [call(): pl.pallas_call(kernel, out_shape=[jax.ShapeDtypeStruct(s, t) for s, t in...]
  transfers between devices with their start and end apart: 6 -> 4, of which waited for: 5 -> 4; matrix products, arithmetic and copies ran while one was open for 2% -> 0% of each run, Pallas kernels for 0% -> 0%
where the time goes in v1:
time: 176 us; the launch traced here: 173 us
  blocking collectives  121 us (69%)
  starting transfers between devices  19.2 us (11%)
  waiting for transfers between devices  15.5 us (9%)
  Pallas kernels  12.4 us (7%)
  local copies, waits for them, and re-layouts  4.12 us (2%)
    all_to_all x5, blocking collectives, turn(): return lax.all_to_all(x, chips, split_axis=0, concat_axis=0, tiled=True)  121 us
    pallas_call x5, Pallas kernels, call(): pl.pallas_call(kernel, out_shape=[jax.ShapeDtypeStruct(s, t) for s, t in...  12.4 us
    all_to_all x1, waiting for transfers between devices, turn(): return lax.all_to_all(x, chips, split_axis=0, concat_axis=0, tiled=True)  12 us
    all_to_all x1, starting transfers between devices, turn(): return lax.all_to_all(x, chips, split_axis=0, concat_axis=0, tiled=True)  7.56 us
    ppermute x2, starting transfers between devices, shards(): sib = lax.ppermute(own, 'core', swap)  6.98 us
    ppermute x1, starting transfers between devices, shards(): mine = (mine + lax.ppermute(mine, 'core', swap)) / 384.0  4.62 us
  transfers between devices with their start and end apart: 4, of which 4 were waited for; matrix products, arithmetic and copies ran while one was open for 0% of the time, Pallas kernels for 0%

profile of v1, /device:TPU:1, one launch (start us, length us, event | category | flops | bytes accessed | tf_op | source)
XLA Modules:
  0.0 173.4 jit_solution(17445272710260717263)
XLA Ops:
  0.6 0.0 copy-start
  0.6 0.9 copy-done
  1.6 0.9 copy-done.2
  2.5 0.7 copy-done.6
  3.1 1.0 shard_map.92
  4.1 32.1 %all_to_all.30.own_ref = bf16[128,16,128]{2,1,0:T(8,128)(2,1)S(1)} all-to-all(bf16[128,16,128]{2,1,0:T(8,128)(2,1)S(1)} %get-tuple-element.17), channel_id=1, replica_groups=mesh['row'=16,'q'=8,'core'=2] {'row','q'}, dimensions={0} | all-to-all | bytes 1048576 | tf_op jit(solution)/shard_map/all_to_all | solution.py:214
  36.2 3.5 %collective-permute-start = (bf16[128,16,128]{2,1,0:T(8,128)(2,1)S(1)}, bf16[128,16,128]{2,1,0:T(8,128)(2,1)S(1)}, u32[]{:S(2)}, u32[]{:S(2)}) collective-permute-start(bf16[128,16,128]{2,1,0:T(8,128)(2,1)S(1)} %all_to_all.30.own_ref), channel_id=1, source_target_pairs={{0,1},{1,0},{2,3},{3,2},{4,5},{5,4},{6,7},{7,6},{8,9},{9,8},{10,11... | collective-permute-start | bytes 1572872 | tf_op jit(solution)/shard_map/ppermute | solution.py:221
  39.6 1.5 collective-permute-done.sib_ref
  41.2 4.9 %shard_map.93 = (bf16[128,8,128]{2,1,0:T(8,128)(2,1)}, bf16[384,256]{1,0:T(8,128)(2,1)S(1)}, bf16[8,2,32,256]{3,2,1,0:T(8,128)(2,1)S(1)}) custom-call(s32[1]{0:T(128)} %bitcast.core_ref, bf16[128,16,128]{2,1,0:T(8,128)(2,1)S(1)} %all_to_all.30.own_ref, bf16[128,16,128]{2,1,0:T(8,128)(2,1)S(1)} %collective-permute-done.sib_ref), custom_call_target="tpu_custom_call" | custom-call | tf_op jit(solution)/shard_map/pallas_call | solution.py:199
  46.0 7.6 %all-to-all-start.1 = ((bf16[128,8,128]{2,1,0:T(8,128)(2,1)}), bf16[128,8,128]{2,1,0:T(8,128)(2,1)S(1)}, u32[]{:S(2)}, u32[]{:S(2)}) async-start(bf16[128,8,128]{2,1,0:T(8,128)(2,1)} %get-tuple-element.18), calls=%async_computation.1 | async-start | bytes 524288 | tf_op jit(solution)/shard_map/all_to_all | solution.py:214
  53.6 0.0 copy-done.1
  53.6 0.0 copy-start.5
  53.6 0.0 copy-start.7
  53.7 12.0 %all-to-all-done.1.recv_ref = bf16[128,8,128]{2,1,0:T(8,128)(2,1)S(1)} async-done(((bf16[128,8,128]{2,1,0:T(8,128)(2,1)}), bf16[128,8,128]{2,1,0:T(8,128)(2,1)S(1)}, u32[]{:S(2)}, u32[]{:S(2)}) %all-to-all-start.1) | async-done | bytes 262176 | tf_op jit(solution)/shard_map/all_to_all | solution.py:214
  65.6 0.0 copy-done.4
  65.6 0.0 copy-done.5
  65.6 1.5 shard_map.94
  67.2 18.9 %all_to_all.31.own_ref = bf16[128,8,128]{2,1,0:T(8,128)(2,1)S(1)} all-to-all(bf16[128,8,128]{2,1,0:T(8,128)(2,1)S(1)} %get-tuple-element.21), channel_id=1, replica_groups=mesh['row'=16,'q'=8,'core'=2] {'row','q'}, dimensions={0} | all-to-all | bytes 524288 | tf_op jit(solution)/shard_map/all_to_all | solution.py:214
  86.1 3.5 %collective-permute-start.1 = (bf16[128,8,128]{2,1,0:T(8,128)(2,1)S(1)}, bf16[128,8,128]{2,1,0:T(8,128)(2,1)S(1)}, u32[]{:S(2)}, u32[]{:S(2)}) collective-permute-start(bf16[128,8,128]{2,1,0:T(8,128)(2,1)S(1)} %all_to_all.31.own_ref), channel_id=1, source_target_pairs={{0,1},{1,0},{2,3},{3,2},{4,5},{5,4},{6,7},{7,6},{8,9},{9,8},{10,11... | collective-permute-start | bytes 786440 | tf_op jit(solution)/shard_map/ppermute | solution.py:256
  89.6 1.2 collective-permute-done.1.sib_ref
  90.8 3.1 %shard_map.95 = bf16[128,16,128]{2,1,0:T(8,128)(2,1)S(1)} custom-call(s32[1]{0:T(128)} %bitcast.core_ref, bf16[128,8,128]{2,1,0:T(8,128)(2,1)S(1)} %all_to_all.31.own_ref, bf16[128,8,128]{2,1,0:T(8,128)(2,1)S(1)} %collective-permute-done.1.sib_ref, bf16[384,256]{1,0:T(8,128)(2,1)S(1)} %get-tuple-element.22.a_ref, ...), custom_call_target="tpu_custom_call" | custom-call | tf_op jit(solution)/shard_map/pallas_call | solution.py:199
  93.8 0.0 copy-start.3
  93.9 22.7 %all_to_all.32.recv_ref = bf16[128,16,128]{2,1,0:T(8,128)(2,1)S(1)} all-to-all(bf16[128,16,128]{2,1,0:T(8,128)(2,1)S(1)} %shard_map.95), channel_id=1, replica_groups=mesh['row'=16,'q'=8,'core'=2] {'row','q'}, dimensions={0} | all-to-all | bytes 1048576 | tf_op jit(solution)/shard_map/all_to_all | solution.py:214
  116.6 2.0 %shard_map.96 = (bf16[24,24,128]{2,1,0:T(8,128)(2,1)}, f32[1024,128]{1,0:T(8,128)S(1)}) custom-call(bf16[128,16,128]{2,1,0:T(8,128)(2,1)S(1)} %all_to_all.32.recv_ref, bf16[768,128]{1,0:T(8,128)(2,1)S(1)} %get-tuple-element.19.zn_ref, bf16[24,24,128]{2,1,0:T(8,128)(2,1)S(1)} %copy-done.3, bf16[128,640]{1,0:T(8,128)(2,1)S(1)} %copy-done.1, ...), custom_call_target="tpu_custom_call" | custom-call | tf_op jit(solution)/shard_map/pallas_call | solution.py:199
  118.6 23.5 %all_to_all.33 = f32[128,8,128]{2,1,0:T(8,128)S(1)} all-to-all(f32[128,8,128]{2,1,0:T(8,128)S(1)} %bitcast.9), channel_id=1, replica_groups=mesh['row'=16,'q'=8,'core'=2] {'row','q'}, dimensions={0} | all-to-all | bytes 1048576 | tf_op jit(solution)/shard_map/all_to_all | solution.py:214
  142.1 0.1 reduce_sum.9
  142.2 4.6 %collective-permute-start.2 = (f32[8,128]{1,0:T(8,128)S(1)}, f32[8,128]{1,0:T(8,128)S(1)}, u32[]{:S(2)}, u32[]{:S(2)}) collective-permute-start(f32[8,128]{1,0:T(8,128)S(1)} %reduce_sum.9), channel_id=1, source_target_pairs={{0,1},{1,0},{2,3},{3,2},{4,5},{5,4},{6,7},{7,6},{8,9},{9,8},{10,11... | collective-permute-start | bytes 12296 | tf_op jit(solution)/shard_map/ppermute | solution.py:283
  146.9 0.8 collective-permute-done.2
  147.7 23.5 %all_to_all.34 = f32[128,8,128]{2,1,0:T(8,128)S(1)} all-to-all(f32[128,8,128]{2,1,0:T(8,128)S(1)} %broadcast_in_dim.2), channel_id=1, replica_groups=mesh['row'=16,'q'=8,'core'=2] {'row','q'}, dimensions={0} | all-to-all | bytes 1048576 | tf_op jit(solution)/shard_map/all_to_all | solution.py:214
  171.3 0.9 copy.11
  172.2 0.6 pad_maximum_fusion
  172.8 0.6 slice_bitcast_fusion.1
  (11 shorter events, 0.1 us)
Async XLA Ops:
  0.6 0.9 copy-start
  1.5 0.9 copy-start.2
  2.5 0.7 copy-start.6
  36.2 5.0 %collective-permute-start = (bf16[128,16,128]{2,1,0:T(8,128)(2,1)S(1)}, bf16[128,16,128]{2,1,0:T(8,128)(2,1)S(1)}, u32[]{:S(2)}, u32[]{:S(2)}) collective-permute-start(bf16[128,16,128]{2,1,0:T(8,128)(2,1)S(1)} %all_to_all.30.own_ref), channel_id=1, source_target_pairs={{0,1},{1,0},{2,3},{3,2},{4,5},{5,4},{6,7},{7,6},{8,9},{9,8},{10,11... | collective-permute-start | bytes 1572872 | tf_op jit(solution)/shard_map/ppermute | solution.py:221
  46.0 7.6 %copy-start.1 = (bf16[128,640]{1,0:T(8,128)(2,1)S(1)}, bf16[128,640]{1,0:T(8,128)(2,1)}, u32[]{:S(2)}) copy-start(bf16[128,640]{1,0:T(8,128)(2,1)} %w_ref.3) | copy-start | bytes 491524
  46.0 19.6 %copy-start.4 = (bf16[24,24,128]{2,1,0:T(8,128)(2,1)S(1)}, bf16[24,24,128]{2,1,0:T(8,128)(2,1)}, u32[]{:S(2)}) copy-start(bf16[24,24,128]{2,1,0:T(8,128)(2,1)} %cot_ref.1) | copy-start | bytes 442372
  46.0 19.6 %all-to-all-start.1 = ((bf16[128,8,128]{2,1,0:T(8,128)(2,1)}), bf16[128,8,128]{2,1,0:T(8,128)(2,1)S(1)}, u32[]{:S(2)}, u32[]{:S(2)}) async-start(bf16[128,8,128]{2,1,0:T(8,128)(2,1)} %get-tuple-element.18), calls=%async_computation.1 | async-start | bytes 524288 | tf_op jit(solution)/shard_map/all_to_all | solution.py:214
  53.6 12.0 %copy-start.5 = (bf16[128,128]{1,0:T(8,128)(2,1)S(1)}, bf16[128,128]{1,0:T(8,128)(2,1)}, u32[]{:S(2)}) copy-start(bf16[128,128]{1,0:T(8,128)(2,1)} %wo_ref.1) | copy-start | bytes 98308
  53.6 12.0 %copy-start.7 = (f32[4,128]{1,0:T(4,128)S(1)}, f32[4,128]{1,0:T(4,128)}, u32[]{:S(2)}) copy-start(f32[4,128]{1,0:T(4,128)} %norm_ref.5) | copy-start | bytes 6148
  86.1 4.7 %collective-permute-start.1 = (bf16[128,8,128]{2,1,0:T(8,128)(2,1)S(1)}, bf16[128,8,128]{2,1,0:T(8,128)(2,1)S(1)}, u32[]{:S(2)}, u32[]{:S(2)}) collective-permute-start(bf16[128,8,128]{2,1,0:T(8,128)(2,1)S(1)} %all_to_all.31.own_ref), channel_id=1, source_target_pairs={{0,1},{1,0},{2,3},{3,2},{4,5},{5,4},{6,7},{7,6},{8,9},{9,8},{10,11... | collective-permute-start | bytes 786440 | tf_op jit(solution)/shard_map/ppermute | solution.py:256
  93.8 22.7 %copy-start.3 = (bf16[24,24,128]{2,1,0:T(8,128)(2,1)S(1)}, bf16[24,24,128]{2,1,0:T(8,128)(2,1)}, u32[]{:S(2)}) copy-start(bf16[24,24,128]{2,1,0:T(8,128)(2,1)} %pair_ref.3) | copy-start | bytes 442372
  142.2 5.4 %collective-permute-start.2 = (f32[8,128]{1,0:T(8,128)S(1)}, f32[8,128]{1,0:T(8,128)S(1)}, u32[]{:S(2)}, u32[]{:S(2)}) collective-permute-start(f32[8,128]{1,0:T(8,128)S(1)} %reduce_sum.9), channel_id=1, source_target_pairs={{0,1},{1,0},{2,3},{3,2},{4,5},{5,4},{6,7},{7,6},{8,9},{9,8},{10,11... | collective-permute-start | bytes 12296 | tf_op jit(solution)/shard_map/ppermute | solution.py:283

commit v2 on v1

v2 whole, which is shorter than its diff:
```python
import jax
import jax.numpy as jnp
from jax import lax
from jax.experimental import pallas as pl
from jax.experimental.pallas import tpu as pltpu
from jax.sharding import Mesh
from jax.sharding import PartitionSpec as P

F32 = jnp.float32
BF16 = jnp.bfloat16
EPS = 1e-05
ROWS = 16
COLS = 8
CHIPS = 128
TILE = 24
WIDE = 32
TROWS = 6
POS = TILE * WIDE
C = 128


def dot(x, y, cx, cy):
    return lax.dot_general(x, y, (((cx,), (cy,)), ((), ())), preferred_element_type=F32)


def block_turn(parts):
    lane = lax.broadcasted_iota(jnp.int32, parts[0].shape, 1)
    for bit, shift in ((1, 32), (2, 64)):
        low = (lane & shift) == 0
        out = [None] * 4
        for i in range(4):
            if i & bit:
                continue
            x, y = parts[i], parts[i | bit]
            out[i] = jnp.where(low, x, pltpu.roll(y, shift, 1))
            out[i | bit] = jnp.where(low, pltpu.roll(x, 128 - shift, 1), y)
        parts = out
    return parts


def norm_lanes(v):
    mu = jnp.mean(v, axis=-1, keepdims=True)
    d = v - mu
    rstd = 1.0 / jnp.sqrt(jnp.mean(d * d, axis=-1, keepdims=True) + EPS)
    return d * rstd, rstd


def padded(tile):
    wide = jnp.concatenate([tile.astype(F32), jnp.zeros((TILE, WIDE - TILE, C), F32)], axis=1)
    return wide.reshape(POS, C)


def first_kernel(pair_hbm, w_hbm, norm_hbm, send_ref, zn_ref, pair_ref, w_ref, norm_ref, sems):
    copies = [
        pltpu.make_async_copy(src, dst, sems.at[i])
        for i, (src, dst) in enumerate(((pair_hbm, pair_ref), (norm_hbm, norm_ref), (w_hbm, w_ref)))
    ]
    for copy in copies:
        copy.start()
    copies[0].wait()
    hat, _ = norm_lanes(pair_ref[...].astype(F32))
    copies[1].wait()
    zn = padded(hat * norm_ref[0:1, :][None] + norm_ref[1:2, :][None]).astype(BF16)
    zn_ref[...] = zn
    copies[2].wait()
    for m in range(2):
        p = dot(w_ref[:, 2 * m * C : (2 * m + 2) * C], zn, 0, 1)
        send_ref[:, m, :] = (jax.nn.sigmoid(p[C:]) * p[:C]).astype(BF16)


def unpack(src, row, t0, scr):
    for t in range(src.shape[2] // 128):
        scr[pl.ds((t0 + t) * CHIPS, CHIPS), :] = src[:, row, t * 128 : (t + 1) * 128].astype(F32)


def gather_rows(scr, t0, dst):
    for g in range(2):
        for t in range(TROWS):
            parts = [scr[pl.ds((t0 + t) * CHIPS + 4 * g + u, ROWS, stride=COLS), :] for u in range(4)]
            for v, o in enumerate(block_turn(parts)):
                dst[pl.ds(16 * (4 * t + v), 16), g * 128 : (g + 1) * 128] = o.astype(BF16)


def scatter_rows(val, scr, t0):
    for g in range(2):
        for t in range(TROWS):
            parts = [val[16 * (4 * t + v) : 16 * (4 * t + v) + 16, g * 128 : (g + 1) * 128] for v in range(4)]
            for u, o in enumerate(block_turn(parts)):
                scr[pl.ds((t0 + t) * CHIPS + 4 * g + u, ROWS, stride=COLS), :] = o


def product(core, src, a_dst, b_dst, scr, bscr):
    unpack(src, 0, 0, scr)
    unpack(src, 1, TROWS, scr)
    gather_rows(scr, 0, a_dst)
    for half in range(2 * 16):
        bscr[pl.ds(half * WIDE + TILE, WIDE - TILE), :] = jnp.zeros((WIDE - TILE, 128), F32)
    for g in range(2):
        for t in range(TROWS):
            parts = [scr[pl.ds((TROWS + t) * CHIPS + 4 * g + u, ROWS, stride=COLS), :] for u in range(4)]
            for v, o in enumerate(block_turn(parts)):
                bscr[pl.ds(512 * g + 4 * t + v, ROWS, stride=WIDE), :] = o
    for g in range(2):
        b_dst[:, :, :, g * 128 : (g + 1) * 128] = bscr[512 * g : 512 * g + 512, :].astype(BF16).reshape(COLS, 2, WIDE, 128)
    return dot(a_dst[...], b_dst[:, core].reshape(COLS * WIDE, 256), 1, 1)


def second_kernel(core_ref, src_ref, part_ref, a_ref, b_ref, scr, bscr):
    part_ref[...] = product(core_ref[0], src_ref, a_ref, b_ref, scr, bscr)


def second_kernel_sib(core_ref, src_ref, part_ref, send_ref, scr, bscr, a_ref, b_ref):
    total = part_ref[...] + product(core_ref[0], src_ref, a_ref, b_ref, scr, bscr)
    scatter_rows(total, scr, 0)
    pack(scr, 0, send_ref, 384)


def pack(scr, t0, dst, width):
    per = width // 128
    for s in range(2):
        for t in range(per):
            dst[:, s, t * 128 : (t + 1) * 128] = scr[pl.ds((t0 + s * per + t) * CHIPS, CHIPS), :].astype(BF16)


def column(row):
    return jnp.broadcast_to(row, (C, C)).T[:, :1]


def lane_sums(val):
    part = val[:, :128]
    for t in range(1, TROWS):
        part = part + val[:, t * 128 : (t + 1) * 128]
    return jnp.sum(part.T, axis=0, keepdims=True)


def third_kernel(recv_ref, zn_ref, cot_ref, w_ref, wo_ref, norm_ref, send_ref, upd_ref, dp4_ref, gwo_ref, mid_ref):
    x = jnp.concatenate([recv_ref[:, s, :].astype(F32) for s in range(2)], axis=1)
    gain, bias = column(norm_ref[2:3, :]), column(norm_ref[3:4, :])
    mu = jnp.mean(x, axis=0, keepdims=True)
    d = x - mu
    rstd = 1.0 / jnp.sqrt(jnp.mean(d * d, axis=0, keepdims=True) + EPS)
    hat = d * rstd
    xn = (hat * gain + bias).astype(BF16)
    y = dot(wo_ref[...], xn, 0, 0)
    gate = jax.nn.sigmoid(dot(w_ref[:, 4 * C :], zn_ref[...], 0, 1))
    upd = (gate * y).T.reshape(TILE, WIDE, C)[:, :TILE, :]
    upd_ref[...] = upd.astype(BF16)
    cot = padded(cot_ref[...]).T
    cg = cot * gate
    dy = cg.astype(BF16)
    dp4_ref[...] = (cg * y * (1.0 - gate)).astype(BF16)
    gwo_ref[...] = dot(xn, dy, 1, 1)
    dxn = dot(wo_ref[...], dy, 1, 0)
    mid_ref[0:1, :] = lane_sums(dxn * hat)
    mid_ref[1:2, :] = lane_sums(dxn)
    mid_ref[2:8, :] = jnp.zeros((6, 128), F32)
    e = dxn * gain
    dx = rstd * (e - jnp.mean(e, axis=0, keepdims=True) - hat * jnp.mean(e * hat, axis=0, keepdims=True))
    for half in range(2):
        send_ref[:, half, :] = dx[:, half * 384 : (half + 1) * 384].astype(BF16)


def back_product(side, src, a_ref, b_ref, scr, d_ref, dbscr, sscr):
    unpack(src, 0, 0, scr)
    unpack(src, 1, 3, scr)
    gather_rows(scr, 0, d_ref)
    dx = d_ref[...]
    db = dot(dx, a_ref[...], 0, 0)
    for g in range(2):
        dbscr[pl.ds(256 * g, 256), :] = db[:, g * 128 : (g + 1) * 128]
    for g in range(2):
        for t in range(TROWS):
            parts = [dbscr[pl.ds(256 * g + 4 * t + v, COLS, stride=WIDE), :] for v in range(4)]
            for u, o in enumerate(block_turn(parts)):
                sscr[pl.ds(t * CHIPS + 8 * side + 4 * g + u, COLS, stride=16), :] = o
    return dot(dx, b_ref[:, side].reshape(COLS * WIDE, 256), 1, 0)


def fourth_kernel(core_ref, src_ref, a_ref, b_ref, da_ref, db_ref, scr, d_ref, dbscr):
    da_ref[...] = back_product(core_ref[0], src_ref, a_ref, b_ref, scr, d_ref, dbscr, db_ref)


def fourth_kernel_sib(core_ref, src_ref, a_ref, b_ref, da_ref, db_ref, send_ref, scr, d_ref, dbscr, sscr):
    core = core_ref[0]
    da = da_ref[...] + back_product(1 - core, src_ref, a_ref, b_ref, scr, d_ref, dbscr, sscr)
    mine = (lax.broadcasted_iota(jnp.int32, (CHIPS, 128), 0) // COLS) % 2 == core
    for t in range(TROWS):
        tile = pl.ds(t * CHIPS, CHIPS)
        send_ref[:, 1, t * 128 : (t + 1) * 128] = jnp.where(mine, db_ref[tile, :], sscr[tile, :]).astype(BF16)
    scatter_rows(da, scr, 0)
    for t in range(TROWS):
        send_ref[:, 0, t * 128 : (t + 1) * 128] = scr[pl.ds(t * CHIPS, CHIPS), :].astype(BF16)


def fifth_kernel(recv_ref, zn_ref, pair_ref, w_ref, dp4_ref, gwo_ref, mid_ref, norm_ref, gpair_ref, g_ref):
    zn = zn_ref[...]
    blocks = []
    for m in range(2):
        grad = recv_ref[:, m, :].astype(F32)
        p = dot(w_ref[:, 2 * m * C : (2 * m + 2) * C], zn, 0, 1)
        s = jax.nn.sigmoid(p[C:])
        gs = grad * s
        blocks += [gs.astype(BF16), (gs * p[:C] * (1.0 - s)).astype(BF16)]
    dp = jnp.concatenate(blocks + [dp4_ref[...]], axis=0)
    g_ref[0 : 5 * C, :] = dot(dp, zn, 1, 0).astype(BF16)
    g_ref[5 * C : 6 * C, :] = gwo_ref[...].astype(BF16)
    dzn = dot(w_ref[...], dp, 1, 0).T
    hat, rstd = norm_lanes(padded(pair_ref[...]))
    e = dzn * norm_ref[0:1, :]
    back = rstd * (e - jnp.mean(e, axis=-1, keepdims=True) - hat * jnp.mean(e * hat, axis=-1, keepdims=True))
    gpair_ref[...] = back.reshape(TILE, WIDE, C)[:, :TILE, :].astype(BF16)
    first = jnp.sum(dzn * hat, axis=0, keepdims=True)
    second = jnp.sum(dzn, axis=0, keepdims=True)
    rows = jnp.concatenate([first, second, mid_ref[0:2, :], jnp.zeros((12, 128), F32)], axis=0)
    g_ref[6 * C : 6 * C + 16, :] = rows.astype(BF16)
    g_ref[6 * C + 16 : 8 * C, :] = jnp.zeros((2 * C - 16, 128), BF16)


def last_kernel(full_ref, gwi_ref, gwo_ref, gn_ref):
    for m in range(5):
        gwi_ref[:, m * C : (m + 1) * C] = full_ref[m * C : (m + 1) * C, :].astype(F32).T
    gwo_ref[...] = full_ref[5 * C : 6 * C, :].astype(F32)
    gn_ref[...] = full_ref[6 * C : 6 * C + 16, :].astype(F32)[0:4, :]


def call(kernel, outs, scratch, *args, scalars=0, anywhere=False):
    vmem = pl.BlockSpec(memory_space=pltpu.VMEM)
    smem = pl.BlockSpec(memory_space=pltpu.SMEM)
    rest = pl.BlockSpec(memory_space=pltpu.HBM) if anywhere else vmem
    return pl.pallas_call(
        kernel,
        out_shape=[jax.ShapeDtypeStruct(s, t) for s, t in outs],
        in_specs=[smem] * scalars + [rest] * (len(args) - scalars),
        out_specs=[vmem] * len(outs),
        scratch_shapes=scratch,
        compiler_params=pltpu.CompilerParams(vmem_limit_bytes=40 * 1024 * 1024),
    )(*args)


def shards(pair, cotangent, w_in, w_out, norm_params):
    chips = ("row", "q")
    swap = [(0, 1), (1, 0)]
    f32, bf16 = (lambda *s: pltpu.VMEM(s, F32)), (lambda *s: pltpu.VMEM(s, BF16))
    wide, thin = ((CHIPS, 2, 768), BF16), ((CHIPS, 2, 384), BF16)
    tiles = 2 * TROWS * CHIPS

    def turn(x):
        return lax.all_to_all(x, chips, split_axis=0, concat_axis=0, tiled=True)

    core = lax.axis_index("core").astype(jnp.int32).reshape(1)
    send, zn = call(
        first_kernel,
        [wide, ((POS, C), BF16)],
        [bf16(TILE, TILE, C), bf16(C, 5 * C), f32(4, C), pltpu.SemaphoreType.DMA((3,))],
        pair,
        w_in,
        norm_params,
        anywhere=True,
    )
    own = turn(send)
    sib = lax.ppermute(own, "core", swap)
    part, a_own, b_own = call(
        second_kernel,
        [((384, 256), F32), ((384, 256), BF16), ((COLS, 2, WIDE, 256), BF16)],
        [f32(tiles, 128), f32(1024, 128)],
        core,
        own,
        scalars=1,
    )
    (send,) = call(
        second_kernel_sib,
        [thin],
        [f32(tiles, 128), f32(1024, 128), bf16(384, 256), bf16(COLS, 2, WIDE, 256)],
        core,
        sib,
        part,
        scalars=1,
    )
    send, update, dp4, gwo, mid = call(
        third_kernel,
        [thin, ((TILE, TILE, C), BF16), ((C, POS), BF16), ((C, C), F32), ((8, 128), F32)],
        [],
        turn(send),
        zn,
        cotangent,
        w_in,
        w_out,
        norm_params,
    )
    own = turn(send)
    sib = lax.ppermute(own, "core", swap)
    scratch = [f32(tiles // 2, 128), bf16(384, 256), f32(512, 128)]
    da, db = call(
        fourth_kernel,
        [((384, 256), F32), ((tiles // 2, 128), F32)],
        scratch,
        core,
        own,
        a_own,
        b_own,
        scalars=1,
    )
    (send,) = call(
        fourth_kernel_sib, [wide], scratch + [f32(tiles // 2, 128)], core, sib, a_own, b_own, da, db, scalars=1
    )
    grad_pair, grads = call(
        fifth_kernel,
        [((TILE, TILE, C), BF16), ((8 * C, 128), BF16)],
        [],
        turn(send),
        zn,
        pair,
        w_in,
        dp4,
        gwo,
        mid,
        norm_params,
    )
    mine = jnp.sum(turn(grads.reshape(CHIPS, 8, 128)).astype(F32), axis=0)
    mine = ((mine + lax.ppermute(mine, "core", swap)) / 384.0).astype(BF16)
    full = turn(jnp.broadcast_to(mine[None], (CHIPS, 8, 128))).reshape(8 * C, 128)
    grad_w_in, grad_w_out, grad_norm = call(
        last_kernel, [((C, 5 * C), F32), ((C, C), F32), ((4, C), F32)], [], full
    )
    return (update, grad_pair, grad_w_in, grad_w_out, grad_norm)


def solution(mesh):
    fine = Mesh(mesh.devices.reshape(ROWS, COLS, 2), ("row", "q", "core"))
    placed = (P("row", ("q", "core"), None), P("row", ("q", "core"), None), P(), P(), P())
    return jax.shard_map(shards, mesh=fine, in_specs=placed, out_specs=placed, check_vma=False)
```

time: 176 us -> 154 us (0.88)
  waiting for transfers between devices: 15.5 us -> 0.83 us
  starting transfers between devices: 19.2 us -> 9.83 us
  blocking collectives: 121 us -> 124 us
  Pallas kernels: 12.4 us -> 14.4 us
    all_to_all x1 -> x0, waiting for transfers between devices: 12 us -> none  [turn(): return lax.all_to_all(x, chips, split_axis=0, concat_axis=0, tiled=True)]
    all_to_all x1 -> x0, starting transfers between devices: 7.56 us -> none  [turn(): return lax.all_to_all(x, chips, split_axis=0, concat_axis=0, tiled=True)]
    all_to_all x5 -> x6, blocking collectives: 121 us -> 124 us  [turn(): return lax.all_to_all(x, chips, split_axis=0, concat_axis=0, tiled=True)]
    ppermute x2, waiting for transfers between devices: 2.7 us -> 0.01 us  [shards(): sib = lax.ppermute(own, 'core', swap)]
    pallas_call x5 -> x8, Pallas kernels: 12.4 us -> 14.4 us  [call(): pl.pallas_call(kernel, out_shape=[jax.ShapeDtypeStruct(s, t) for s, t in...]
  transfers between devices with their start and end apart: 4 -> 3, of which waited for: 4 -> 1; matrix products, arithmetic and copies ran while one was open for 0% -> 0% of each run, Pallas kernels for 0% -> 2%
where the time goes in v2:
time: 154 us; the launch traced here: 153 us
  blocking collectives  124 us (81%)
  Pallas kernels  14.4 us (9%)
  starting transfers between devices  9.83 us (6%)
  local copies, waits for them, and re-layouts  2.57 us (2%)
    all_to_all x6, blocking collectives, turn(): return lax.all_to_all(x, chips, split_axis=0, concat_axis=0, tiled=True)  124 us
    pallas_call x8, Pallas kernels, call(): pl.pallas_call(kernel, out_shape=[jax.ShapeDtypeStruct(s, t) for s, t in...  14.4 us
    ppermute x2, starting transfers between devices, shards(): sib = lax.ppermute(own, 'core', swap)  6.22 us
    ppermute x1, starting transfers between devices, shards(): mine = ((mine + lax.ppermute(mine, 'core', swap)) / 384.0).astype(BF16)  3.61 us
  transfers between devices with their start and end apart: 3, of which 1 were waited for; matrix products, arithmetic and copies ran while one was open for 0% of the time, Pallas kernels for 2%

profile of v2, /device:TPU:1, one launch (start us, length us, event | category | flops | bytes accessed | tf_op | source)
XLA Modules:
  0.0 153.0 jit_solution(12303944917764349419)
XLA Ops:
  0.6 0.0 copy-start
  0.6 0.9 copy-done
  1.6 0.9 copy-done.2
  2.5 0.7 copy-done.6
  3.1 1.2 shard_map.92
  4.4 29.8 %all_to_all.30.src_ref = bf16[128,2,768]{2,1,0:T(2,128)(2,1)S(1)} all-to-all(bf16[128,2,768]{2,1,0:T(2,128)(2,1)S(1)} %get-tuple-element.22), channel_id=1, replica_groups=mesh['row'=16,'q'=8,'core'=2] {'row','q'}, dimensions={0} | all-to-all | bytes 786432 | tf_op jit(solution)/shard_map/all_to_all | solution.py:248
  34.2 3.4 %collective-permute-start = (bf16[128,2,768]{2,1,0:T(2,128)(2,1)S(1)}, bf16[128,2,768]{2,1,0:T(2,128)(2,1)S(1)}, u32[]{:S(2)}, u32[]{:S(2)}) collective-permute-start(bf16[128,2,768]{2,1,0:T(2,128)(2,1)S(1)} %all_to_all.30.src_ref), channel_id=1, source_target_pairs={{0,1},{1,0},{2,3},{3,2},{4,5},{5,4},{6,7},{7,6},{8,9},{9,8},{10,11... | collective-permute-start | bytes 1179656 | tf_op jit(solution)/shard_map/ppermute | solution.py:261
  37.6 1.8 %shard_map.93 = (f32[384,256]{1,0:T(8,128)S(1)}, bf16[384,256]{1,0:T(8,128)(2,1)S(1)}, bf16[8,2,32,256]{3,2,1,0:T(8,128)(2,1)S(1)}) custom-call(s32[1]{0:T(128)} %bitcast.core_ref, bf16[128,2,768]{2,1,0:T(2,128)(2,1)S(1)} %all_to_all.30.src_ref), custom_call_target="tpu_custom_call" | custom-call | tf_op jit(solution)/shard_map/pallas_call | solution.py:230
  39.4 0.0 collective-permute-done.src_ref
  39.4 2.7 %shard_map.94 = bf16[128,2,384]{2,1,0:T(2,128)(2,1)S(1)} custom-call(s32[1]{0:T(128)} %bitcast.core_ref, bf16[128,2,768]{2,1,0:T(2,128)(2,1)S(1)} %collective-permute-done.src_ref, f32[384,256]{1,0:T(8,128)S(1)} %get-tuple-element.23.part_ref), custom_call_target="tpu_custom_call" | custom-call | tf_op jit(solution)/shard_map/pallas_call | solution.py:230
  42.1 0.0 copy-start.1
  42.1 0.0 copy-start.4
  42.1 0.0 copy-start.5
  42.2 0.0 copy-start.7
  42.2 18.8 %all_to_all.31.recv_ref = bf16[128,2,384]{2,1,0:T(2,128)(2,1)S(1)} all-to-all(bf16[128,2,384]{2,1,0:T(2,128)(2,1)S(1)} %shard_map.94), channel_id=1, replica_groups=mesh['row'=16,'q'=8,'core'=2] {'row','q'}, dimensions={0} | all-to-all | bytes 393216 | tf_op jit(solution)/shard_map/all_to_all | solution.py:248
  61.0 0.0 copy-done.1
  61.0 1.8 %shard_map.95 = (bf16[128,2,384]{2,1,0:T(2,128)(2,1)S(1)}, bf16[24,24,128]{2,1,0:T(8,128)(2,1)}, bf16[128,768]{1,0:T(8,128)(2,1)S(1)}, f32[128,128]{1,0:T(8,128)S(1)}, f32[8,128]{1,0:T(8,128)S(1)}) custom-call(bf16[128,2,384]{2,1,0:T(2,128)(2,1)S(1)} %all_to_all.31.recv_ref, bf16[768,128]{1,0:T(8,128)(2,1)S(1)} %get-tuple-element.24.zn_ref, ...), custom_call_target="tpu_custom_call" | custom-call | tf_op jit(solution)/shard_map/pallas_call | solution.py:230
  62.8 17.8 %all_to_all.32.src_ref = bf16[128,2,384]{2,1,0:T(2,128)(2,1)S(1)} all-to-all(bf16[128,2,384]{2,1,0:T(2,128)(2,1)S(1)} %get-tuple-element.26), channel_id=1, replica_groups=mesh['row'=16,'q'=8,'core'=2] {'row','q'}, dimensions={0} | all-to-all | bytes 393216 | tf_op jit(solution)/shard_map/all_to_all | solution.py:248
  80.6 2.8 %collective-permute-start.1 = (bf16[128,2,384]{2,1,0:T(2,128)(2,1)S(1)}, bf16[128,2,384]{2,1,0:T(2,128)(2,1)S(1)}, u32[]{:S(2)}, u32[]{:S(2)}) collective-permute-start(bf16[128,2,384]{2,1,0:T(2,128)(2,1)S(1)} %all_to_all.32.src_ref), channel_id=1, source_target_pairs={{0,1},{1,0},{2,3},{3,2},{4,5},{5,4},{6,7},{7,6},{8,9},{9,8},{10,11... | collective-permute-start | bytes 589832 | tf_op jit(solution)/shard_map/ppermute | solution.py:291
  83.4 1.3 shard_map.96
  84.7 0.0 collective-permute-done.1.src_ref
  84.7 2.8 %shard_map.97 = bf16[128,2,768]{2,1,0:T(2,128)(2,1)S(1)} custom-call(s32[1]{0:T(128)} %bitcast.core_ref, bf16[128,2,384]{2,1,0:T(2,128)(2,1)S(1)} %collective-permute-done.1.src_ref, bf16[384,256]{1,0:T(8,128)(2,1)S(1)} %get-tuple-element.27.a_ref, bf16[8,2,32,256]{3,2,1,0:T(8,128)(2,1)S(1)} %get-tuple-element.28.b_ref, ...), custom_call_target="tpu_custom_call" | custom-call | tf_op jit(solution)/shard_map/pallas_call | solution.py:230
  87.4 0.0 copy-start.3
  87.5 20.3 %all_to_all.33.recv_ref = bf16[128,2,768]{2,1,0:T(2,128)(2,1)S(1)} all-to-all(bf16[128,2,768]{2,1,0:T(2,128)(2,1)S(1)} %shard_map.97), channel_id=1, replica_groups=mesh['row'=16,'q'=8,'core'=2] {'row','q'}, dimensions={0} | all-to-all | bytes 786432 | tf_op jit(solution)/shard_map/all_to_all | solution.py:248
  107.7 0.0 copy-done.3
  107.7 2.0 %shard_map.98 = (bf16[24,24,128]{2,1,0:T(8,128)(2,1)}, bf16[1024,128]{1,0:T(8,128)(2,1)S(1)}) custom-call(bf16[128,2,768]{2,1,0:T(2,128)(2,1)S(1)} %all_to_all.33.recv_ref, bf16[768,128]{1,0:T(8,128)(2,1)S(1)} %get-tuple-element.24.zn_ref, bf16[24,24,128]{2,1,0:T(8,128)(2,1)S(1)} %copy-done.3, bf16[128,640]{1,0:T(8,128)(2,1)S(1)} %copy-done.1, ...), custom_call_target="tpu_custom_call" | custom-call | tf_op jit(solution)/shard_map/pallas_call | solution.py:230
  109.8 19.4 %all_to_all.34 = bf16[128,8,128]{2,1,0:T(8,128)(2,1)S(1)} all-to-all(bf16[128,8,128]{2,1,0:T(8,128)(2,1)S(1)} %bitcast.4), channel_id=1, replica_groups=mesh['row'=16,'q'=8,'core'=2] {'row','q'}, dimensions={0} | all-to-all | bytes 524288 | tf_op jit(solution)/shard_map/all_to_all | solution.py:248
  129.2 0.1 convert_reduce_fusion
  129.4 3.6 %collective-permute-start.2 = (f32[8,128]{1,0:T(8,128)S(1)}, f32[8,128]{1,0:T(8,128)S(1)}, u32[]{:S(2)}, u32[]{:S(2)}) collective-permute-start(f32[8,128]{1,0:T(8,128)S(1)} %convert_reduce_fusion), channel_id=1, source_target_pairs={{0,1},{1,0},{2,3},{3,2},{4,5},{5,4},{6,7},{7,6},{8,9},{9,8},{10,11... | collective-permute-start | bytes 12296 | tf_op jit(solution)/shard_map/ppermute | solution.py:320
  133.0 0.8 collective-permute-done.2
  133.8 18.3 %all_to_all.35 = bf16[128,8,128]{2,1,0:T(8,128)(2,1)S(1)} all-to-all(bf16[128,8,128]{2,1,0:T(8,128)(2,1)S(1)} %broadcast_in_dim.2), channel_id=1, replica_groups=mesh['row'=16,'q'=8,'core'=2] {'row','q'}, dimensions={0} | all-to-all | bytes 524288 | tf_op jit(solution)/shard_map/all_to_all | solution.py:248
  152.2 0.9 shard_map.99
  (7 shorter events, 0.1 us)
Async XLA Ops:
  0.6 0.9 copy-start
  1.5 0.9 copy-start.2
  2.5 0.7 copy-start.6
  34.2 5.3 %collective-permute-start = (bf16[128,2,768]{2,1,0:T(2,128)(2,1)S(1)}, bf16[128,2,768]{2,1,0:T(2,128)(2,1)S(1)}, u32[]{:S(2)}, u32[]{:S(2)}) collective-permute-start(bf16[128,2,768]{2,1,0:T(2,128)(2,1)S(1)} %all_to_all.30.src_ref), channel_id=1, source_target_pairs={{0,1},{1,0},{2,3},{3,2},{4,5},{5,4},{6,7},{7,6},{8,9},{9,8},{10,11... | collective-permute-start | bytes 1179656 | tf_op jit(solution)/shard_map/ppermute | solution.py:261
  42.1 18.9 %copy-start.1 = (bf16[128,640]{1,0:T(8,128)(2,1)S(1)}, bf16[128,640]{1,0:T(8,128)(2,1)}, u32[]{:S(2)}) copy-start(bf16[128,640]{1,0:T(8,128)(2,1)} %w_ref.3) | copy-start | bytes 491524
  42.1 18.9 %copy-start.4 = (bf16[24,24,128]{2,1,0:T(8,128)(2,1)S(1)}, bf16[24,24,128]{2,1,0:T(8,128)(2,1)}, u32[]{:S(2)}) copy-start(bf16[24,24,128]{2,1,0:T(8,128)(2,1)} %cot_ref.1) | copy-start | bytes 442372
  42.1 18.9 %copy-start.5 = (bf16[128,128]{1,0:T(8,128)(2,1)S(1)}, bf16[128,128]{1,0:T(8,128)(2,1)}, u32[]{:S(2)}) copy-start(bf16[128,128]{1,0:T(8,128)(2,1)} %wo_ref.1) | copy-start | bytes 98308
  42.2 18.8 %copy-start.7 = (f32[4,128]{1,0:T(4,128)S(1)}, f32[4,128]{1,0:T(4,128)}, u32[]{:S(2)}) copy-start(f32[4,128]{1,0:T(4,128)} %norm_ref.3) | copy-start | bytes 6148
  80.6 4.1 %collective-permute-start.1 = (bf16[128,2,384]{2,1,0:T(2,128)(2,1)S(1)}, bf16[128,2,384]{2,1,0:T(2,128)(2,1)S(1)}, u32[]{:S(2)}, u32[]{:S(2)}) collective-permute-start(bf16[128,2,384]{2,1,0:T(2,128)(2,1)S(1)} %all_to_all.32.src_ref), channel_id=1, source_target_pairs={{0,1},{1,0},{2,3},{3,2},{4,5},{5,4},{6,7},{7,6},{8,9},{9,8},{10,11... | collective-permute-start | bytes 589832 | tf_op jit(solution)/shard_map/ppermute | solution.py:291
  87.4 20.3 %copy-start.3 = (bf16[24,24,128]{2,1,0:T(8,128)(2,1)S(1)}, bf16[24,24,128]{2,1,0:T(8,128)(2,1)}, u32[]{:S(2)}) copy-start(bf16[24,24,128]{2,1,0:T(8,128)(2,1)} %pair_ref.1) | copy-start | bytes 442372
  129.4 4.4 %collective-permute-start.2 = (f32[8,128]{1,0:T(8,128)S(1)}, f32[8,128]{1,0:T(8,128)S(1)}, u32[]{:S(2)}, u32[]{:S(2)}) collective-permute-start(f32[8,128]{1,0:T(8,128)S(1)} %convert_reduce_fusion), channel_id=1, source_target_pairs={{0,1},{1,0},{2,3},{3,2},{4,5},{5,4},{6,7},{7,6},{8,9},{9,8},{10,11... | collective-permute-start | bytes 12296 | tf_op jit(solution)/shard_map/ppermute | solution.py:320

commit v3 on v2

--- a/solution.py
+++ b/solution.py
@@ -1,3 +1,5 @@
+import functools
+
 import jax
 import jax.numpy as jnp
 from jax import lax
@@ -17,6 +19,9 @@
 TROWS = 6
 POS = TILE * WIDE
 C = 128
+PLANE = 32
+CHIP_AXES = ("z", "yl", "x", "yh")
+PLANE_AXES = ("yl", "x", "yh", "core")
 
 
 def dot(x, y, cx, cy):
@@ -202,8 +207,6 @@
         gs = grad * s
         blocks += [gs.astype(BF16), (gs * p[:C] * (1.0 - s)).astype(BF16)]
     dp = jnp.concatenate(blocks + [dp4_ref[...]], axis=0)
-    g_ref[0 : 5 * C, :] = dot(dp, zn, 1, 0).astype(BF16)
-    g_ref[5 * C : 6 * C, :] = gwo_ref[...].astype(BF16)
     dzn = dot(w_ref[...], dp, 1, 0).T
     hat, rstd = norm_lanes(padded(pair_ref[...]))
     e = dzn * norm_ref[0:1, :]
@@ -211,16 +214,24 @@
     gpair_ref[...] = back.reshape(TILE, WIDE, C)[:, :TILE, :].astype(BF16)
     first = jnp.sum(dzn * hat, axis=0, keepdims=True)
     second = jnp.sum(dzn, axis=0, keepdims=True)
-    rows = jnp.concatenate([first, second, mid_ref[0:2, :], jnp.zeros((12, 128), F32)], axis=0)
-    g_ref[6 * C : 6 * C + 16, :] = rows.astype(BF16)
-    g_ref[6 * C + 16 : 8 * C, :] = jnp.zeros((2 * C - 16, 128), BF16)
+    grads = jnp.concatenate([dot(dp, zn, 1, 0), gwo_ref[...]], axis=0).reshape(PLANE, 24, C)
+    sums = jnp.concatenate([first, second, mid_ref[0:2, :], jnp.zeros((4, C), F32)], axis=0)[None]
+    sums = jnp.concatenate([sums, jnp.zeros((PLANE - 1, 8, C), F32)], axis=0)
+    g_ref[...] = jnp.concatenate([grads, sums], axis=1).astype(BF16)
+
+
+def spread_kernel(recv_ref, send_ref, *, scale):
+    total = jnp.sum(recv_ref[...].astype(F32), axis=0) * scale
+    send_ref[...] = jnp.broadcast_to(total[None], send_ref.shape).astype(BF16)
 
 
 def last_kernel(full_ref, gwi_ref, gwo_ref, gn_ref):
+    full = full_ref[...].astype(F32)
+    grads = full[:, :24, :].reshape(6 * C, C)
     for m in range(5):
-        gwi_ref[:, m * C : (m + 1) * C] = full_ref[m * C : (m + 1) * C, :].astype(F32).T
-    gwo_ref[...] = full_ref[5 * C : 6 * C, :].astype(F32)
-    gn_ref[...] = full_ref[6 * C : 6 * C + 16, :].astype(F32)[0:4, :]
+        gwi_ref[:, m * C : (m + 1) * C] = grads[m * C : (m + 1) * C, :].T
+    gwo_ref[...] = grads[5 * C :, :]
+    gn_ref[...] = full[0, 24:28, :]
 
 
 def call(kernel, outs, scratch, *args, scalars=0, anywhere=False):
@@ -238,14 +249,15 @@
 
 
 def shards(pair, cotangent, w_in, w_out, norm_params):
-    chips = ("row", "q")
     swap = [(0, 1), (1, 0)]
     f32, bf16 = (lambda *s: pltpu.VMEM(s, F32)), (lambda *s: pltpu.VMEM(s, BF16))
     wide, thin = ((CHIPS, 2, 768), BF16), ((CHIPS, 2, 384), BF16)
     tiles = 2 * TROWS * CHIPS
 
-    def turn(x):
-        return lax.all_to_all(x, chips, split_axis=0, concat_axis=0, tiled=True)
+    chunks = ((PLANE, 32, C), BF16)
+
+    def turn(x, axes=CHIP_AXES):
+        return lax.all_to_all(x, axes, split_axis=0, concat_axis=0, tiled=True)
 
     core = lax.axis_index("core").astype(jnp.int32).reshape(1)
     send, zn = call(
@@ -305,7 +317,7 @@
     )
     grad_pair, grads = call(
         fifth_kernel,
-        [((TILE, TILE, C), BF16), ((8 * C, 128), BF16)],
+        [((TILE, TILE, C), BF16), chunks],
         [],
         turn(send),
         zn,
@@ -316,16 +328,16 @@
         mid,
         norm_params,
     )
-    mine = jnp.sum(turn(grads.reshape(CHIPS, 8, 128)).astype(F32), axis=0)
-    mine = ((mine + lax.ppermute(mine, "core", swap)) / 384.0).astype(BF16)
-    full = turn(jnp.broadcast_to(mine[None], (CHIPS, 8, 128))).reshape(8 * C, 128)
+    (send,) = call(functools.partial(spread_kernel, scale=1.0), [((8, 32, C), BF16)], [], turn(grads, PLANE_AXES))
+    (send,) = call(functools.partial(spread_kernel, scale=1.0 / 384.0), [chunks], [], turn(send, "z"))
     grad_w_in, grad_w_out, grad_norm = call(
-        last_kernel, [((C, 5 * C), F32), ((C, C), F32), ((4, C), F32)], [], full
+        last_kernel, [((C, 5 * C), F32), ((C, C), F32), ((4, C), F32)], [], turn(send, PLANE_AXES)
     )
     return (update, grad_pair, grad_w_in, grad_w_out, grad_norm)
 
 
 def solution(mesh):
-    fine = Mesh(mesh.devices.reshape(ROWS, COLS, 2), ("row", "q", "core"))
-    placed = (P("row", ("q", "core"), None), P("row", ("q", "core"), None), P(), P(), P())
+    fine = Mesh(mesh.devices.reshape(8, 2, 4, 2, 2), CHIP_AXES + ("core",))
+    tile = P(("z", "yl"), ("x", "yh", "core"), None)
+    placed = (tile, tile, P(), P(), P())
     return jax.shard_map(shards, mesh=fine, in_specs=placed, out_specs=placed, check_vma=False)

time: 154 us -> 151 us (0.981)
  starting transfers between devices: 9.83 us -> 6.22 us
  blocking collectives: 124 us -> 126 us
    ppermute x1 -> x0, starting transfers between devices: 3.61 us -> none  [shards(): mine = ((mine + lax.ppermute(mine, 'core', swap)) / 384.0).astype(BF16)]
    all_to_all x6 -> x7, blocking collectives: 124 us -> 126 us  [turn(): return lax.all_to_all(x, axes, split_axis=0, concat_axis=0, tiled=True)]
    pallas_call x8 -> x10, Pallas kernels: 14.4 us -> 14.4 us  [call(): pl.pallas_call(kernel, out_shape=[jax.ShapeDtypeStruct(s, t) for s, t in...]
  transfers between devices with their start and end apart: 3 -> 2, of which waited for: 1 -> 0; matrix products, arithmetic and copies ran while one was open for 0% -> 0% of each run, Pallas kernels for 2% -> 2%
where the time goes in v3:
time: 151 us; the launch traced here: 150 us
  blocking collectives  126 us (83%)
  Pallas kernels  14.4 us (10%)
  starting transfers between devices  6.22 us (4%)
  local copies, waits for them, and re-layouts  2.53 us (2%)
    all_to_all x7, blocking collectives, turn(): return lax.all_to_all(x, axes, split_axis=0, concat_axis=0, tiled=True)  126 us
    pallas_call x10, Pallas kernels, call(): pl.pallas_call(kernel, out_shape=[jax.ShapeDtypeStruct(s, t) for s, t in...  14.4 us
    ppermute x2, starting transfers between devices, shards(): sib = lax.ppermute(own, 'core', swap)  6.22 us
  transfers between devices with their start and end apart: 2, of which 0 were waited for; matrix products, arithmetic and copies ran while one was open for 0% of the time, Pallas kernels for 2%

profile of v3, /device:TPU:1, one launch (start us, length us, event | category | flops | bytes accessed | tf_op | source)
XLA Modules:
  0.0 150.3 jit_solution(14263992910505389883)
XLA Ops:
  0.6 0.0 copy-start
  0.6 0.9 copy-done
  1.6 0.9 copy-done.2
  2.5 0.7 copy-done.6
  3.1 1.2 shard_map.92
  4.4 29.8 %all_to_all.35.src_ref = bf16[128,2,768]{2,1,0:T(2,128)(2,1)S(1)} all-to-all(bf16[128,2,768]{2,1,0:T(2,128)(2,1)S(1)} %get-tuple-element.22), channel_id=1, replica_groups=mesh['z'=8,'yl'=2,'x'=4,'yh'=2,'core'=2] {'z','yl','x','yh'}, dimensions={0} | all-to-all | bytes 786432 | tf_op jit(solution)/shard_map/all_to_all | solution.py:260
  34.2 3.4 %collective-permute-start = (bf16[128,2,768]{2,1,0:T(2,128)(2,1)S(1)}, bf16[128,2,768]{2,1,0:T(2,128)(2,1)S(1)}, u32[]{:S(2)}, u32[]{:S(2)}) collective-permute-start(bf16[128,2,768]{2,1,0:T(2,128)(2,1)S(1)} %all_to_all.35.src_ref), channel_id=1, source_target_pairs={{0,1},{1,0},{2,3},{3,2},{4,5},{5,4},{6,7},{7,6},{8,9},{9,8},{10,11... | collective-permute-start | bytes 1179656 | tf_op jit(solution)/shard_map/ppermute | solution.py:273
  37.6 1.8 %shard_map.93 = (f32[384,256]{1,0:T(8,128)S(1)}, bf16[384,256]{1,0:T(8,128)(2,1)S(1)}, bf16[8,2,32,256]{3,2,1,0:T(8,128)(2,1)S(1)}) custom-call(s32[1]{0:T(128)} %bitcast.core_ref, bf16[128,2,768]{2,1,0:T(2,128)(2,1)S(1)} %all_to_all.35.src_ref), custom_call_target="tpu_custom_call" | custom-call | tf_op jit(solution)/shard_map/pallas_call | solution.py:241
  39.4 0.0 collective-permute-done.src_ref
  39.4 2.7 %shard_map.94 = bf16[128,2,384]{2,1,0:T(2,128)(2,1)S(1)} custom-call(s32[1]{0:T(128)} %bitcast.core_ref, bf16[128,2,768]{2,1,0:T(2,128)(2,1)S(1)} %collective-permute-done.src_ref, f32[384,256]{1,0:T(8,128)S(1)} %get-tuple-element.23.part_ref), custom_call_target="tpu_custom_call" | custom-call | tf_op jit(solution)/shard_map/pallas_call | solution.py:241
  42.1 0.0 copy-start.1
  42.1 0.0 copy-start.4
  42.1 0.0 copy-start.5
  42.2 0.0 copy-start.7
  42.2 18.8 %all_to_all.36.recv_ref = bf16[128,2,384]{2,1,0:T(2,128)(2,1)S(1)} all-to-all(bf16[128,2,384]{2,1,0:T(2,128)(2,1)S(1)} %shard_map.94), channel_id=1, replica_groups=mesh['z'=8,'yl'=2,'x'=4,'yh'=2,'core'=2] {'z','yl','x','yh'}, dimensions={0} | all-to-all | bytes 393216 | tf_op jit(solution)/shard_map/all_to_all | solution.py:260
  61.0 0.0 copy-done.1
  61.0 0.0 copy-done.4
  61.0 0.0 copy-done.5
  61.0 0.0 copy-done.7
  61.0 1.8 %shard_map.95 = (bf16[128,2,384]{2,1,0:T(2,128)(2,1)S(1)}, bf16[24,24,128]{2,1,0:T(8,128)(2,1)}, bf16[128,768]{1,0:T(8,128)(2,1)S(1)}, f32[128,128]{1,0:T(8,128)S(1)}, f32[8,128]{1,0:T(8,128)S(1)}) custom-call(bf16[128,2,384]{2,1,0:T(2,128)(2,1)S(1)} %all_to_all.36.recv_ref, bf16[768,128]{1,0:T(8,128)(2,1)S(1)} %get-tuple-element.24.zn_ref, ...), custom_call_target="tpu_custom_call" | custom-call | tf_op jit(solution)/shard_map/pallas_call | solution.py:241
  62.8 17.8 %all_to_all.37.src_ref = bf16[128,2,384]{2,1,0:T(2,128)(2,1)S(1)} all-to-all(bf16[128,2,384]{2,1,0:T(2,128)(2,1)S(1)} %get-tuple-element.26), channel_id=1, replica_groups=mesh['z'=8,'yl'=2,'x'=4,'yh'=2,'core'=2] {'z','yl','x','yh'}, dimensions={0} | all-to-all | bytes 393216 | tf_op jit(solution)/shard_map/all_to_all | solution.py:260
  80.6 2.8 %collective-permute-start.1 = (bf16[128,2,384]{2,1,0:T(2,128)(2,1)S(1)}, bf16[128,2,384]{2,1,0:T(2,128)(2,1)S(1)}, u32[]{:S(2)}, u32[]{:S(2)}) collective-permute-start(bf16[128,2,384]{2,1,0:T(2,128)(2,1)S(1)} %all_to_all.37.src_ref), channel_id=1, source_target_pairs={{0,1},{1,0},{2,3},{3,2},{4,5},{5,4},{6,7},{7,6},{8,9},{9,8},{10,11... | collective-permute-start | bytes 589832 | tf_op jit(solution)/shard_map/ppermute | solution.py:303
  83.4 1.3 shard_map.96
  84.7 0.0 collective-permute-done.1.src_ref
  84.7 2.8 %shard_map.97 = bf16[128,2,768]{2,1,0:T(2,128)(2,1)S(1)} custom-call(s32[1]{0:T(128)} %bitcast.core_ref, bf16[128,2,384]{2,1,0:T(2,128)(2,1)S(1)} %collective-permute-done.1.src_ref, bf16[384,256]{1,0:T(8,128)(2,1)S(1)} %get-tuple-element.27.a_ref, bf16[8,2,32,256]{3,2,1,0:T(8,128)(2,1)S(1)} %get-tuple-element.28.b_ref, ...), custom_call_target="tpu_custom_call" | custom-call | tf_op jit(solution)/shard_map/pallas_call | solution.py:241
  87.4 0.0 copy-start.3
  87.5 20.3 %all_to_all.38.recv_ref = bf16[128,2,768]{2,1,0:T(2,128)(2,1)S(1)} all-to-all(bf16[128,2,768]{2,1,0:T(2,128)(2,1)S(1)} %shard_map.97), channel_id=1, replica_groups=mesh['z'=8,'yl'=2,'x'=4,'yh'=2,'core'=2] {'z','yl','x','yh'}, dimensions={0} | all-to-all | bytes 786432 | tf_op jit(solution)/shard_map/all_to_all | solution.py:260
  107.7 1.9 %shard_map.98 = (bf16[24,24,128]{2,1,0:T(8,128)(2,1)}, bf16[32,32,128]{2,1,0:T(8,128)(2,1)S(1)}) custom-call(bf16[128,2,768]{2,1,0:T(2,128)(2,1)S(1)} %all_to_all.38.recv_ref, bf16[768,128]{1,0:T(8,128)(2,1)S(1)} %get-tuple-element.24.zn_ref, bf16[24,24,128]{2,1,0:T(8,128)(2,1)S(1)} %copy-done.3, bf16[128,640]{1,0:T(8,128)(2,1)S(1)} %copy-done.1, ...), custom_call_target="tpu_custom_call" | custom-call | tf_op jit(solution)/shard_map/pallas_call | solution.py:241
  109.7 16.4 %all_to_all.39.recv_ref = bf16[32,32,128]{2,1,0:T(8,128)(2,1)S(1)} all-to-all(bf16[32,32,128]{2,1,0:T(8,128)(2,1)S(1)} %get-tuple-element.35), channel_id=1, replica_groups=mesh['z'=8,'yl'=2,'x'=4,'yh'=2,'core'=2] {'yl','x','yh','core'}, dimensions={0} | all-to-all | bytes 524288 | tf_op jit(solution)/shard_map/all_to_all | solution.py:260
  126.1 9.5 %all_to_all.40.recv_ref = bf16[8,32,128]{2,1,0:T(8,128)(2,1)S(1)} all-to-all(bf16[8,32,128]{2,1,0:T(8,128)(2,1)S(1)} %shard_map.99), channel_id=1, replica_groups=mesh['z'=8,'yl'=2,'x'=4,'yh'=2,'core'=2] {'z'}, dimensions={0} | all-to-all | bytes 131072 | tf_op jit(solution)/shard_map/all_to_all | solution.py:260
  135.7 13.7 %all_to_all.41.full_ref = bf16[32,32,128]{2,1,0:T(8,128)(2,1)S(1)} all-to-all(bf16[32,32,128]{2,1,0:T(8,128)(2,1)S(1)} %shard_map.100), channel_id=1, replica_groups=mesh['z'=8,'yl'=2,'x'=4,'yh'=2,'core'=2] {'yl','x','yh','core'}, dimensions={0} | all-to-all | bytes 524288 | tf_op jit(solution)/shard_map/all_to_all | solution.py:260
  149.4 0.9 shard_map.101
  (5 shorter events, 0.1 us)
Async XLA Ops:
  0.6 0.9 copy-start
  1.5 0.9 copy-start.2
  2.5 0.7 copy-start.6
  34.2 5.3 %collective-permute-start = (bf16[128,2,768]{2,1,0:T(2,128)(2,1)S(1)}, bf16[128,2,768]{2,1,0:T(2,128)(2,1)S(1)}, u32[]{:S(2)}, u32[]{:S(2)}) collective-permute-start(bf16[128,2,768]{2,1,0:T(2,128)(2,1)S(1)} %all_to_all.35.src_ref), channel_id=1, source_target_pairs={{0,1},{1,0},{2,3},{3,2},{4,5},{5,4},{6,7},{7,6},{8,9},{9,8},{10,11... | collective-permute-start | bytes 1179656 | tf_op jit(solution)/shard_map/ppermute | solution.py:273
  42.1 18.9 %copy-start.1 = (bf16[128,640]{1,0:T(8,128)(2,1)S(1)}, bf16[128,640]{1,0:T(8,128)(2,1)}, u32[]{:S(2)}) copy-start(bf16[128,640]{1,0:T(8,128)(2,1)} %w_ref.3) | copy-start | bytes 491524
  42.1 18.9 %copy-start.4 = (bf16[24,24,128]{2,1,0:T(8,128)(2,1)S(1)}, bf16[24,24,128]{2,1,0:T(8,128)(2,1)}, u32[]{:S(2)}) copy-start(bf16[24,24,128]{2,1,0:T(8,128)(2,1)} %cot_ref.1) | copy-start | bytes 442372
  42.1 18.9 %copy-start.5 = (bf16[128,128]{1,0:T(8,128)(2,1)S(1)}, bf16[128,128]{1,0:T(8,128)(2,1)}, u32[]{:S(2)}) copy-start(bf16[128,128]{1,0:T(8,128)(2,1)} %wo_ref.1) | copy-start | bytes 98308
  42.2 18.8 %copy-start.7 = (f32[4,128]{1,0:T(4,128)S(1)}, f32[4,128]{1,0:T(4,128)}, u32[]{:S(2)}) copy-start(f32[4,128]{1,0:T(4,128)} %norm_ref.3) | copy-start | bytes 6148
  80.6 4.1 %collective-permute-start.1 = (bf16[128,2,384]{2,1,0:T(2,128)(2,1)S(1)}, bf16[128,2,384]{2,1,0:T(2,128)(2,1)S(1)}, u32[]{:S(2)}, u32[]{:S(2)}) collective-permute-start(bf16[128,2,384]{2,1,0:T(2,128)(2,1)S(1)} %all_to_all.37.src_ref), channel_id=1, source_target_pairs={{0,1},{1,0},{2,3},{3,2},{4,5},{5,4},{6,7},{7,6},{8,9},{9,8},{10,11... | collective-permute-start | bytes 589832 | tf_op jit(solution)/shard_map/ppermute | solution.py:303
  87.4 20.3 %copy-start.3 = (bf16[24,24,128]{2,1,0:T(8,128)(2,1)S(1)}, bf16[24,24,128]{2,1,0:T(8,128)(2,1)}, u32[]{:S(2)}) copy-start(bf16[24,24,128]{2,1,0:T(8,128)(2,1)} %pair_ref.1) | copy-start | bytes 442372

commit v4 on v3

v4 whole, which is shorter than its diff:
```python
import functools

import jax
import jax.numpy as jnp
from jax import lax
from jax.experimental import pallas as pl
from jax.experimental.pallas import tpu as pltpu
from jax.sharding import Mesh
from jax.sharding import PartitionSpec as P

F32 = jnp.float32
BF16 = jnp.bfloat16
EPS = 1e-05
ROWS = 16
COLS = 8
CHIPS = 128
TILE = 24
WIDE = 32
TROWS = 5
POS = 128 * TROWS
C = 128
PLANE = 32
CHIP_AXES = ("x", "yh", "z", "yl")
PLANE_AXES = ("yl", "x", "yh", "core")


def dot(x, y, cx, cy):
    return lax.dot_general(x, y, (((cx,), (cy,)), ((), ())), preferred_element_type=F32)


def windows(rows):
    lane = lax.broadcasted_iota(jnp.int32, (rows, 128), 1)
    return lane, [((lane - 8 * n) & 127) < TILE for n in range(16)]


def block_turn(parts, wins, step, count, out_step, used):
    lane, masks = wins
    rolled = [p if a == 0 else pltpu.roll(p, step * a % 128, 1) for a, p in enumerate(parts)]
    outs = []
    for b in range(count):
        mixed = rolled[0]
        for a in range(1, len(parts)):
            mixed = jnp.where(masks[(step * a + out_step * b) % 128 // 8], rolled[a], mixed)
        if b:
            mixed = pltpu.roll(mixed, (128 - out_step * b) % 128, 1)
        outs.append(jnp.where(used, mixed, 0.0))
    return outs


def spread_turn(parts, wins, t):
    return block_turn(parts, wins, WIDE, min(5, TILE - 5 * t), TILE, (wins[0] & 31) < TILE)


def dense_turn(parts, wins):
    return block_turn(parts, wins, TILE, 4, WIDE, wins[0] < TILE * len(parts))


def rows_of(t):
    return range(5 * t, min(5 * t + 5, TILE))


def norm_lanes(v):
    mu = jnp.mean(v, axis=-1, keepdims=True)
    d = v - mu
    rstd = 1.0 / jnp.sqrt(jnp.mean(d * d, axis=-1, keepdims=True) + EPS)
    return d * rstd, rstd


def padded(tile):
    tile = tile.astype(F32)
    parts = []
    for t in range(TROWS):
        rows = len(rows_of(t))
        parts += [tile[5 * t : 5 * t + rows].reshape(rows * TILE, C), jnp.zeros((128 - rows * TILE, C), F32)]
    return jnp.concatenate(parts, axis=0)


def compact(val):
    parts = [val[128 * t : 128 * t + TILE * len(rows_of(t))].reshape(-1, TILE, C) for t in range(TROWS)]
    return jnp.concatenate(parts, axis=0)


def first_kernel(pair_hbm, w_hbm, norm_hbm, send_hbm, zn_hbm, pair_ref, w_ref, norm_ref, send_ref, zn_ref, sems):
    ends = ((pair_hbm, pair_ref), (norm_hbm, norm_ref), (w_hbm, w_ref), (zn_ref, zn_hbm))
    ends += tuple((send_ref.at[pl.ds(64 * n, 64)], send_hbm.at[pl.ds(64 * n, 64)]) for n in range(2))
    copies = [pltpu.make_async_copy(src, dst, sems.at[i]) for i, (src, dst) in enumerate(ends)]
    for copy in copies[:3]:
        copy.start()
    copies[0].wait()
    hat, _ = norm_lanes(pair_ref[...].astype(F32))
    copies[1].wait()
    zn = padded(hat * norm_ref[0:1, :][None] + norm_ref[1:2, :][None]).astype(BF16)
    zn_ref[...] = zn
    copies[3].start()
    copies[2].wait()
    p = [dot(w_ref[:, n * C : (n + 1) * C], zn, 0, 1) for n in range(4)]
    for n in range(2):
        part = slice(64 * n, 64 * n + 64)
        for m in range(2):
            send_ref[part, m, :] = (jax.nn.sigmoid(p[2 * m + 1][part]) * p[2 * m][part]).astype(BF16)
        copies[4 + n].start()
    for copy in copies[3:]:
        copy.wait()


def block(src, q, row, t):
    return src[pl.ds(ROWS * q, ROWS), row, t * 128 : (t + 1) * 128].astype(F32)


def tile_of(row, per, t):
    return (row, t) if per == TROWS else (t // per, t % per)


def gather_rows(src, row, per, dst):
    wins = windows(ROWS)
    for g in range(2):
        for t in range(TROWS):
            parts = [block(src, 4 * g + u, *tile_of(row, per, t)) for u in range(4)]
            for i, o in zip(rows_of(t), spread_turn(parts, wins, t)):
                dst[pl.ds(16 * i, 16), g * 128 : (g + 1) * 128] = o.astype(BF16)


def scatter_rows(val, dst, row, per):
    wins = windows(ROWS)
    for g in range(2):
        for t in range(TROWS):
            parts = [val[16 * i : 16 * i + 16, g * 128 : (g + 1) * 128] for i in rows_of(t)]
            s, lanes = tile_of(row, per, t)
            for u, o in enumerate(dense_turn(parts, wins)):
                dst[pl.ds(ROWS * (4 * g + u), ROWS), s, lanes * 128 : (lanes + 1) * 128] = o.astype(BF16)


def product(core, src, a_dst, b_dst, bscr):
    gather_rows(src, 0, TROWS, a_dst)
    for half in range(2 * 16):
        bscr[pl.ds(half * WIDE + TILE, WIDE - TILE), :] = jnp.zeros((WIDE - TILE, 128), F32)
    wins = windows(ROWS)
    for g in range(2):
        for t in range(TROWS):
            parts = [block(src, 4 * g + u, 1, t) for u in range(4)]
            for j, o in zip(rows_of(t), spread_turn(parts, wins, t)):
                bscr[pl.ds(512 * g + j, ROWS, stride=WIDE), :] = o
    for g in range(2):
        b_dst[:, :, :, g * 128 : (g + 1) * 128] = bscr[512 * g : 512 * g + 512, :].astype(BF16).reshape(COLS, 2, WIDE, 128)
    return dot(a_dst[...], b_dst[:, core].reshape(COLS * WIDE, 256), 1, 1)


def second_kernel(core_ref, src_ref, part_ref, a_ref, b_ref, bscr):
    part_ref[...] = product(core_ref[0], src_ref, a_ref, b_ref, bscr)


def second_kernel_sib(core_ref, src_ref, part_ref, send_ref, bscr, a_ref, b_ref):
    total = part_ref[...] + product(core_ref[0], src_ref, a_ref, b_ref, bscr)
    scatter_rows(total, send_ref, 0, 3)
    send_ref[:, 1, 256:] = jnp.zeros((CHIPS, 128), BF16)


def column(row):
    return jnp.broadcast_to(row, (C, C)).T[:, :1]


def lane_sums(val):
    part = val[:, :128]
    for t in range(1, TROWS):
        part = part + val[:, t * 128 : (t + 1) * 128]
    return jnp.sum(part.T, axis=0, keepdims=True)


def third_kernel(recv_ref, zn_ref, cot_ref, w_ref, wo_ref, norm_ref, send_ref, upd_ref, dp4_ref, gwo_ref, mid_ref):
    x = jnp.concatenate([recv_ref[:, s, :].astype(F32) for s in range(2)], axis=1)[:, :POS]
    gain, bias = column(norm_ref[2:3, :]), column(norm_ref[3:4, :])
    mu = jnp.mean(x, axis=0, keepdims=True)
    d = x - mu
    rstd = 1.0 / jnp.sqrt(jnp.mean(d * d, axis=0, keepdims=True) + EPS)
    hat = d * rstd
    xn = (hat * gain + bias).astype(BF16)
    y = dot(wo_ref[...], xn, 0, 0)
    gate = jax.nn.sigmoid(dot(w_ref[:, 4 * C :], zn_ref[...], 0, 1))
    upd = compact((gate * y).T)
    upd_ref[...] = upd.astype(BF16)
    cot = padded(cot_ref[...]).T
    cg = cot * gate
    dy = cg.astype(BF16)
    dp4_ref[...] = (cg * y * (1.0 - gate)).astype(BF16)
    gwo_ref[...] = dot(xn, dy, 1, 1)
    dxn = dot(wo_ref[...], dy, 1, 0)
    mid_ref[0:1, :] = lane_sums(dxn * hat)
    mid_ref[1:2, :] = lane_sums(dxn)
    mid_ref[2:8, :] = jnp.zeros((6, 128), F32)
    e = dxn * gain
    dx = rstd * (e - jnp.mean(e, axis=0, keepdims=True) - hat * jnp.mean(e * hat, axis=0, keepdims=True))
    dx = jnp.concatenate([dx, jnp.zeros((C, 768 - POS), F32)], axis=1)
    for half in range(2):
        send_ref[:, half, :] = dx[:, half * 384 : (half + 1) * 384].astype(BF16)


def back_product(side, src, a_ref, b_ref, d_ref, dbscr, sscr):
    gather_rows(src, 0, 3, d_ref)
    dx = d_ref[...]
    db = dot(dx, a_ref[...], 0, 0)
    for g in range(2):
        dbscr[pl.ds(256 * g, 256), :] = db[:, g * 128 : (g + 1) * 128]
    wins = windows(COLS)
    for g in range(2):
        for t in range(TROWS):
            parts = [dbscr[pl.ds(256 * g + j, COLS, stride=WIDE), :] for j in rows_of(t)]
            for u, o in enumerate(dense_turn(parts, wins)):
                sscr[pl.ds(t * CHIPS + ROWS * (4 * g + u) + side, COLS, stride=2), :] = o
    return dot(dx, b_ref[:, side].reshape(COLS * WIDE, 256), 1, 0)


def fourth_kernel(core_ref, src_ref, a_ref, b_ref, da_ref, db_ref, d_ref, dbscr):
    da_ref[...] = back_product(core_ref[0], src_ref, a_ref, b_ref, d_ref, dbscr, db_ref)


def fourth_kernel_sib(core_ref, src_ref, a_ref, b_ref, da_ref, db_ref, send_ref, d_ref, dbscr, sscr):
    core = core_ref[0]
    da = da_ref[...] + back_product(1 - core, src_ref, a_ref, b_ref, d_ref, dbscr, sscr)
    mine = lax.broadcasted_iota(jnp.int32, (CHIPS, 128), 0) % 2 == core
    for t in range(TROWS):
        tile = pl.ds(t * CHIPS, CHIPS)
        send_ref[:, 1, t * 128 : (t + 1) * 128] = jnp.where(mine, db_ref[tile, :], sscr[tile, :]).astype(BF16)
    scatter_rows(da, send_ref, 0, TROWS)


def fifth_kernel(recv_ref, zn_ref, pair_ref, w_ref, dp4_ref, gwo_ref, mid_ref, norm_ref, gpair_ref, g_ref):
    zn = zn_ref[...]
    blocks = []
    for m in range(2):
        grad = recv_ref[:, m, :].astype(F32)
        p = dot(w_ref[:, 2 * m * C : (2 * m + 2) * C], zn, 0, 1)
        s = jax.nn.sigmoid(p[C:])
        gs = grad * s
        blocks += [gs.astype(BF16), (gs * p[:C] * (1.0 - s)).astype(BF16)]
    dp = jnp.concatenate(blocks + [dp4_ref[...]], axis=0)
    dzn = dot(w_ref[...], dp, 1, 0).T
    hat, rstd = norm_lanes(padded(pair_ref[...]))
    e = dzn * norm_ref[0:1, :]
    back = rstd * (e - jnp.mean(e, axis=-1, keepdims=True) - hat * jnp.mean(e * hat, axis=-1, keepdims=True))
    gpair_ref[...] = compact(back).astype(BF16)
    first = jnp.sum(dzn * hat, axis=0, keepdims=True)
    second = jnp.sum(dzn, axis=0, keepdims=True)
    grads = jnp.concatenate([dot(dp, zn, 1, 0), gwo_ref[...]], axis=0).reshape(PLANE, 24, C)
    sums = jnp.concatenate([first, second, mid_ref[0:2, :], jnp.zeros((4, C), F32)], axis=0)[None]
    sums = jnp.concatenate([sums, jnp.zeros((PLANE - 1, 8, C), F32)], axis=0)
    g_ref[...] = jnp.concatenate([grads, sums], axis=1).astype(BF16)


def spread_kernel(recv_ref, send_ref, *, scale):
    total = jnp.sum(recv_ref[...].astype(F32), axis=0) * scale
    send_ref[...] = jnp.broadcast_to(total[None], send_ref.shape).astype(BF16)


def last_kernel(full_ref, gwi_ref, gwo_ref, gn_ref):
    full = full_ref[...].astype(F32)
    grads = full[:, :24, :].reshape(6 * C, C)
    for m in range(5):
        gwi_ref[:, m * C : (m + 1) * C] = grads[m * C : (m + 1) * C, :].T
    gwo_ref[...] = grads[5 * C :, :]
    gn_ref[...] = full[0, 24:28, :]


def call(kernel, outs, scratch, *args, scalars=0, anywhere=False):
    vmem = pl.BlockSpec(memory_space=pltpu.VMEM)
    smem = pl.BlockSpec(memory_space=pltpu.SMEM)
    rest = pl.BlockSpec(memory_space=pltpu.HBM) if anywhere else vmem
    return pl.pallas_call(
        kernel,
        out_shape=[jax.ShapeDtypeStruct(s, t) for s, t in outs],
        in_specs=[smem] * scalars + [rest] * (len(args) - scalars),
        out_specs=[rest] * len(outs),
        scratch_shapes=scratch,
        compiler_params=pltpu.CompilerParams(vmem_limit_bytes=62000000 if anywhere else 40 * 1024 * 1024),
    )(*args)


def shards(pair, cotangent, w_in, w_out, norm_params):
    swap = [(0, 1), (1, 0)]
    f32, bf16 = (lambda *s: pltpu.VMEM(s, F32)), (lambda *s: pltpu.VMEM(s, BF16))
    wide, thin = ((CHIPS, 2, POS), BF16), ((CHIPS, 2, 384), BF16)
    tiles = TROWS * CHIPS

    chunks = ((PLANE, 32, C), BF16)

    def turn(x, axes=CHIP_AXES):
        return lax.all_to_all(x, axes, split_axis=0, concat_axis=0, tiled=True)

    core = lax.axis_index("core").astype(jnp.int32).reshape(1)
    send, zn = call(
        first_kernel,
        [wide, ((POS, C), BF16)],
        [
            bf16(TILE, TILE, C),
            bf16(C, 5 * C),
            f32(4, C),
            bf16(CHIPS, 2, POS),
            bf16(POS, C),
            pltpu.SemaphoreType.DMA((6,)),
        ],
        pair,
        w_in,
        norm_params,
        anywhere=True,
    )
    own = turn(send)
    sib = lax.ppermute(own, "core", swap)
    part, a_own, b_own = call(
        second_kernel,
        [((384, 256), F32), ((384, 256), BF16), ((COLS, 2, WIDE, 256), BF16)],
        [f32(1024, 128)],
        core,
        own,
        scalars=1,
    )
    (send,) = call(
        second_kernel_sib,
        [thin],
        [f32(1024, 128), bf16(384, 256), bf16(COLS, 2, WIDE, 256)],
        core,
        sib,
        part,
        scalars=1,
    )
    send, update, dp4, gwo, mid = call(
        third_kernel,
        [thin, ((TILE, TILE, C), BF16), ((C, POS), BF16), ((C, C), F32), ((8, 128), F32)],
        [],
        turn(send),
        zn,
        cotangent,
        w_in,
        w_out,
        norm_params,
    )
    own = turn(send)
    sib = lax.ppermute(own, "core", swap)
    scratch = [bf16(384, 256), f32(512, 128)]
    da, db = call(
        fourth_kernel,
        [((384, 256), F32), ((tiles, 128), F32)],
        scratch,
        core,
        own,
        a_own,
        b_own,
        scalars=1,
    )
    (send,) = call(
        fourth_kernel_sib, [wide], scratch + [f32(tiles, 128)], core, sib, a_own, b_own, da, db, scalars=1
    )
    grad_pair, grads = call(
        fifth_kernel,
        [((TILE, TILE, C), BF16), chunks],
        [],
        turn(send),
        zn,
        pair,
        w_in,
        dp4,
        gwo,
        mid,
        norm_params,
    )
    (send,) = call(functools.partial(spread_kernel, scale=1.0), [((8, 32, C), BF16)], [], turn(grads, PLANE_AXES))
    (send,) = call(functools.partial(spread_kernel, scale=1.0 / 384.0), [chunks], [], turn(send, "z"))
    grad_w_in, grad_w_out, grad_norm = call(
        last_kernel, [((C, 5 * C), F32), ((C, C), F32), ((4, C), F32)], [], turn(send, PLANE_AXES)
    )
    return (update, grad_pair, grad_w_in, grad_w_out, grad_norm)


def solution(mesh):
    fine = Mesh(mesh.devices.reshape(8, 2, 4, 2, 2), ("z", "yl", "x", "yh", "core"))
    tile = P(("z", "yl"), ("x", "yh", "core"), None)
    placed = (tile, tile, P(), P(), P())
    return jax.shard_map(shards, mesh=fine, in_specs=placed, out_specs=placed, check_vma=False)
```

time: 151 us -> 145 us (0.960)
  local copies, waits for them, and re-layouts: 2.53 us -> 0.04 us
    unnamed x16 -> x12, local copies, waits for them, and re-layouts: 2.53 us -> 0.04 us
    all_to_all x7, blocking collectives: 126 us -> 125 us  [turn(): return lax.all_to_all(x, axes, split_axis=0, concat_axis=0, tiled=True)]
  transfers between devices with their start and end apart: 2 -> 2, of which waited for: 0 -> 1; matrix products, arithmetic and copies ran while one was open for 0% -> 0% of each run, Pallas kernels for 2% -> 2%
where the time goes in v4:
time: 145 us; the launch traced here: 144 us
  blocking collectives  125 us (86%)
  Pallas kernels  13.1 us (9%)
  starting transfers between devices  5.65 us (4%)
    all_to_all x7, blocking collectives, turn(): return lax.all_to_all(x, axes, split_axis=0, concat_axis=0, tiled=True)  125 us
    pallas_call x10, Pallas kernels, call(): pl.pallas_call(kernel, out_shape=[jax.ShapeDtypeStruct(s, t) for s, t in...  13.1 us
    ppermute x2, starting transfers between devices, shards(): sib = lax.ppermute(own, 'core', swap)  5.65 us
  transfers between devices with their start and end apart: 2, of which 1 were waited for; matrix products, arithmetic and copies ran while one was open for 0% of the time, Pallas kernels for 2%

profile of v4, /device:TPU:1, one launch (start us, length us, event | category | flops | bytes accessed | tf_op | source)
XLA Modules:
  0.0 144.3 jit_solution(10254404707713200984)
XLA Ops:
  0.6 2.5 %shard_map.92 = (bf16[128,2,640]{2,1,0:T(2,128)(2,1)}, bf16[640,128]{1,0:T(8,128)(2,1)}) custom-call(bf16[24,24,128]{2,1,0:T(8,128)(2,1)} %pair_ref.1, bf16[128,640]{1,0:T(8,128)(2,1)} %w_ref.3, f32[4,128]{1,0:T(4,128)} %norm_ref.3), custom_call_target="tpu_custom_call" | custom-call | tf_op jit(solution)/shard_map/pallas_call | solution.py:267
  3.1 30.3 %all_to_all.35.src_ref = bf16[128,2,640]{2,1,0:T(2,128)(2,1)S(1)} all-to-all(bf16[128,2,640]{2,1,0:T(2,128)(2,1)} %get-tuple-element.22), channel_id=1, replica_groups=mesh['z'=8,'yl'=2,'x'=4,'yh'=2,'core'=2] {'x','yh','z','yl'}, dimensions={0} | all-to-all | bytes 655360 | tf_op jit(solution)/shard_map/all_to_all | solution.py:286
  33.4 2.9 %collective-permute-start = (bf16[128,2,640]{2,1,0:T(2,128)(2,1)S(1)}, bf16[128,2,640]{2,1,0:T(2,128)(2,1)S(1)}, u32[]{:S(2)}, u32[]{:S(2)}) collective-permute-start(bf16[128,2,640]{2,1,0:T(2,128)(2,1)S(1)} %all_to_all.35.src_ref), channel_id=1, source_target_pairs={{0,1},{1,0},{2,3},{3,2},{4,5},{5,4},{6,7},{7,6},{8,9},{9,8},{10,11... | collective-permute-start | bytes 983048 | tf_op jit(solution)/shard_map/ppermute | solution.py:306
  36.2 1.3 shard_map.93
  37.5 0.0 collective-permute-done.src_ref
  37.5 0.0 copy-start.3
  37.6 1.8 %shard_map.94 = bf16[128,2,384]{2,1,0:T(2,128)(2,1)S(1)} custom-call(s32[1]{0:T(128)} %bitcast.core_ref, bf16[128,2,640]{2,1,0:T(2,128)(2,1)S(1)} %collective-permute-done.src_ref, f32[384,256]{1,0:T(8,128)S(1)} %get-tuple-element.23.part_ref), custom_call_target="tpu_custom_call" | custom-call | tf_op jit(solution)/shard_map/pallas_call | solution.py:267
  39.3 0.0 copy-start
  39.4 0.0 copy-start.1
  39.4 0.0 copy-start.4
  39.4 0.0 copy-start.5
  39.4 18.1 %all_to_all.36.recv_ref = bf16[128,2,384]{2,1,0:T(2,128)(2,1)S(1)} all-to-all(bf16[128,2,384]{2,1,0:T(2,128)(2,1)S(1)} %shard_map.94), channel_id=1, replica_groups=mesh['z'=8,'yl'=2,'x'=4,'yh'=2,'core'=2] {'x','yh','z','yl'}, dimensions={0} | all-to-all | bytes 393216 | tf_op jit(solution)/shard_map/all_to_all | solution.py:286
  57.4 0.0 copy-done.3
  57.5 0.0 copy-done
  57.5 0.0 copy-done.1
  57.5 0.0 copy-done.4
  57.5 0.0 copy-done.5
  57.5 1.8 %shard_map.95 = (bf16[128,2,384]{2,1,0:T(2,128)(2,1)S(1)}, bf16[24,24,128]{2,1,0:T(8,128)(2,1)}, bf16[128,640]{1,0:T(8,128)(2,1)S(1)}, f32[128,128]{1,0:T(8,128)S(1)}, f32[8,128]{1,0:T(8,128)S(1)}) custom-call(bf16[128,2,384]{2,1,0:T(2,128)(2,1)S(1)} %all_to_all.36.recv_ref, bf16[640,128]{1,0:T(8,128)(2,1)S(1)} %copy-done.1, ...), custom_call_target="tpu_custom_call" | custom-call | tf_op jit(solution)/shard_map/pallas_call | solution.py:267
  59.2 18.3 %all_to_all.37.src_ref = bf16[128,2,384]{2,1,0:T(2,128)(2,1)S(1)} all-to-all(bf16[128,2,384]{2,1,0:T(2,128)(2,1)S(1)} %get-tuple-element.26), channel_id=1, replica_groups=mesh['z'=8,'yl'=2,'x'=4,'yh'=2,'core'=2] {'x','yh','z','yl'}, dimensions={0} | all-to-all | bytes 393216 | tf_op jit(solution)/shard_map/all_to_all | solution.py:286
  77.6 2.8 %collective-permute-start.1 = (bf16[128,2,384]{2,1,0:T(2,128)(2,1)S(1)}, bf16[128,2,384]{2,1,0:T(2,128)(2,1)S(1)}, u32[]{:S(2)}, u32[]{:S(2)}) collective-permute-start(bf16[128,2,384]{2,1,0:T(2,128)(2,1)S(1)} %all_to_all.37.src_ref), channel_id=1, source_target_pairs={{0,1},{1,0},{2,3},{3,2},{4,5},{5,4},{6,7},{7,6},{8,9},{9,8},{10,11... | collective-permute-start | bytes 589832 | tf_op jit(solution)/shard_map/ppermute | solution.py:336
  80.4 1.0 shard_map.96
  81.4 0.1 collective-permute-done.1.src_ref
  81.4 1.9 %shard_map.97 = bf16[128,2,640]{2,1,0:T(2,128)(2,1)S(1)} custom-call(s32[1]{0:T(128)} %bitcast.core_ref, bf16[128,2,384]{2,1,0:T(2,128)(2,1)S(1)} %collective-permute-done.1.src_ref, bf16[384,256]{1,0:T(8,128)(2,1)S(1)} %get-tuple-element.27.a_ref, bf16[8,2,32,256]{3,2,1,0:T(8,128)(2,1)S(1)} %get-tuple-element.28.b_ref, ...), custom_call_target="tpu_custom_call" | custom-call | tf_op jit(solution)/shard_map/pallas_call | solution.py:267
  83.3 0.0 copy-start.2
  83.3 20.1 %all_to_all.38.recv_ref = bf16[128,2,640]{2,1,0:T(2,128)(2,1)S(1)} all-to-all(bf16[128,2,640]{2,1,0:T(2,128)(2,1)S(1)} %shard_map.97), channel_id=1, replica_groups=mesh['z'=8,'yl'=2,'x'=4,'yh'=2,'core'=2] {'x','yh','z','yl'}, dimensions={0} | all-to-all | bytes 655360 | tf_op jit(solution)/shard_map/all_to_all | solution.py:286
  103.4 0.0 copy-done.2
  103.4 1.9 %shard_map.98 = (bf16[24,24,128]{2,1,0:T(8,128)(2,1)}, bf16[32,32,128]{2,1,0:T(8,128)(2,1)S(1)}) custom-call(bf16[128,2,640]{2,1,0:T(2,128)(2,1)S(1)} %all_to_all.38.recv_ref, bf16[640,128]{1,0:T(8,128)(2,1)S(1)} %copy-done.1, bf16[24,24,128]{2,1,0:T(8,128)(2,1)S(1)} %copy-done.2, bf16[128,640]{1,0:T(8,128)(2,1)S(1)} %copy-done, ...), custom_call_target="tpu_custom_call" | custom-call | tf_op jit(solution)/shard_map/pallas_call | solution.py:267
  105.4 14.7 %all_to_all.39.recv_ref = bf16[32,32,128]{2,1,0:T(8,128)(2,1)S(1)} all-to-all(bf16[32,32,128]{2,1,0:T(8,128)(2,1)S(1)} %get-tuple-element.35), channel_id=1, replica_groups=mesh['z'=8,'yl'=2,'x'=4,'yh'=2,'core'=2] {'yl','x','yh','core'}, dimensions={0} | all-to-all | bytes 524288 | tf_op jit(solution)/shard_map/all_to_all | solution.py:286
  120.1 9.5 %all_to_all.40.recv_ref = bf16[8,32,128]{2,1,0:T(8,128)(2,1)S(1)} all-to-all(bf16[8,32,128]{2,1,0:T(8,128)(2,1)S(1)} %shard_map.99), channel_id=1, replica_groups=mesh['z'=8,'yl'=2,'x'=4,'yh'=2,'core'=2] {'z'}, dimensions={0} | all-to-all | bytes 131072 | tf_op jit(solution)/shard_map/all_to_all | solution.py:286
  129.7 13.7 %all_to_all.41.full_ref = bf16[32,32,128]{2,1,0:T(8,128)(2,1)S(1)} all-to-all(bf16[32,32,128]{2,1,0:T(8,128)(2,1)S(1)} %shard_map.100), channel_id=1, replica_groups=mesh['z'=8,'yl'=2,'x'=4,'yh'=2,'core'=2] {'yl','x','yh','core'}, dimensions={0} | all-to-all | bytes 524288 | tf_op jit(solution)/shard_map/all_to_all | solution.py:286
  143.4 0.9 shard_map.101
  (2 shorter events, 0.1 us)
Async XLA Ops:
  33.4 4.2 %collective-permute-start = (bf16[128,2,640]{2,1,0:T(2,128)(2,1)S(1)}, bf16[128,2,640]{2,1,0:T(2,128)(2,1)S(1)}, u32[]{:S(2)}, u32[]{:S(2)}) collective-permute-start(bf16[128,2,640]{2,1,0:T(2,128)(2,1)S(1)} %all_to_all.35.src_ref), channel_id=1, source_target_pairs={{0,1},{1,0},{2,3},{3,2},{4,5},{5,4},{6,7},{7,6},{8,9},{9,8},{10,11... | collective-permute-start | bytes 983048 | tf_op jit(solution)/shard_map/ppermute | solution.py:306
  37.5 19.9 %copy-start.3 = (bf16[24,24,128]{2,1,0:T(8,128)(2,1)S(1)}, bf16[24,24,128]{2,1,0:T(8,128)(2,1)}, u32[]{:S(2)}) copy-start(bf16[24,24,128]{2,1,0:T(8,128)(2,1)} %cot_ref.1) | copy-start | bytes 442372
  39.3 18.1 %copy-start = (bf16[128,640]{1,0:T(8,128)(2,1)S(1)}, bf16[128,640]{1,0:T(8,128)(2,1)}, u32[]{:S(2)}) copy-start(bf16[128,640]{1,0:T(8,128)(2,1)} %w_ref.3) | copy-start | bytes 491524
  39.4 18.1 %copy-start.1 = (bf16[640,128]{1,0:T(8,128)(2,1)S(1)}, bf16[640,128]{1,0:T(8,128)(2,1)}, u32[]{:S(2)}) copy-start(bf16[640,128]{1,0:T(8,128)(2,1)} %get-tuple-element.24.zn_ref) | copy-start | bytes 491524
  39.4 18.1 %copy-start.4 = (bf16[128,128]{1,0:T(8,128)(2,1)S(1)}, bf16[128,128]{1,0:T(8,128)(2,1)}, u32[]{:S(2)}) copy-start(bf16[128,128]{1,0:T(8,128)(2,1)} %wo_ref.1) | copy-start | bytes 98308
  39.4 18.1 %copy-start.5 = (f32[4,128]{1,0:T(4,128)S(1)}, f32[4,128]{1,0:T(4,128)}, u32[]{:S(2)}) copy-start(f32[4,128]{1,0:T(4,128)} %norm_ref.3) | copy-start | bytes 6148
  77.6 3.9 %collective-permute-start.1 = (bf16[128,2,384]{2,1,0:T(2,128)(2,1)S(1)}, bf16[128,2,384]{2,1,0:T(2,128)(2,1)S(1)}, u32[]{:S(2)}, u32[]{:S(2)}) collective-permute-start(bf16[128,2,384]{2,1,0:T(2,128)(2,1)S(1)} %all_to_all.37.src_ref), channel_id=1, source_target_pairs={{0,1},{1,0},{2,3},{3,2},{4,5},{5,4},{6,7},{7,6},{8,9},{9,8},{10,11... | collective-permute-start | bytes 589832 | tf_op jit(solution)/shard_map/ppermute | solution.py:336
  83.3 20.1 %copy-start.2 = (bf16[24,24,128]{2,1,0:T(8,128)(2,1)S(1)}, bf16[24,24,128]{2,1,0:T(8,128)(2,1)}, u32[]{:S(2)}) copy-start(bf16[24,24,128]{2,1,0:T(8,128)(2,1)} %pair_ref.1) | copy-start | bytes 442372

commit v5 on v4

--- a/solution.py
+++ b/solution.py
@@ -80,27 +80,20 @@
     return jnp.concatenate(parts, axis=0)
 
 
-def first_kernel(pair_hbm, w_hbm, norm_hbm, send_hbm, zn_hbm, pair_ref, w_ref, norm_ref, send_ref, zn_ref, sems):
-    ends = ((pair_hbm, pair_ref), (norm_hbm, norm_ref), (w_hbm, w_ref), (zn_ref, zn_hbm))
-    ends += tuple((send_ref.at[pl.ds(64 * n, 64)], send_hbm.at[pl.ds(64 * n, 64)]) for n in range(2))
+def first_kernel(pair_hbm, w_hbm, norm_hbm, send_ref, zn_ref, pair_ref, w_ref, norm_ref, sems):
+    ends = ((pair_hbm, pair_ref), (norm_hbm, norm_ref), (w_hbm, w_ref))
     copies = [pltpu.make_async_copy(src, dst, sems.at[i]) for i, (src, dst) in enumerate(ends)]
-    for copy in copies[:3]:
+    for copy in copies:
         copy.start()
     copies[0].wait()
     hat, _ = norm_lanes(pair_ref[...].astype(F32))
     copies[1].wait()
     zn = padded(hat * norm_ref[0:1, :][None] + norm_ref[1:2, :][None]).astype(BF16)
     zn_ref[...] = zn
-    copies[3].start()
     copies[2].wait()
-    p = [dot(w_ref[:, n * C : (n + 1) * C], zn, 0, 1) for n in range(4)]
-    for n in range(2):
-        part = slice(64 * n, 64 * n + 64)
-        for m in range(2):
-            send_ref[part, m, :] = (jax.nn.sigmoid(p[2 * m + 1][part]) * p[2 * m][part]).astype(BF16)
-        copies[4 + n].start()
-    for copy in copies[3:]:
-        copy.wait()
+    for m in range(2):
+        p = dot(w_ref[:, 2 * m * C : (2 * m + 2) * C], zn, 0, 1)
+        send_ref[:, m, :] = (jax.nn.sigmoid(p[C:]) * p[:C]).astype(BF16)
 
 
 def block(src, q, row, t):
@@ -223,27 +216,40 @@
     scatter_rows(da, send_ref, 0, TROWS)
 
 
-def fifth_kernel(recv_ref, zn_ref, pair_ref, w_ref, dp4_ref, gwo_ref, mid_ref, norm_ref, gpair_ref, g_ref):
+def fifth_kernel(core_ref, recv_ref, zn_ref, w_ref, dp4_ref, gwo_ref, keep_ref, give_ref, dp_ref, scr):
+    core = core_ref[0]
     zn = zn_ref[...]
-    blocks = []
     for m in range(2):
         grad = recv_ref[:, m, :].astype(F32)
         p = dot(w_ref[:, 2 * m * C : (2 * m + 2) * C], zn, 0, 1)
         s = jax.nn.sigmoid(p[C:])
         gs = grad * s
-        blocks += [gs.astype(BF16), (gs * p[:C] * (1.0 - s)).astype(BF16)]
-    dp = jnp.concatenate(blocks + [dp4_ref[...]], axis=0)
-    dzn = dot(w_ref[...], dp, 1, 0).T
+        dp_ref[2 * m * C : (2 * m + 1) * C, :] = gs.astype(BF16)
+        dp_ref[(2 * m + 1) * C : (2 * m + 2) * C, :] = (gs * p[:C] * (1.0 - s)).astype(BF16)
+    dp_ref[4 * C :, :] = dp4_ref[...]
+    grads = dot(dp_ref[...], zn, 1, 0)
+    scr[0] = grads[: 3 * C]
+    scr[1, : 2 * C, :] = grads[3 * C :]
+    scr[1, 2 * C :, :] = gwo_ref[...]
+    keep_ref[...] = scr[core]
+    give_ref[...] = scr[1 - core]
+
+
+def sixth_kernel(dp_ref, pair_ref, w_ref, mid_ref, norm_ref, gpair_ref, sums_ref):
+    dzn = dot(w_ref[...], dp_ref[...], 1, 0).T
     hat, rstd = norm_lanes(padded(pair_ref[...]))
     e = dzn * norm_ref[0:1, :]
     back = rstd * (e - jnp.mean(e, axis=-1, keepdims=True) - hat * jnp.mean(e * hat, axis=-1, keepdims=True))
     gpair_ref[...] = compact(back).astype(BF16)
     first = jnp.sum(dzn * hat, axis=0, keepdims=True)
     second = jnp.sum(dzn, axis=0, keepdims=True)
-    grads = jnp.concatenate([dot(dp, zn, 1, 0), gwo_ref[...]], axis=0).reshape(PLANE, 24, C)
-    sums = jnp.concatenate([first, second, mid_ref[0:2, :], jnp.zeros((4, C), F32)], axis=0)[None]
-    sums = jnp.concatenate([sums, jnp.zeros((PLANE - 1, 8, C), F32)], axis=0)
-    g_ref[...] = jnp.concatenate([grads, sums], axis=1).astype(BF16)
+    sums_ref[...] = jnp.concatenate([first, second, mid_ref[0:2, :], jnp.zeros((4, C), F32)], axis=0)
+
+
+def join_kernel(keep_ref, sib_ref, sums_ref, send_ref):
+    grads = (keep_ref[...] + sib_ref[...]).reshape(PLANE // 2, 24, C)
+    sums = jnp.concatenate([sums_ref[...][None], jnp.zeros((PLANE // 2 - 1, 8, C), F32)], axis=0)
+    send_ref[...] = jnp.concatenate([grads, sums], axis=1).astype(BF16)
 
 
 def spread_kernel(recv_ref, send_ref, *, scale):
@@ -252,25 +258,25 @@
 
 
 def last_kernel(full_ref, gwi_ref, gwo_ref, gn_ref):
-    full = full_ref[...].astype(F32)
-    grads = full[:, :24, :].reshape(6 * C, C)
+    full = full_ref[...].astype(F32).reshape(PLANE // 2, 2, 32, C)
+    halves = [full[:, h, :24, :].reshape(3 * C, C) for h in range(2)]
     for m in range(5):
-        gwi_ref[:, m * C : (m + 1) * C] = grads[m * C : (m + 1) * C, :].T
-    gwo_ref[...] = grads[5 * C :, :]
-    gn_ref[...] = full[0, 24:28, :]
-
-
-def call(kernel, outs, scratch, *args, scalars=0, anywhere=False):
+        gwi_ref[:, m * C : (m + 1) * C] = halves[m // 3][m % 3 * C : (m % 3 + 1) * C, :].T
+    gwo_ref[...] = halves[1][2 * C :, :]
+    gn_ref[...] = full[0, 0, 24:28, :] + full[0, 1, 24:28, :]
+
+
+def call(kernel, outs, scratch, *args, scalars=0, far=False):
     vmem = pl.BlockSpec(memory_space=pltpu.VMEM)
     smem = pl.BlockSpec(memory_space=pltpu.SMEM)
-    rest = pl.BlockSpec(memory_space=pltpu.HBM) if anywhere else vmem
+    rest = pl.BlockSpec(memory_space=pltpu.HBM) if far else vmem
     return pl.pallas_call(
         kernel,
         out_shape=[jax.ShapeDtypeStruct(s, t) for s, t in outs],
         in_specs=[smem] * scalars + [rest] * (len(args) - scalars),
-        out_specs=[rest] * len(outs),
+        out_specs=[vmem] * len(outs),
         scratch_shapes=scratch,
-        compiler_params=pltpu.CompilerParams(vmem_limit_bytes=62000000 if anywhere else 40 * 1024 * 1024),
+        compiler_params=pltpu.CompilerParams(vmem_limit_bytes=40 * 1024 * 1024),
     )(*args)
 
 
@@ -289,18 +295,9 @@
     send, zn = call(
         first_kernel,
         [wide, ((POS, C), BF16)],
-        [
-            bf16(TILE, TILE, C),
-            bf16(C, 5 * C),
-            f32(4, C),
-            bf16(CHIPS, 2, POS),
-            bf16(POS, C),
-            pltpu.SemaphoreType.DMA((6,)),
-        ],
-        pair,
-        w_in,
-        norm_params,
-        anywhere=True,
+        [bf16(TILE, TILE, C), bf16(C, 5 * C), f32(4, C), pltpu.SemaphoreType.DMA((3,))],
+        *[pltpu.with_memory_space_constraint(v, pltpu.HBM) for v in (pair, w_in, norm_params)],
+        far=True,
     )
     own = turn(send)
     sib = lax.ppermute(own, "core", swap)
@@ -348,20 +345,26 @@
     (send,) = call(
         fourth_kernel_sib, [wide], scratch + [f32(tiles, 128)], core, sib, a_own, b_own, da, db, scalars=1
     )
-    grad_pair, grads = call(
+    half = ((3 * C, C), F32)
+    keep, give, dp = call(
         fifth_kernel,
-        [((TILE, TILE, C), BF16), chunks],
-        [],
+        [half, half, ((5 * C, POS), BF16)],
+        [f32(2, 3 * C, C)],
+        core,
         turn(send),
         zn,
-        pair,
         w_in,
         dp4,
         gwo,
-        mid,
-        norm_params,
-    )
-    (send,) = call(functools.partial(spread_kernel, scale=1.0), [((8, 32, C), BF16)], [], turn(grads, PLANE_AXES))
+        scalars=1,
+    )
+    sib = lax.ppermute(give, "core", swap)
+    grad_pair, sums = call(
+        sixth_kernel, [((TILE, TILE, C), BF16), ((8, C), F32)], [], dp, pair, w_in, mid, norm_params
+    )
+    (send,) = call(join_kernel, [((PLANE // 2, 32, C), BF16)], [], keep, sib, sums)
+    send = turn(send, PLANE_AXES[:3])
+    (send,) = call(functools.partial(spread_kernel, scale=1.0), [((8, 32, C), BF16)], [], send)
     (send,) = call(functools.partial(spread_kernel, scale=1.0 / 384.0), [chunks], [], turn(send, "z"))
     grad_w_in, grad_w_out, grad_norm = call(
         last_kernel, [((C, 5 * C), F32), ((C, C), F32), ((4, C), F32)], [], turn(send, PLANE_AXES)

time: 145 us -> 143 us (0.986)
  blocking collectives: 125 us -> 121 us
  starting transfers between devices: 5.65 us -> 8.14 us
    all_to_all x7, blocking collectives: 125 us -> 121 us  [turn(): return lax.all_to_all(x, axes, split_axis=0, concat_axis=0, tiled=True)]
    ppermute x0 -> x1, starting transfers between devices: none -> 2.5 us  [shards(): sib = lax.ppermute(give, 'core', swap)]
    pallas_call x10 -> x12, Pallas kernels: 13.1 us -> 12.7 us  [call(): pl.pallas_call(kernel, out_shape=[jax.ShapeDtypeStruct(s, t) for s, t in...]
  transfers between devices with their start and end apart: 2 -> 3, of which waited for: 1 -> 1; matrix products, arithmetic and copies ran while one was open for 0% -> 0% of each run, Pallas kernels for 2% -> 3%
where the time goes in v5:
time: 143 us; the launch traced here: 142 us
  blocking collectives  121 us (85%)
  Pallas kernels  12.7 us (9%)
  starting transfers between devices  8.14 us (6%)
    all_to_all x7, blocking collectives, turn(): return lax.all_to_all(x, axes, split_axis=0, concat_axis=0, tiled=True)  121 us
    pallas_call x12, Pallas kernels, call(): pl.pallas_call(kernel, out_shape=[jax.ShapeDtypeStruct(s, t) for s, t in...  12.7 us
    ppermute x2, starting transfers between devices, shards(): sib = lax.ppermute(own, 'core', swap)  5.65 us
  transfers between devices with their start and end apart: 3, of which 1 were waited for; matrix products, arithmetic and copies ran while one was open for 0% of the time, Pallas kernels for 3%

profile of v5, /device:TPU:1, one launch (start us, length us, event | category | flops | bytes accessed | tf_op | source)
XLA Modules:
  0.0 142.5 jit_solution(16013170791484788007)
XLA Ops:
  0.6 1.7 %shard_map.92 = (bf16[128,2,640]{2,1,0:T(2,128)(2,1)S(1)}, bf16[640,128]{1,0:T(8,128)(2,1)S(1)}) custom-call(bf16[24,24,128]{2,1,0:T(8,128)(2,1)} %pair_ref.1, bf16[128,640]{1,0:T(8,128)(2,1)} %w_ref.5, f32[4,128]{1,0:T(4,128)} %norm_ref.3), custom_call_target="tpu_custom_call" | custom-call | tf_op jit(solution)/shard_map/pallas_call | solution.py:273
  2.4 30.1 %all_to_all.35.src_ref = bf16[128,2,640]{2,1,0:T(2,128)(2,1)S(1)} all-to-all(bf16[128,2,640]{2,1,0:T(2,128)(2,1)S(1)} %get-tuple-element.25), channel_id=1, replica_groups=mesh['z'=8,'yl'=2,'x'=4,'yh'=2,'core'=2] {'x','yh','z','yl'}, dimensions={0} | all-to-all | bytes 655360 | tf_op jit(solution)/shard_map/all_to_all | solution.py:292
  32.4 2.9 %collective-permute-start = (bf16[128,2,640]{2,1,0:T(2,128)(2,1)S(1)}, bf16[128,2,640]{2,1,0:T(2,128)(2,1)S(1)}, u32[]{:S(2)}, u32[]{:S(2)}) collective-permute-start(bf16[128,2,640]{2,1,0:T(2,128)(2,1)S(1)} %all_to_all.35.src_ref), channel_id=1, source_target_pairs={{0,1},{1,0},{2,3},{3,2},{4,5},{5,4},{6,7},{7,6},{8,9},{9,8},{10,11... | collective-permute-start | bytes 983048 | tf_op jit(solution)/shard_map/ppermute | solution.py:303
  35.3 1.3 shard_map.93
  36.6 0.0 collective-permute-done.src_ref
  36.6 1.8 %shard_map.94 = bf16[128,2,384]{2,1,0:T(2,128)(2,1)S(1)} custom-call(s32[1]{0:T(128)} %bitcast.core_ref, bf16[128,2,640]{2,1,0:T(2,128)(2,1)S(1)} %collective-permute-done.src_ref, f32[384,256]{1,0:T(8,128)S(1)} %get-tuple-element.26.part_ref), custom_call_target="tpu_custom_call" | custom-call | tf_op jit(solution)/shard_map/pallas_call | solution.py:273
  38.4 0.0 copy-start
  38.4 0.0 copy-start.2
  38.4 0.0 copy-start.3
  38.4 0.0 copy-start.4
  38.5 18.1 %all_to_all.36.recv_ref = bf16[128,2,384]{2,1,0:T(2,128)(2,1)S(1)} all-to-all(bf16[128,2,384]{2,1,0:T(2,128)(2,1)S(1)} %shard_map.94), channel_id=1, replica_groups=mesh['z'=8,'yl'=2,'x'=4,'yh'=2,'core'=2] {'x','yh','z','yl'}, dimensions={0} | all-to-all | bytes 393216 | tf_op jit(solution)/shard_map/all_to_all | solution.py:292
  56.5 0.0 copy-done
  56.5 0.0 copy-done.2
  56.5 0.0 copy-done.3
  56.5 0.0 copy-done.4
  56.5 1.8 %shard_map.95 = (bf16[128,2,384]{2,1,0:T(2,128)(2,1)S(1)}, bf16[24,24,128]{2,1,0:T(8,128)(2,1)}, bf16[128,640]{1,0:T(8,128)(2,1)S(1)}, f32[128,128]{1,0:T(8,128)S(1)}, f32[8,128]{1,0:T(8,128)S(1)}) custom-call(bf16[128,2,384]{2,1,0:T(2,128)(2,1)S(1)} %all_to_all.36.recv_ref, bf16[640,128]{1,0:T(8,128)(2,1)S(1)} %get-tuple-element.27.zn_ref, ...), custom_call_target="tpu_custom_call" | custom-call | tf_op jit(solution)/shard_map/pallas_call | solution.py:273
  58.3 18.3 %all_to_all.37.src_ref = bf16[128,2,384]{2,1,0:T(2,128)(2,1)S(1)} all-to-all(bf16[128,2,384]{2,1,0:T(2,128)(2,1)S(1)} %get-tuple-element.29), channel_id=1, replica_groups=mesh['z'=8,'yl'=2,'x'=4,'yh'=2,'core'=2] {'x','yh','z','yl'}, dimensions={0} | all-to-all | bytes 393216 | tf_op jit(solution)/shard_map/all_to_all | solution.py:292
  76.6 2.8 %collective-permute-start.1 = (bf16[128,2,384]{2,1,0:T(2,128)(2,1)S(1)}, bf16[128,2,384]{2,1,0:T(2,128)(2,1)S(1)}, u32[]{:S(2)}, u32[]{:S(2)}) collective-permute-start(bf16[128,2,384]{2,1,0:T(2,128)(2,1)S(1)} %all_to_all.37.src_ref), channel_id=1, source_target_pairs={{0,1},{1,0},{2,3},{3,2},{4,5},{5,4},{6,7},{7,6},{8,9},{9,8},{10,11... | collective-permute-start | bytes 589832 | tf_op jit(solution)/shard_map/ppermute | solution.py:333
  79.4 1.0 shard_map.96
  80.4 0.1 collective-permute-done.1.src_ref
  80.5 1.9 %shard_map.97 = bf16[128,2,640]{2,1,0:T(2,128)(2,1)S(1)} custom-call(s32[1]{0:T(128)} %bitcast.core_ref, bf16[128,2,384]{2,1,0:T(2,128)(2,1)S(1)} %collective-permute-done.1.src_ref, bf16[384,256]{1,0:T(8,128)(2,1)S(1)} %get-tuple-element.30.a_ref, bf16[8,2,32,256]{3,2,1,0:T(8,128)(2,1)S(1)} %get-tuple-element.31.b_ref, ...), custom_call_target="tpu_custom_call" | custom-call | tf_op jit(solution)/shard_map/pallas_call | solution.py:273
  82.4 20.0 %all_to_all.38.recv_ref = bf16[128,2,640]{2,1,0:T(2,128)(2,1)S(1)} all-to-all(bf16[128,2,640]{2,1,0:T(2,128)(2,1)S(1)} %shard_map.97), channel_id=1, replica_groups=mesh['z'=8,'yl'=2,'x'=4,'yh'=2,'core'=2] {'x','yh','z','yl'}, dimensions={0} | all-to-all | bytes 655360 | tf_op jit(solution)/shard_map/all_to_all | solution.py:292
  102.3 0.0 copy-start.1
  102.3 0.9 shard_map.98
  103.3 2.5 %collective-permute-start.2 = (f32[384,128]{1,0:T(8,128)S(1)}, f32[384,128]{1,0:T(8,128)S(1)}, u32[]{:S(2)}, u32[]{:S(2)}) collective-permute-start(f32[384,128]{1,0:T(8,128)S(1)} %get-tuple-element.40), channel_id=1, source_target_pairs={{0,1},{1,0},{2,3},{3,2},{4,5},{5,4},{6,7},{7,6},{8,9},{9,8},{10,11... | collective-permute-start | bytes 589832 | tf_op jit(solution)/shard_map/ppermute | solution.py:361
  105.8 0.0 copy-done.1
  105.8 1.3 shard_map.99
  107.1 0.0 collective-permute-done.2.sib_ref
  107.1 10.3 %all_to_all.39.recv_ref = bf16[16,32,128]{2,1,0:T(8,128)(2,1)S(1)} all-to-all(bf16[16,32,128]{2,1,0:T(8,128)(2,1)S(1)} %shard_map.100), channel_id=1, replica_groups=mesh['z'=8,'yl'=2,'x'=4,'yh'=2,'core'=2] {'yl','x','yh'}, dimensions={0} | all-to-all | bytes 262144 | tf_op jit(solution)/shard_map/all_to_all | solution.py:292
  117.4 9.6 %all_to_all.40.recv_ref = bf16[8,32,128]{2,1,0:T(8,128)(2,1)S(1)} all-to-all(bf16[8,32,128]{2,1,0:T(8,128)(2,1)S(1)} %shard_map.101), channel_id=1, replica_groups=mesh['z'=8,'yl'=2,'x'=4,'yh'=2,'core'=2] {'z'}, dimensions={0} | all-to-all | bytes 131072 | tf_op jit(solution)/shard_map/all_to_all | solution.py:292
  127.0 14.6 %all_to_all.41.full_ref = bf16[32,32,128]{2,1,0:T(8,128)(2,1)S(1)} all-to-all(bf16[32,32,128]{2,1,0:T(8,128)(2,1)S(1)} %shard_map.102), channel_id=1, replica_groups=mesh['z'=8,'yl'=2,'x'=4,'yh'=2,'core'=2] {'yl','x','yh','core'}, dimensions={0} | all-to-all | bytes 524288 | tf_op jit(solution)/shard_map/all_to_all | solution.py:292
  141.6 0.9 shard_map.103
  (3 shorter events, 0.1 us)
Async XLA Ops:
  32.4 4.2 %collective-permute-start = (bf16[128,2,640]{2,1,0:T(2,128)(2,1)S(1)}, bf16[128,2,640]{2,1,0:T(2,128)(2,1)S(1)}, u32[]{:S(2)}, u32[]{:S(2)}) collective-permute-start(bf16[128,2,640]{2,1,0:T(2,128)(2,1)S(1)} %all_to_all.35.src_ref), channel_id=1, source_target_pairs={{0,1},{1,0},{2,3},{3,2},{4,5},{5,4},{6,7},{7,6},{8,9},{9,8},{10,11... | collective-permute-start | bytes 983048 | tf_op jit(solution)/shard_map/ppermute | solution.py:303
  38.4 18.1 %copy-start = (bf16[128,640]{1,0:T(8,128)(2,1)S(1)}, bf16[128,640]{1,0:T(8,128)(2,1)}, u32[]{:S(2)}) copy-start(bf16[128,640]{1,0:T(8,128)(2,1)} %w_ref.5) | copy-start | bytes 491524
  38.4 18.1 %copy-start.2 = (bf16[24,24,128]{2,1,0:T(8,128)(2,1)S(1)}, bf16[24,24,128]{2,1,0:T(8,128)(2,1)}, u32[]{:S(2)}) copy-start(bf16[24,24,128]{2,1,0:T(8,128)(2,1)} %cot_ref.1) | copy-start | bytes 442372
  38.4 18.1 %copy-start.3 = (bf16[128,128]{1,0:T(8,128)(2,1)S(1)}, bf16[128,128]{1,0:T(8,128)(2,1)}, u32[]{:S(2)}) copy-start(bf16[128,128]{1,0:T(8,128)(2,1)} %wo_ref.1) | copy-start | bytes 98308
  38.4 18.1 %copy-start.4 = (f32[4,128]{1,0:T(4,128)S(1)}, f32[4,128]{1,0:T(4,128)}, u32[]{:S(2)}) copy-start(f32[4,128]{1,0:T(4,128)} %norm_ref.3) | copy-start | bytes 6148
  76.6 3.9 %collective-permute-start.1 = (bf16[128,2,384]{2,1,0:T(2,128)(2,1)S(1)}, bf16[128,2,384]{2,1,0:T(2,128)(2,1)S(1)}, u32[]{:S(2)}, u32[]{:S(2)}) collective-permute-start(bf16[128,2,384]{2,1,0:T(2,128)(2,1)S(1)} %all_to_all.37.src_ref), channel_id=1, source_target_pairs={{0,1},{1,0},{2,3},{3,2},{4,5},{5,4},{6,7},{7,6},{8,9},{9,8},{10,11... | collective-permute-start | bytes 589832 | tf_op jit(solution)/shard_map/ppermute | solution.py:333
  102.3 3.4 %copy-start.1 = (bf16[24,24,128]{2,1,0:T(8,128)(2,1)S(1)}, bf16[24,24,128]{2,1,0:T(8,128)(2,1)}, u32[]{:S(2)}) copy-start(bf16[24,24,128]{2,1,0:T(8,128)(2,1)} %pair_ref.1) | copy-start | bytes 442372
  103.3 3.8 %collective-permute-start.2 = (f32[384,128]{1,0:T(8,128)S(1)}, f32[384,128]{1,0:T(8,128)S(1)}, u32[]{:S(2)}, u32[]{:S(2)}) collective-permute-start(f32[384,128]{1,0:T(8,128)S(1)} %get-tuple-element.40), channel_id=1, source_target_pairs={{0,1},{1,0},{2,3},{3,2},{4,5},{5,4},{6,7},{7,6},{8,9},{9,8},{10,11... | collective-permute-start | bytes 589832 | tf_op jit(solution)/shard_map/ppermute | solution.py:361

commit v6 on v5

--- a/solution.py
+++ b/solution.py
@@ -20,8 +20,9 @@
 POS = 128 * TROWS
 C = 128
 PLANE = 32
-CHIP_AXES = ("x", "yh", "z", "yl")
+CHIP_AXES = ("x", "yh", "yl", "z")
 PLANE_AXES = ("yl", "x", "yh", "core")
+FLIPS = {"x": 2, "yh": 1, "z": 4}
 
 
 def dot(x, y, cx, cy):
@@ -96,8 +97,8 @@
         send_ref[:, m, :] = (jax.nn.sigmoid(p[C:]) * p[:C]).astype(BF16)
 
 
-def block(src, q, row, t):
-    return src[pl.ds(ROWS * q, ROWS), row, t * 128 : (t + 1) * 128].astype(F32)
+def block(src, q, row, t, first=0, rows=ROWS):
+    return src[pl.ds(ROWS * q + first, rows), row, t * 128 : (t + 1) * 128].astype(F32)
 
 
 def tile_of(row, per, t):
@@ -113,38 +114,45 @@
                 dst[pl.ds(16 * i, 16), g * 128 : (g + 1) * 128] = o.astype(BF16)
 
 
-def scatter_rows(val, dst, row, per):
+def scatter_rows(val, scr):
     wins = windows(ROWS)
     for g in range(2):
         for t in range(TROWS):
             parts = [val[16 * i : 16 * i + 16, g * 128 : (g + 1) * 128] for i in rows_of(t)]
-            s, lanes = tile_of(row, per, t)
             for u, o in enumerate(dense_turn(parts, wins)):
-                dst[pl.ds(ROWS * (4 * g + u), ROWS), s, lanes * 128 : (lanes + 1) * 128] = o.astype(BF16)
-
-
-def product(core, src, a_dst, b_dst, bscr):
-    gather_rows(src, 0, TROWS, a_dst)
-    for half in range(2 * 16):
-        bscr[pl.ds(half * WIDE + TILE, WIDE - TILE), :] = jnp.zeros((WIDE - TILE, 128), F32)
-    wins = windows(ROWS)
+                scr[ROWS * (4 * g + u) : ROWS * (4 * g + u + 1), t * 128 : (t + 1) * 128] = o
+
+
+def swap_blocks(val):
+    pairs = val.reshape(-1, 2, WIDE, val.shape[1])
+    return jnp.concatenate([pairs[:, 1:], pairs[:, :1]], axis=1).reshape(val.shape)
+
+
+def gather_b(src, first, rows, bscr, b_dst):
+    for n in range(2 * rows):
+        bscr[pl.ds(n * WIDE + TILE, WIDE - TILE), :] = jnp.zeros((WIDE - TILE, 128), F32)
+    wins = windows(rows)
     for g in range(2):
         for t in range(TROWS):
-            parts = [block(src, 4 * g + u, 1, t) for u in range(4)]
+            parts = [block(src, 4 * g + u, 1, t, first, rows) for u in range(4)]
             for j, o in zip(rows_of(t), spread_turn(parts, wins, t)):
-                bscr[pl.ds(512 * g + j, ROWS, stride=WIDE), :] = o
-    for g in range(2):
-        b_dst[:, :, :, g * 128 : (g + 1) * 128] = bscr[512 * g : 512 * g + 512, :].astype(BF16).reshape(COLS, 2, WIDE, 128)
-    return dot(a_dst[...], b_dst[:, core].reshape(COLS * WIDE, 256), 1, 1)
+                bscr[pl.ds(rows * WIDE * g + j, rows, stride=WIDE), :] = o
+        part = swap_blocks(bscr[rows * WIDE * g : rows * WIDE * (g + 1), :]).astype(BF16)
+        b_dst[:, :, g * 128 : (g + 1) * 128] = part.reshape(rows // COLS, COLS * WIDE, 128)
 
 
 def second_kernel(core_ref, src_ref, part_ref, a_ref, b_ref, bscr):
-    part_ref[...] = product(core_ref[0], src_ref, a_ref, b_ref, bscr)
-
-
-def second_kernel_sib(core_ref, src_ref, part_ref, send_ref, bscr, a_ref, b_ref):
-    total = part_ref[...] + product(core_ref[0], src_ref, a_ref, b_ref, bscr)
-    scatter_rows(total, send_ref, 0, 3)
+    gather_rows(src_ref, 0, TROWS, a_ref)
+    gather_b(src_ref, 0, ROWS, bscr, b_ref)
+    part_ref[...] = dot(a_ref[...], b_ref[core_ref[0]], 1, 1)
+
+
+def second_kernel_sib(core_ref, src_ref, part_ref, send_ref, bscr, a_ref, b_ref, scr):
+    gather_rows(src_ref, 0, TROWS, a_ref)
+    gather_b(src_ref, COLS * core_ref[0], COLS, bscr, b_ref)
+    scatter_rows(part_ref[...] + dot(a_ref[...], b_ref[0], 1, 1), scr)
+    for t in range(TROWS):
+        send_ref[:, t // 3, t % 3 * 128 : (t % 3 + 1) * 128] = scr[:, t * 128 : (t + 1) * 128].astype(BF16)
     send_ref[:, 1, 256:] = jnp.zeros((CHIPS, 128), BF16)
 
 
@@ -187,33 +195,40 @@
         send_ref[:, half, :] = dx[:, half * 384 : (half + 1) * 384].astype(BF16)
 
 
-def back_product(side, src, a_ref, b_ref, d_ref, dbscr, sscr):
+def back_product(side, src, a_ref, b_ref, d_ref, dbscr, store):
     gather_rows(src, 0, 3, d_ref)
     dx = d_ref[...]
     db = dot(dx, a_ref[...], 0, 0)
     for g in range(2):
-        dbscr[pl.ds(256 * g, 256), :] = db[:, g * 128 : (g + 1) * 128]
+        dbscr[pl.ds(256 * g, 256), :] = swap_blocks(db[:, g * 128 : (g + 1) * 128])
     wins = windows(COLS)
     for g in range(2):
         for t in range(TROWS):
             parts = [dbscr[pl.ds(256 * g + j, COLS, stride=WIDE), :] for j in rows_of(t)]
             for u, o in enumerate(dense_turn(parts, wins)):
-                sscr[pl.ds(t * CHIPS + ROWS * (4 * g + u) + side, COLS, stride=2), :] = o
-    return dot(dx, b_ref[:, side].reshape(COLS * WIDE, 256), 1, 0)
+                store(4 * g + u, slice(t * 128, (t + 1) * 128), o)
+    return dot(dx, b_ref[side], 1, 0)
 
 
 def fourth_kernel(core_ref, src_ref, a_ref, b_ref, da_ref, db_ref, d_ref, dbscr):
-    da_ref[...] = back_product(core_ref[0], src_ref, a_ref, b_ref, d_ref, dbscr, db_ref)
-
-
-def fourth_kernel_sib(core_ref, src_ref, a_ref, b_ref, da_ref, db_ref, send_ref, d_ref, dbscr, sscr):
+    def store(q, lanes, val):
+        db_ref[COLS * q : COLS * (q + 1), lanes] = val
+
+    da_ref[...] = back_product(core_ref[0], src_ref, a_ref, b_ref, d_ref, dbscr, store)
+
+
+def fourth_kernel_sib(core_ref, src_ref, a_ref, b_ref, da_ref, db_ref, send_ref, d_ref, dbscr, scr):
     core = core_ref[0]
-    da = da_ref[...] + back_product(1 - core, src_ref, a_ref, b_ref, d_ref, dbscr, sscr)
-    mine = lax.broadcasted_iota(jnp.int32, (CHIPS, 128), 0) % 2 == core
-    for t in range(TROWS):
-        tile = pl.ds(t * CHIPS, CHIPS)
-        send_ref[:, 1, t * 128 : (t + 1) * 128] = jnp.where(mine, db_ref[tile, :], sscr[tile, :]).astype(BF16)
-    scatter_rows(da, send_ref, 0, TROWS)
+
+    def store(q, lanes, val):
+        scr[pl.ds(pl.multiple_of(ROWS * q + COLS * (1 - core), COLS), COLS), lanes] = val
+
+    da = da_ref[...] + back_product(1 - core, src_ref, a_ref, b_ref, d_ref, dbscr, store)
+    for q in range(COLS):
+        scr[pl.ds(pl.multiple_of(ROWS * q + COLS * core, COLS), COLS), :] = db_ref[COLS * q : COLS * (q + 1), :]
+    send_ref[:, 1, :] = scr[...].astype(BF16)
+    scatter_rows(da, scr)
+    send_ref[:, 0, :] = scr[...].astype(BF16)
 
 
 def fifth_kernel(core_ref, recv_ref, zn_ref, w_ref, dp4_ref, gwo_ref, keep_ref, give_ref, dp_ref, scr):
@@ -284,12 +299,15 @@
     swap = [(0, 1), (1, 0)]
     f32, bf16 = (lambda *s: pltpu.VMEM(s, F32)), (lambda *s: pltpu.VMEM(s, BF16))
     wide, thin = ((CHIPS, 2, POS), BF16), ((CHIPS, 2, 384), BF16)
-    tiles = TROWS * CHIPS
 
     chunks = ((PLANE, 32, C), BF16)
 
     def turn(x, axes=CHIP_AXES):
-        return lax.all_to_all(x, axes, split_axis=0, concat_axis=0, tiled=True)
+        flip = 0
+        for axis in axes:
+            flip = flip * lax.axis_size(axis) + FLIPS.get(axis, 0)
+        groups = [[n ^ flip for n in range(x.shape[0])]]
+        return lax.all_to_all(x, axes, split_axis=0, concat_axis=0, axis_index_groups=groups, tiled=True)
 
     core = lax.axis_index("core").astype(jnp.int32).reshape(1)
     send, zn = call(
@@ -303,7 +321,7 @@
     sib = lax.ppermute(own, "core", swap)
     part, a_own, b_own = call(
         second_kernel,
-        [((384, 256), F32), ((384, 256), BF16), ((COLS, 2, WIDE, 256), BF16)],
+        [((384, 256), F32), ((384, 256), BF16), ((2, COLS * WIDE, 256), BF16)],
         [f32(1024, 128)],
         core,
         own,
@@ -312,7 +330,7 @@
     (send,) = call(
         second_kernel_sib,
         [thin],
-        [f32(1024, 128), bf16(384, 256), bf16(COLS, 2, WIDE, 256)],
+        [f32(512, 128), bf16(384, 256), bf16(1, COLS * WIDE, 256), f32(CHIPS, POS)],
         core,
         sib,
         part,
@@ -334,7 +352,7 @@
     scratch = [bf16(384, 256), f32(512, 128)]
     da, db = call(
         fourth_kernel,
-        [((384, 256), F32), ((tiles, 128), F32)],
+        [((384, 256), F32), ((CHIPS // 2, POS), F32)],
         scratch,
         core,
         own,
@@ -343,7 +361,7 @@
         scalars=1,
     )
     (send,) = call(
-        fourth_kernel_sib, [wide], scratch + [f32(tiles, 128)], core, sib, a_own, b_own, da, db, scalars=1
+        fourth_kernel_sib, [wide], scratch + [f32(CHIPS, POS)], core, sib, a_own, b_own, da, db, scalars=1
     )
     half = ((3 * C, C), F32)
     keep, give, dp = call(
@@ -365,9 +383,12 @@
     (send,) = call(join_kernel, [((PLANE // 2, 32, C), BF16)], [], keep, sib, sums)
     send = turn(send, PLANE_AXES[:3])
     (send,) = call(functools.partial(spread_kernel, scale=1.0), [((8, 32, C), BF16)], [], send)
-    (send,) = call(functools.partial(spread_kernel, scale=1.0 / 384.0), [chunks], [], turn(send, "z"))
+    (send,) = call(functools.partial(spread_kernel, scale=1.0 / 384.0), [chunks], [], turn(send, ("z",)))
     grad_w_in, grad_w_out, grad_norm = call(
-        last_kernel, [((C, 5 * C), F32), ((C, C), F32), ((4, C), F32)], [], turn(send, PLANE_AXES)
+        last_kernel,
+        [((C, 5 * C), F32), ((C, C), F32), ((4, C), F32)],
+        [],
+        turn(send, PLANE_AXES),
     )
     return (update, grad_pair, grad_w_in, grad_w_out, grad_norm)
 

time: 143 us -> 134 us (0.937)
  starting transfers between devices: 8.14 us -> 3.62 us
  blocking collectives: 121 us -> 117 us
    all_to_all x7, blocking collectives: 121 us -> 117 us  [turn(): lax.all_to_all(x, axes, split_axis=0, concat_axis=0, axis_index_groups=gr...]
    ppermute x2, starting transfers between devices: 5.65 us -> 2.59 us  [shards(): sib = lax.ppermute(own, 'core', swap)]
    ppermute x1, starting transfers between devices: 2.5 us -> 1.04 us  [shards(): sib = lax.ppermute(give, 'core', swap)]
where the time goes in v6:
time: 134 us; the launch traced here: 133 us
  blocking collectives  117 us (87%)
  Pallas kernels  11.7 us (9%)
  starting transfers between devices  3.62 us (3%)
    all_to_all x7, blocking collectives, turn(): lax.all_to_all(x, axes, split_axis=0, concat_axis=0, axis_index_groups=gr...  117 us
    pallas_call x12, Pallas kernels, call(): pl.pallas_call(kernel, out_shape=[jax.ShapeDtypeStruct(s, t) for s, t in...  11.7 us
  transfers between devices with their start and end apart: 3, of which 1 were waited for; matrix products, arithmetic and copies ran while one was open for 0% of the time, Pallas kernels for 3%

profile of v6, /device:TPU:1, one launch (start us, length us, event | category | flops | bytes accessed | tf_op | source)
XLA Modules:
  0.0 133.3 jit_solution(18108519040258537151)
XLA Ops:
  0.6 1.7 %shard_map.92 = (bf16[128,2,640]{2,1,0:T(2,128)(2,1)S(1)}, bf16[640,128]{1,0:T(8,128)(2,1)S(1)}) custom-call(bf16[24,24,128]{2,1,0:T(8,128)(2,1)} %pair_ref.1, bf16[128,640]{1,0:T(8,128)(2,1)} %w_ref.5, f32[4,128]{1,0:T(4,128)} %norm_ref.3), custom_call_target="tpu_custom_call" | custom-call | tf_op jit(solution)/shard_map/pallas_call | solution.py:288
  2.4 25.7 %all_to_all.35.src_ref = bf16[128,2,640]{2,1,0:T(2,128)(2,1)S(1)} all-to-all(bf16[128,2,640]{2,1,0:T(2,128)(2,1)S(1)} %get-tuple-element.25), channel_id=1, replica_groups={{138,170,202,234,10,42,74,106,154,186,218,250,26,58,90,122,136,168,200,..., dimensions={0} | all-to-all | bytes 655360 | tf_op jit(solution)/shard_map/all_to_all | solution.py:310
  28.1 1.0 collective-permute-start
  29.1 1.3 shard_map.93
  30.4 0.0 collective-permute-done.src_ref
  30.4 1.4 %shard_map.94 = bf16[128,2,384]{2,1,0:T(2,128)(2,1)S(1)} custom-call(s32[1]{0:T(128)} %bitcast.core_ref, bf16[128,2,640]{2,1,0:T(2,128)(2,1)S(1)} %collective-permute-done.src_ref, f32[384,256]{1,0:T(8,128)S(1)} %get-tuple-element.26.part_ref), custom_call_target="tpu_custom_call" | custom-call | tf_op jit(solution)/shard_map/pallas_call | solution.py:288
  31.8 0.0 copy-start
  31.8 0.0 copy-start.2
  31.8 0.0 copy-start.3
  31.8 0.0 copy-start.4
  31.9 18.9 %all_to_all.36.recv_ref = bf16[128,2,384]{2,1,0:T(2,128)(2,1)S(1)} all-to-all(bf16[128,2,384]{2,1,0:T(2,128)(2,1)S(1)} %shard_map.94), channel_id=1, replica_groups={{138,170,202,234,10,42,74,106,154,186,218,250,26,58,90,122,136,168,200,..., dimensions={0} | all-to-all | bytes 393216 | tf_op jit(solution)/shard_map/all_to_all | solution.py:310
  50.8 0.0 copy-done
  50.8 0.0 copy-done.2
  50.8 0.0 copy-done.3
  50.8 0.0 copy-done.4
  50.8 1.8 %shard_map.95 = (bf16[128,2,384]{2,1,0:T(2,128)(2,1)S(1)}, bf16[24,24,128]{2,1,0:T(8,128)(2,1)}, bf16[128,640]{1,0:T(8,128)(2,1)S(1)}, f32[128,128]{1,0:T(8,128)S(1)}, f32[8,128]{1,0:T(8,128)S(1)}) custom-call(bf16[128,2,384]{2,1,0:T(2,128)(2,1)S(1)} %all_to_all.36.recv_ref, bf16[640,128]{1,0:T(8,128)(2,1)S(1)} %get-tuple-element.27.zn_ref, ...), custom_call_target="tpu_custom_call" | custom-call | tf_op jit(solution)/shard_map/pallas_call | solution.py:288
  52.6 18.0 %all_to_all.37.src_ref = bf16[128,2,384]{2,1,0:T(2,128)(2,1)S(1)} all-to-all(bf16[128,2,384]{2,1,0:T(2,128)(2,1)S(1)} %get-tuple-element.29), channel_id=1, replica_groups={{138,170,202,234,10,42,74,106,154,186,218,250,26,58,90,122,136,168,200,..., dimensions={0} | all-to-all | bytes 393216 | tf_op jit(solution)/shard_map/all_to_all | solution.py:310
  70.5 1.6 %collective-permute-start.1 = (bf16[128,2,384]{2,1,0:T(2,128)(2,1)S(1)}, bf16[128,2,384]{2,1,0:T(2,128)(2,1)S(1)}, u32[]{:S(2)}, u32[]{:S(2)}) collective-permute-start(bf16[128,2,384]{2,1,0:T(2,128)(2,1)S(1)} %all_to_all.37.src_ref), channel_id=1, source_target_pairs={{0,1},{1,0},{2,3},{3,2},{4,5},{5,4},{6,7},{7,6},{8,9},{9,8},{10,11... | collective-permute-start | bytes 589832 | tf_op jit(solution)/shard_map/ppermute | solution.py:351
  72.1 1.0 shard_map.96
  73.1 0.1 collective-permute-done.1.src_ref
  73.2 1.3 shard_map.97
  74.5 21.4 %all_to_all.38.recv_ref = bf16[128,2,640]{2,1,0:T(2,128)(2,1)S(1)} all-to-all(bf16[128,2,640]{2,1,0:T(2,128)(2,1)S(1)} %shard_map.97), channel_id=1, replica_groups={{138,170,202,234,10,42,74,106,154,186,218,250,26,58,90,122,136,168,200,..., dimensions={0} | all-to-all | bytes 655360 | tf_op jit(solution)/shard_map/all_to_all | solution.py:310
  95.9 0.0 copy-start.1
  95.9 0.9 shard_map.98
  96.8 1.0 collective-permute-start.2
  97.9 0.0 copy-done.1
  97.9 1.3 shard_map.99
  99.2 0.0 collective-permute-done.2.sib_ref
  99.2 10.0 %all_to_all.39.recv_ref = bf16[16,32,128]{2,1,0:T(8,128)(2,1)S(1)} all-to-all(bf16[16,32,128]{2,1,0:T(8,128)(2,1)S(1)} %shard_map.100), channel_id=1, replica_groups={{10,8,14,12,2,0,6,4,26,24,30,28,18,16,22,20},{11,9,15,13,3,1,7,5,27,25,..., dimensions={0} | all-to-all | bytes 262144 | tf_op jit(solution)/shard_map/all_to_all | solution.py:310
  109.2 9.3 %all_to_all.40.recv_ref = bf16[8,32,128]{2,1,0:T(8,128)(2,1)S(1)} all-to-all(bf16[8,32,128]{2,1,0:T(8,128)(2,1)S(1)} %shard_map.101), channel_id=1, replica_groups={{128,160,192,224,0,32,64,96},{129,161,193,225,1,33,65,97},{130,162,194,..., dimensions={0} | all-to-all | bytes 131072 | tf_op jit(solution)/shard_map/all_to_all | solution.py:310
  118.6 13.9 %all_to_all.41.full_ref = bf16[32,32,128]{2,1,0:T(8,128)(2,1)S(1)} all-to-all(bf16[32,32,128]{2,1,0:T(8,128)(2,1)S(1)} %shard_map.102), channel_id=1, replica_groups={{10,11,8,9,14,15,12,13,2,3,0,1,6,7,4,5,26,27,24,25,30,31,28,29,18,19,16..., dimensions={0} | all-to-all | bytes 524288 | tf_op jit(solution)/shard_map/all_to_all | solution.py:310
  132.4 0.9 shard_map.103
  (3 shorter events, 0.1 us)
Async XLA Ops:
  28.1 2.3 %collective-permute-start = (bf16[128,2,640]{2,1,0:T(2,128)(2,1)S(1)}, bf16[128,2,640]{2,1,0:T(2,128)(2,1)S(1)}, u32[]{:S(2)}, u32[]{:S(2)}) collective-permute-start(bf16[128,2,640]{2,1,0:T(2,128)(2,1)S(1)} %all_to_all.35.src_ref), channel_id=1, source_target_pairs={{0,1},{1,0},{2,3},{3,2},{4,5},{5,4},{6,7},{7,6},{8,9},{9,8},{10,11... | collective-permute-start | bytes 983048 | tf_op jit(solution)/shard_map/ppermute | solution.py:321
  31.8 19.0 %copy-start = (bf16[128,640]{1,0:T(8,128)(2,1)S(1)}, bf16[128,640]{1,0:T(8,128)(2,1)}, u32[]{:S(2)}) copy-start(bf16[128,640]{1,0:T(8,128)(2,1)} %w_ref.5) | copy-start | bytes 491524
  31.8 19.0 %copy-start.2 = (bf16[24,24,128]{2,1,0:T(8,128)(2,1)S(1)}, bf16[24,24,128]{2,1,0:T(8,128)(2,1)}, u32[]{:S(2)}) copy-start(bf16[24,24,128]{2,1,0:T(8,128)(2,1)} %cot_ref.1) | copy-start | bytes 442372
  31.8 19.0 %copy-start.3 = (bf16[128,128]{1,0:T(8,128)(2,1)S(1)}, bf16[128,128]{1,0:T(8,128)(2,1)}, u32[]{:S(2)}) copy-start(bf16[128,128]{1,0:T(8,128)(2,1)} %wo_ref.1) | copy-start | bytes 98308
  31.8 19.0 %copy-start.4 = (f32[4,128]{1,0:T(4,128)S(1)}, f32[4,128]{1,0:T(4,128)}, u32[]{:S(2)}) copy-start(f32[4,128]{1,0:T(4,128)} %norm_ref.3) | copy-start | bytes 6148
  70.5 2.7 %collective-permute-start.1 = (bf16[128,2,384]{2,1,0:T(2,128)(2,1)S(1)}, bf16[128,2,384]{2,1,0:T(2,128)(2,1)S(1)}, u32[]{:S(2)}, u32[]{:S(2)}) collective-permute-start(bf16[128,2,384]{2,1,0:T(2,128)(2,1)S(1)} %all_to_all.37.src_ref), channel_id=1, source_target_pairs={{0,1},{1,0},{2,3},{3,2},{4,5},{5,4},{6,7},{7,6},{8,9},{9,8},{10,11... | collective-permute-start | bytes 589832 | tf_op jit(solution)/shard_map/ppermute | solution.py:351
  95.9 2.0 %copy-start.1 = (bf16[24,24,128]{2,1,0:T(8,128)(2,1)S(1)}, bf16[24,24,128]{2,1,0:T(8,128)(2,1)}, u32[]{:S(2)}) copy-start(bf16[24,24,128]{2,1,0:T(8,128)(2,1)} %pair_ref.1) | copy-start | bytes 442372
  96.8 2.4 %collective-permute-start.2 = (f32[384,128]{1,0:T(8,128)S(1)}, f32[384,128]{1,0:T(8,128)S(1)}, u32[]{:S(2)}, u32[]{:S(2)}) collective-permute-start(f32[384,128]{1,0:T(8,128)S(1)} %get-tuple-element.40), channel_id=1, source_target_pairs={{0,1},{1,0},{2,3},{3,2},{4,5},{5,4},{6,7},{7,6},{8,9},{9,8},{10,11... | collective-permute-start | bytes 589832 | tf_op jit(solution)/shard_map/ppermute | solution.py:379

commit v7 on v6

--- a/solution.py
+++ b/solution.py
@@ -272,7 +272,9 @@
     send_ref[...] = jnp.broadcast_to(total[None], send_ref.shape).astype(BF16)
 
 
-def last_kernel(full_ref, gwi_ref, gwo_ref, gn_ref):
+def last_kernel(full_ref, upd_ref, gpair_ref, gwi_ref, gwo_ref, gn_ref, upd_out, gpair_out):
+    upd_out[...] = upd_ref[...]
+    gpair_out[...] = gpair_ref[...]
     full = full_ref[...].astype(F32).reshape(PLANE // 2, 2, 32, C)
     halves = [full[:, h, :24, :].reshape(3 * C, C) for h in range(2)]
     for m in range(5):
@@ -384,11 +386,14 @@
     send = turn(send, PLANE_AXES[:3])
     (send,) = call(functools.partial(spread_kernel, scale=1.0), [((8, 32, C), BF16)], [], send)
     (send,) = call(functools.partial(spread_kernel, scale=1.0 / 384.0), [chunks], [], turn(send, ("z",)))
-    grad_w_in, grad_w_out, grad_norm = call(
+    tile = ((TILE, TILE, C), BF16)
+    grad_w_in, grad_w_out, grad_norm, update, grad_pair = call(
         last_kernel,
-        [((C, 5 * C), F32), ((C, C), F32), ((4, C), F32)],
+        [((C, 5 * C), F32), ((C, C), F32), ((4, C), F32), tile, tile],
         [],
         turn(send, PLANE_AXES),
+        update,
+        grad_pair,
     )
     return (update, grad_pair, grad_w_in, grad_w_out, grad_norm)
 

time: 134 us -> 133 us (level)
  transfers between devices with their start and end apart: 3 -> 3, of which waited for: 1 -> 2; matrix products, arithmetic and copies ran while one was open for 0% -> 0% of each run, Pallas kernels for 3% -> 2%
where the time goes in v7:
time: 133 us
  blocking collectives  117 us (88%)
  Pallas kernels  10.4 us (8%)
  starting transfers between devices  3.62 us (3%)
    all_to_all x7, blocking collectives, turn(): lax.all_to_all(x, axes, split_axis=0, concat_axis=0, axis_index_groups=gr...  117 us
    pallas_call x12, Pallas kernels, call(): pl.pallas_call(kernel, out_shape=[jax.ShapeDtypeStruct(s, t) for s, t in...  10.4 us
  transfers between devices with their start and end apart: 3, of which 2 were waited for; matrix products, arithmetic and copies ran while one was open for 0% of the time, Pallas kernels for 2%

profile of v7, /device:TPU:1, one launch (start us, length us, event | category | flops | bytes accessed | tf_op | source)
XLA Modules:
  0.0 132.7 jit_solution(956337926873119242)
XLA Ops:
  0.6 1.7 %shard_map.92 = (bf16[128,2,640]{2,1,0:T(2,128)(2,1)S(1)}, bf16[640,128]{1,0:T(8,128)(2,1)S(1)}) custom-call(bf16[24,24,128]{2,1,0:T(8,128)(2,1)} %pair_ref.1, bf16[128,640]{1,0:T(8,128)(2,1)} %w_ref.5, f32[4,128]{1,0:T(4,128)} %norm_ref.3), custom_call_target="tpu_custom_call" | custom-call | tf_op jit(solution)/shard_map/pallas_call | solution.py:290
  2.4 25.7 %all_to_all.35.src_ref = bf16[128,2,640]{2,1,0:T(2,128)(2,1)S(1)} all-to-all(bf16[128,2,640]{2,1,0:T(2,128)(2,1)S(1)} %get-tuple-element.27), channel_id=1, replica_groups={{138,170,202,234,10,42,74,106,154,186,218,250,26,58,90,122,136,168,200,..., dimensions={0} | all-to-all | bytes 655360 | tf_op jit(solution)/shard_map/all_to_all | solution.py:312
  28.1 1.0 collective-permute-start
  29.1 1.3 shard_map.93
  30.4 0.0 collective-permute-done.src_ref
  30.4 1.4 %shard_map.94 = bf16[128,2,384]{2,1,0:T(2,128)(2,1)S(1)} custom-call(s32[1]{0:T(128)} %bitcast.core_ref, bf16[128,2,640]{2,1,0:T(2,128)(2,1)S(1)} %collective-permute-done.src_ref, f32[384,256]{1,0:T(8,128)S(1)} %get-tuple-element.28.part_ref), custom_call_target="tpu_custom_call" | custom-call | tf_op jit(solution)/shard_map/pallas_call | solution.py:290
  31.8 0.0 copy-start
  31.8 0.0 copy-start.2
  31.8 0.0 copy-start.3
  31.8 0.0 copy-start.4
  31.9 18.9 %all_to_all.36.recv_ref = bf16[128,2,384]{2,1,0:T(2,128)(2,1)S(1)} all-to-all(bf16[128,2,384]{2,1,0:T(2,128)(2,1)S(1)} %shard_map.94), channel_id=1, replica_groups={{138,170,202,234,10,42,74,106,154,186,218,250,26,58,90,122,136,168,200,..., dimensions={0} | all-to-all | bytes 393216 | tf_op jit(solution)/shard_map/all_to_all | solution.py:312
  50.8 0.0 copy-done
  50.8 0.0 copy-done.2
  50.8 0.0 copy-done.3
  50.8 0.0 copy-done.4
  50.8 1.1 shard_map.95
  51.9 18.0 %all_to_all.37.src_ref = bf16[128,2,384]{2,1,0:T(2,128)(2,1)S(1)} all-to-all(bf16[128,2,384]{2,1,0:T(2,128)(2,1)S(1)} %get-tuple-element.30), channel_id=1, replica_groups={{138,170,202,234,10,42,74,106,154,186,218,250,26,58,90,122,136,168,200,..., dimensions={0} | all-to-all | bytes 393216 | tf_op jit(solution)/shard_map/all_to_all | solution.py:312
  69.9 1.6 %collective-permute-start.1 = (bf16[128,2,384]{2,1,0:T(2,128)(2,1)S(1)}, bf16[128,2,384]{2,1,0:T(2,128)(2,1)S(1)}, u32[]{:S(2)}, u32[]{:S(2)}) collective-permute-start(bf16[128,2,384]{2,1,0:T(2,128)(2,1)S(1)} %all_to_all.37.src_ref), channel_id=1, source_target_pairs={{0,1},{1,0},{2,3},{3,2},{4,5},{5,4},{6,7},{7,6},{8,9},{9,8},{10,11... | collective-permute-start | bytes 589832 | tf_op jit(solution)/shard_map/ppermute | solution.py:353
  71.5 1.0 shard_map.96
  72.5 0.1 collective-permute-done.1.src_ref
  72.6 1.3 shard_map.97
  73.8 21.4 %all_to_all.38.recv_ref = bf16[128,2,640]{2,1,0:T(2,128)(2,1)S(1)} all-to-all(bf16[128,2,640]{2,1,0:T(2,128)(2,1)S(1)} %shard_map.97), channel_id=1, replica_groups={{138,170,202,234,10,42,74,106,154,186,218,250,26,58,90,122,136,168,200,..., dimensions={0} | all-to-all | bytes 655360 | tf_op jit(solution)/shard_map/all_to_all | solution.py:312
  95.2 0.0 copy-start.1
  95.3 0.9 shard_map.98
  96.2 1.0 collective-permute-start.2
  97.2 0.0 copy-done.1
  97.2 0.7 shard_map.99
  97.9 0.4 collective-permute-done.2.sib_ref
  98.3 9.9 %all_to_all.39.recv_ref = bf16[16,32,128]{2,1,0:T(8,128)(2,1)S(1)} all-to-all(bf16[16,32,128]{2,1,0:T(8,128)(2,1)S(1)} %shard_map.100), channel_id=1, replica_groups={{10,8,14,12,2,0,6,4,26,24,30,28,18,16,22,20},{11,9,15,13,3,1,7,5,27,25,..., dimensions={0} | all-to-all | bytes 262144 | tf_op jit(solution)/shard_map/all_to_all | solution.py:312
  108.3 9.3 %all_to_all.40.recv_ref = bf16[8,32,128]{2,1,0:T(8,128)(2,1)S(1)} all-to-all(bf16[8,32,128]{2,1,0:T(8,128)(2,1)S(1)} %shard_map.101), channel_id=1, replica_groups={{128,160,192,224,0,32,64,96},{129,161,193,225,1,33,65,97},{130,162,194,..., dimensions={0} | all-to-all | bytes 131072 | tf_op jit(solution)/shard_map/all_to_all | solution.py:312
  117.7 14.2 %all_to_all.41.full_ref = bf16[32,32,128]{2,1,0:T(8,128)(2,1)S(1)} all-to-all(bf16[32,32,128]{2,1,0:T(8,128)(2,1)S(1)} %shard_map.102), channel_id=1, replica_groups={{10,11,8,9,14,15,12,13,2,3,0,1,6,7,4,5,26,27,24,25,30,31,28,29,18,19,16..., dimensions={0} | all-to-all | bytes 524288 | tf_op jit(solution)/shard_map/all_to_all | solution.py:312
  131.8 0.9 shard_map.103
  (3 shorter events, 0.1 us)
Async XLA Ops:
  28.1 2.3 %collective-permute-start = (bf16[128,2,640]{2,1,0:T(2,128)(2,1)S(1)}, bf16[128,2,640]{2,1,0:T(2,128)(2,1)S(1)}, u32[]{:S(2)}, u32[]{:S(2)}) collective-permute-start(bf16[128,2,640]{2,1,0:T(2,128)(2,1)S(1)} %all_to_all.35.src_ref), channel_id=1, source_target_pairs={{0,1},{1,0},{2,3},{3,2},{4,5},{5,4},{6,7},{7,6},{8,9},{9,8},{10,11... | collective-permute-start | bytes 983048 | tf_op jit(solution)/shard_map/ppermute | solution.py:323
  31.8 19.0 %copy-start = (bf16[128,640]{1,0:T(8,128)(2,1)S(1)}, bf16[128,640]{1,0:T(8,128)(2,1)}, u32[]{:S(2)}) copy-start(bf16[128,640]{1,0:T(8,128)(2,1)} %w_ref.5) | copy-start | bytes 491524
  31.8 19.0 %copy-start.2 = (bf16[24,24,128]{2,1,0:T(8,128)(2,1)S(1)}, bf16[24,24,128]{2,1,0:T(8,128)(2,1)}, u32[]{:S(2)}) copy-start(bf16[24,24,128]{2,1,0:T(8,128)(2,1)} %cot_ref.1) | copy-start | bytes 442372
  31.8 19.0 %copy-start.3 = (bf16[128,128]{1,0:T(8,128)(2,1)S(1)}, bf16[128,128]{1,0:T(8,128)(2,1)}, u32[]{:S(2)}) copy-start(bf16[128,128]{1,0:T(8,128)(2,1)} %wo_ref.1) | copy-start | bytes 98308
  31.8 19.0 %copy-start.4 = (f32[4,128]{1,0:T(4,128)S(1)}, f32[4,128]{1,0:T(4,128)}, u32[]{:S(2)}) copy-start(f32[4,128]{1,0:T(4,128)} %norm_ref.3) | copy-start | bytes 6148
  69.9 2.7 %collective-permute-start.1 = (bf16[128,2,384]{2,1,0:T(2,128)(2,1)S(1)}, bf16[128,2,384]{2,1,0:T(2,128)(2,1)S(1)}, u32[]{:S(2)}, u32[]{:S(2)}) collective-permute-start(bf16[128,2,384]{2,1,0:T(2,128)(2,1)S(1)} %all_to_all.37.src_ref), channel_id=1, source_target_pairs={{0,1},{1,0},{2,3},{3,2},{4,5},{5,4},{6,7},{7,6},{8,9},{9,8},{10,11... | collective-permute-start | bytes 589832 | tf_op jit(solution)/shard_map/ppermute | solution.py:353
  95.2 2.0 %copy-start.1 = (bf16[24,24,128]{2,1,0:T(8,128)(2,1)S(1)}, bf16[24,24,128]{2,1,0:T(8,128)(2,1)}, u32[]{:S(2)}) copy-start(bf16[24,24,128]{2,1,0:T(8,128)(2,1)} %pair_ref.1) | copy-start | bytes 442372
  96.2 2.1 %collective-permute-start.2 = (f32[384,128]{1,0:T(8,128)S(1)}, f32[384,128]{1,0:T(8,128)S(1)}, u32[]{:S(2)}, u32[]{:S(2)}) collective-permute-start(f32[384,128]{1,0:T(8,128)S(1)} %get-tuple-element.38), channel_id=1, source_target_pairs={{0,1},{1,0},{2,3},{3,2},{4,5},{5,4},{6,7},{7,6},{8,9},{9,8},{10,11... | collective-permute-start | bytes 589832 | tf_op jit(solution)/shard_map/ppermute | solution.py:381

commit v8 on v7

--- a/solution.py
+++ b/solution.py
@@ -324,7 +324,7 @@
     part, a_own, b_own = call(
         second_kernel,
         [((384, 256), F32), ((384, 256), BF16), ((2, COLS * WIDE, 256), BF16)],
-        [f32(1024, 128)],
+        [f32(1024 + WIDE, 128)],
         core,
         own,
         scalars=1,
@@ -332,7 +332,7 @@
     (send,) = call(
         second_kernel_sib,
         [thin],
-        [f32(512, 128), bf16(384, 256), bf16(1, COLS * WIDE, 256), f32(CHIPS, POS)],
+        [f32(512 + WIDE, 128), bf16(384, 256), bf16(1, COLS * WIDE, 256), f32(CHIPS, POS)],
         core,
         sib,
         part,
@@ -351,7 +351,7 @@
     )
     own = turn(send)
     sib = lax.ppermute(own, "core", swap)
-    scratch = [bf16(384, 256), f32(512, 128)]
+    scratch = [bf16(384, 256), f32(512 + WIDE, 128)]
     da, db = call(
         fourth_kernel,
         [((384, 256), F32), ((CHIPS // 2, POS), F32)],

time: 133 us -> 133 us (level)
  no operation moved by 1% of the time
where the time goes in v8:
time: 133 us
  blocking collectives  118 us (89%)
  Pallas kernels  10.4 us (8%)
  starting transfers between devices  3.56 us (3%)
    all_to_all x7, blocking collectives, turn(): lax.all_to_all(x, axes, split_axis=0, concat_axis=0, axis_index_groups=gr...  118 us
    pallas_call x12, Pallas kernels, call(): pl.pallas_call(kernel, out_shape=[jax.ShapeDtypeStruct(s, t) for s, t in...  10.4 us
  transfers between devices with their start and end apart: 3, of which 2 were waited for; matrix products, arithmetic and copies ran while one was open for 0% of the time, Pallas kernels for 2%

profile of v8, /device:TPU:1, one launch (start us, length us, event | category | flops | bytes accessed | tf_op | source)
XLA Modules:
  0.0 132.7 jit_solution(6248119980581024068)
XLA Ops:
  0.6 1.7 %shard_map.92 = (bf16[128,2,640]{2,1,0:T(2,128)(2,1)S(1)}, bf16[640,128]{1,0:T(8,128)(2,1)S(1)}) custom-call(bf16[24,24,128]{2,1,0:T(8,128)(2,1)} %pair_ref.1, bf16[128,640]{1,0:T(8,128)(2,1)} %w_ref.5, f32[4,128]{1,0:T(4,128)} %norm_ref.3), custom_call_target="tpu_custom_call" | custom-call | tf_op jit(solution)/shard_map/pallas_call | solution.py:290
  2.4 25.7 %all_to_all.35.src_ref = bf16[128,2,640]{2,1,0:T(2,128)(2,1)S(1)} all-to-all(bf16[128,2,640]{2,1,0:T(2,128)(2,1)S(1)} %get-tuple-element.27), channel_id=1, replica_groups={{138,170,202,234,10,42,74,106,154,186,218,250,26,58,90,122,136,168,200,..., dimensions={0} | all-to-all | bytes 655360 | tf_op jit(solution)/shard_map/all_to_all | solution.py:312
  28.1 1.0 collective-permute-start
  29.1 1.3 shard_map.93
  30.4 0.0 collective-permute-done.src_ref
  30.4 1.4 %shard_map.94 = bf16[128,2,384]{2,1,0:T(2,128)(2,1)S(1)} custom-call(s32[1]{0:T(128)} %bitcast.core_ref, bf16[128,2,640]{2,1,0:T(2,128)(2,1)S(1)} %collective-permute-done.src_ref, f32[384,256]{1,0:T(8,128)S(1)} %get-tuple-element.28.part_ref), custom_call_target="tpu_custom_call" | custom-call | tf_op jit(solution)/shard_map/pallas_call | solution.py:290
  31.8 0.0 copy-start
  31.8 0.0 copy-start.2
  31.8 0.0 copy-start.3
  31.8 0.0 copy-start.4
  31.9 18.9 %all_to_all.36.recv_ref = bf16[128,2,384]{2,1,0:T(2,128)(2,1)S(1)} all-to-all(bf16[128,2,384]{2,1,0:T(2,128)(2,1)S(1)} %shard_map.94), channel_id=1, replica_groups={{138,170,202,234,10,42,74,106,154,186,218,250,26,58,90,122,136,168,200,..., dimensions={0} | all-to-all | bytes 393216 | tf_op jit(solution)/shard_map/all_to_all | solution.py:312
  50.8 0.0 copy-done
  50.8 0.0 copy-done.2
  50.8 0.0 copy-done.3
  50.8 0.0 copy-done.4
  50.8 1.1 shard_map.95
  51.9 18.1 %all_to_all.37.src_ref = bf16[128,2,384]{2,1,0:T(2,128)(2,1)S(1)} all-to-all(bf16[128,2,384]{2,1,0:T(2,128)(2,1)S(1)} %get-tuple-element.30), channel_id=1, replica_groups={{138,170,202,234,10,42,74,106,154,186,218,250,26,58,90,122,136,168,200,..., dimensions={0} | all-to-all | bytes 393216 | tf_op jit(solution)/shard_map/all_to_all | solution.py:312
  70.0 1.5 %collective-permute-start.1 = (bf16[128,2,384]{2,1,0:T(2,128)(2,1)S(1)}, bf16[128,2,384]{2,1,0:T(2,128)(2,1)S(1)}, u32[]{:S(2)}, u32[]{:S(2)}) collective-permute-start(bf16[128,2,384]{2,1,0:T(2,128)(2,1)S(1)} %all_to_all.37.src_ref), channel_id=1, source_target_pairs={{0,1},{1,0},{2,3},{3,2},{4,5},{5,4},{6,7},{7,6},{8,9},{9,8},{10,11... | collective-permute-start | bytes 589832 | tf_op jit(solution)/shard_map/ppermute | solution.py:353
  71.5 1.0 shard_map.96
  72.5 0.1 collective-permute-done.1.src_ref
  72.6 1.3 shard_map.97
  73.8 21.4 %all_to_all.38.recv_ref = bf16[128,2,640]{2,1,0:T(2,128)(2,1)S(1)} all-to-all(bf16[128,2,640]{2,1,0:T(2,128)(2,1)S(1)} %shard_map.97), channel_id=1, replica_groups={{138,170,202,234,10,42,74,106,154,186,218,250,26,58,90,122,136,168,200,..., dimensions={0} | all-to-all | bytes 655360 | tf_op jit(solution)/shard_map/all_to_all | solution.py:312
  95.2 0.0 copy-start.1
  95.3 0.9 shard_map.98
  96.2 1.0 collective-permute-start.2
  97.2 0.0 copy-done.1
  97.2 0.7 shard_map.99
  97.9 0.4 collective-permute-done.2.sib_ref
  98.3 9.9 %all_to_all.39.recv_ref = bf16[16,32,128]{2,1,0:T(8,128)(2,1)S(1)} all-to-all(bf16[16,32,128]{2,1,0:T(8,128)(2,1)S(1)} %shard_map.100), channel_id=1, replica_groups={{10,8,14,12,2,0,6,4,26,24,30,28,18,16,22,20},{11,9,15,13,3,1,7,5,27,25,..., dimensions={0} | all-to-all | bytes 262144 | tf_op jit(solution)/shard_map/all_to_all | solution.py:312
  108.3 9.3 %all_to_all.40.recv_ref = bf16[8,32,128]{2,1,0:T(8,128)(2,1)S(1)} all-to-all(bf16[8,32,128]{2,1,0:T(8,128)(2,1)S(1)} %shard_map.101), channel_id=1, replica_groups={{128,160,192,224,0,32,64,96},{129,161,193,225,1,33,65,97},{130,162,194,..., dimensions={0} | all-to-all | bytes 131072 | tf_op jit(solution)/shard_map/all_to_all | solution.py:312
  117.7 14.2 %all_to_all.41.full_ref = bf16[32,32,128]{2,1,0:T(8,128)(2,1)S(1)} all-to-all(bf16[32,32,128]{2,1,0:T(8,128)(2,1)S(1)} %shard_map.102), channel_id=1, replica_groups={{10,11,8,9,14,15,12,13,2,3,0,1,6,7,4,5,26,27,24,25,30,31,28,29,18,19,16..., dimensions={0} | all-to-all | bytes 524288 | tf_op jit(solution)/shard_map/all_to_all | solution.py:312
  131.8 0.9 shard_map.103
  (3 shorter events, 0.1 us)
Async XLA Ops:
  28.1 2.3 %collective-permute-start = (bf16[128,2,640]{2,1,0:T(2,128)(2,1)S(1)}, bf16[128,2,640]{2,1,0:T(2,128)(2,1)S(1)}, u32[]{:S(2)}, u32[]{:S(2)}) collective-permute-start(bf16[128,2,640]{2,1,0:T(2,128)(2,1)S(1)} %all_to_all.35.src_ref), channel_id=1, source_target_pairs={{0,1},{1,0},{2,3},{3,2},{4,5},{5,4},{6,7},{7,6},{8,9},{9,8},{10,11... | collective-permute-start | bytes 983048 | tf_op jit(solution)/shard_map/ppermute | solution.py:323
  31.8 19.0 %copy-start = (bf16[128,640]{1,0:T(8,128)(2,1)S(1)}, bf16[128,640]{1,0:T(8,128)(2,1)}, u32[]{:S(2)}) copy-start(bf16[128,640]{1,0:T(8,128)(2,1)} %w_ref.5) | copy-start | bytes 491524
  31.8 19.0 %copy-start.2 = (bf16[24,24,128]{2,1,0:T(8,128)(2,1)S(1)}, bf16[24,24,128]{2,1,0:T(8,128)(2,1)}, u32[]{:S(2)}) copy-start(bf16[24,24,128]{2,1,0:T(8,128)(2,1)} %cot_ref.1) | copy-start | bytes 442372
  31.8 19.0 %copy-start.3 = (bf16[128,128]{1,0:T(8,128)(2,1)S(1)}, bf16[128,128]{1,0:T(8,128)(2,1)}, u32[]{:S(2)}) copy-start(bf16[128,128]{1,0:T(8,128)(2,1)} %wo_ref.1) | copy-start | bytes 98308
  31.8 19.0 %copy-start.4 = (f32[4,128]{1,0:T(4,128)S(1)}, f32[4,128]{1,0:T(4,128)}, u32[]{:S(2)}) copy-start(f32[4,128]{1,0:T(4,128)} %norm_ref.3) | copy-start | bytes 6148
  70.0 2.6 %collective-permute-start.1 = (bf16[128,2,384]{2,1,0:T(2,128)(2,1)S(1)}, bf16[128,2,384]{2,1,0:T(2,128)(2,1)S(1)}, u32[]{:S(2)}, u32[]{:S(2)}) collective-permute-start(bf16[128,2,384]{2,1,0:T(2,128)(2,1)S(1)} %all_to_all.37.src_ref), channel_id=1, source_target_pairs={{0,1},{1,0},{2,3},{3,2},{4,5},{5,4},{6,7},{7,6},{8,9},{9,8},{10,11... | collective-permute-start | bytes 589832 | tf_op jit(solution)/shard_map/ppermute | solution.py:353
  95.2 2.0 %copy-start.1 = (bf16[24,24,128]{2,1,0:T(8,128)(2,1)S(1)}, bf16[24,24,128]{2,1,0:T(8,128)(2,1)}, u32[]{:S(2)}) copy-start(bf16[24,24,128]{2,1,0:T(8,128)(2,1)} %pair_ref.1) | copy-start | bytes 442372
  96.2 2.1 %collective-permute-start.2 = (f32[384,128]{1,0:T(8,128)S(1)}, f32[384,128]{1,0:T(8,128)S(1)}, u32[]{:S(2)}, u32[]{:S(2)}) collective-permute-start(f32[384,128]{1,0:T(8,128)S(1)} %get-tuple-element.38), channel_id=1, source_target_pairs={{0,1},{1,0},{2,3},{3,2},{4,5},{5,4},{6,7},{7,6},{8,9},{9,8},{10,11... | collective-permute-start | bytes 589832 | tf_op jit(solution)/shard_map/ppermute | solution.py:381

commit v9 on v8

--- a/solution.py
+++ b/solution.py
@@ -231,7 +231,13 @@
     send_ref[:, 0, :] = scr[...].astype(BF16)
 
 
-def fifth_kernel(core_ref, recv_ref, zn_ref, w_ref, dp4_ref, gwo_ref, keep_ref, give_ref, dp_ref, scr):
+def half_of(half, dp_ref, zn_ref, gwo_ref):
+    grads = dot(dp_ref[pl.ds(pl.multiple_of(3 * C * half, 3 * C), 3 * C), :], zn_ref[...], 1, 0)
+    last = grads[2 * C :] + jnp.where(half == 1, gwo_ref[...], 0.0)
+    return jnp.concatenate([grads[: 2 * C], last], axis=0)
+
+
+def fifth_kernel(core_ref, recv_ref, zn_ref, w_ref, dp4_ref, gwo_ref, give_ref, dp_ref):
     core = core_ref[0]
     zn = zn_ref[...]
     for m in range(2):
@@ -241,17 +247,14 @@
         gs = grad * s
         dp_ref[2 * m * C : (2 * m + 1) * C, :] = gs.astype(BF16)
         dp_ref[(2 * m + 1) * C : (2 * m + 2) * C, :] = (gs * p[:C] * (1.0 - s)).astype(BF16)
-    dp_ref[4 * C :, :] = dp4_ref[...]
-    grads = dot(dp_ref[...], zn, 1, 0)
-    scr[0] = grads[: 3 * C]
-    scr[1, : 2 * C, :] = grads[3 * C :]
-    scr[1, 2 * C :, :] = gwo_ref[...]
-    keep_ref[...] = scr[core]
-    give_ref[...] = scr[1 - core]
-
-
-def sixth_kernel(dp_ref, pair_ref, w_ref, mid_ref, norm_ref, gpair_ref, sums_ref):
-    dzn = dot(w_ref[...], dp_ref[...], 1, 0).T
+    dp_ref[4 * C : 5 * C, :] = dp4_ref[...]
+    dp_ref[5 * C :, :] = jnp.zeros((C, POS), BF16)
+    give_ref[...] = half_of(1 - core, dp_ref, zn_ref, gwo_ref).astype(BF16)
+
+
+def sixth_kernel(core_ref, dp_ref, zn_ref, gwo_ref, pair_ref, w_ref, mid_ref, norm_ref, gpair_ref, sums_ref, keep_ref):
+    keep_ref[...] = half_of(core_ref[0], dp_ref, zn_ref, gwo_ref)
+    dzn = dot(w_ref[...], dp_ref[: 5 * C, :], 1, 0).T
     hat, rstd = norm_lanes(padded(pair_ref[...]))
     e = dzn * norm_ref[0:1, :]
     back = rstd * (e - jnp.mean(e, axis=-1, keepdims=True) - hat * jnp.mean(e * hat, axis=-1, keepdims=True))
@@ -262,7 +265,7 @@
 
 
 def join_kernel(keep_ref, sib_ref, sums_ref, send_ref):
-    grads = (keep_ref[...] + sib_ref[...]).reshape(PLANE // 2, 24, C)
+    grads = (keep_ref[...] + sib_ref[...].astype(F32)).reshape(PLANE // 2, 24, C)
     sums = jnp.concatenate([sums_ref[...][None], jnp.zeros((PLANE // 2 - 1, 8, C), F32)], axis=0)
     send_ref[...] = jnp.concatenate([grads, sums], axis=1).astype(BF16)
 
@@ -365,11 +368,10 @@
     (send,) = call(
         fourth_kernel_sib, [wide], scratch + [f32(CHIPS, POS)], core, sib, a_own, b_own, da, db, scalars=1
     )
-    half = ((3 * C, C), F32)
-    keep, give, dp = call(
+    give, dp = call(
         fifth_kernel,
-        [half, half, ((5 * C, POS), BF16)],
-        [f32(2, 3 * C, C)],
+        [((3 * C, C), BF16), ((6 * C, POS), BF16)],
+        [],
         core,
         turn(send),
         zn,
@@ -379,8 +381,19 @@
         scalars=1,
     )
     sib = lax.ppermute(give, "core", swap)
-    grad_pair, sums = call(
-        sixth_kernel, [((TILE, TILE, C), BF16), ((8, C), F32)], [], dp, pair, w_in, mid, norm_params
+    grad_pair, sums, keep = call(
+        sixth_kernel,
+        [((TILE, TILE, C), BF16), ((8, C), F32), ((3 * C, C), F32)],
+        [],
+        core,
+        dp,
+        zn,
+        gwo,
+        pair,
+        w_in,
+        mid,
+        norm_params,
+        scalars=1,
     )
     (send,) = call(join_kernel, [((PLANE // 2, 32, C), BF16)], [], keep, sib, sums)
     send = turn(send, PLANE_AXES[:3])

time: 133 us -> 133 us (level)
  no operation moved by 1% of the time
where the time goes in v9:
time: 133 us
  blocking collectives  117 us (88%)
  Pallas kernels  10.4 us (8%)
  starting transfers between devices  3.62 us (3%)
    all_to_all x7, blocking collectives, turn(): lax.all_to_all(x, axes, split_axis=0, concat_axis=0, axis_index_groups=gr...  117 us
    pallas_call x12, Pallas kernels, call(): pl.pallas_call(kernel, out_shape=[jax.ShapeDtypeStruct(s, t) for s, t in...  10.4 us
  transfers between devices with their start and end apart: 3, of which 2 were waited for; matrix products, arithmetic and copies ran while one was open for 0% of the time, Pallas kernels for 2%

profile of v9, /device:TPU:1, one launch (start us, length us, event | category | flops | bytes accessed | tf_op | source)
XLA Modules:
  0.0 132.5 jit_solution(3842176266819627235)
XLA Ops:
  0.6 1.7 %shard_map.92 = (bf16[128,2,640]{2,1,0:T(2,128)(2,1)S(1)}, bf16[640,128]{1,0:T(8,128)(2,1)S(1)}) custom-call(bf16[24,24,128]{2,1,0:T(8,128)(2,1)} %pair_ref.1, bf16[128,640]{1,0:T(8,128)(2,1)} %w_ref.5, f32[4,128]{1,0:T(4,128)} %norm_ref.3), custom_call_target="tpu_custom_call" | custom-call | tf_op jit(solution)/shard_map/pallas_call | solution.py:293
  2.4 25.7 %all_to_all.35.src_ref = bf16[128,2,640]{2,1,0:T(2,128)(2,1)S(1)} all-to-all(bf16[128,2,640]{2,1,0:T(2,128)(2,1)S(1)} %get-tuple-element.27), channel_id=1, replica_groups={{138,170,202,234,10,42,74,106,154,186,218,250,26,58,90,122,136,168,200,..., dimensions={0} | all-to-all | bytes 655360 | tf_op jit(solution)/shard_map/all_to_all | solution.py:315
  28.1 1.0 collective-permute-start
  29.1 1.3 shard_map.93
  30.4 0.0 collective-permute-done.src_ref
  30.4 1.4 %shard_map.94 = bf16[128,2,384]{2,1,0:T(2,128)(2,1)S(1)} custom-call(s32[1]{0:T(128)} %bitcast.core_ref, bf16[128,2,640]{2,1,0:T(2,128)(2,1)S(1)} %collective-permute-done.src_ref, f32[384,256]{1,0:T(8,128)S(1)} %get-tuple-element.28.part_ref), custom_call_target="tpu_custom_call" | custom-call | tf_op jit(solution)/shard_map/pallas_call | solution.py:293
  31.8 0.0 copy-start
  31.8 0.0 copy-start.2
  31.8 0.0 copy-start.3
  31.8 0.0 copy-start.4
  31.9 18.9 %all_to_all.36.recv_ref = bf16[128,2,384]{2,1,0:T(2,128)(2,1)S(1)} all-to-all(bf16[128,2,384]{2,1,0:T(2,128)(2,1)S(1)} %shard_map.94), channel_id=1, replica_groups={{138,170,202,234,10,42,74,106,154,186,218,250,26,58,90,122,136,168,200,..., dimensions={0} | all-to-all | bytes 393216 | tf_op jit(solution)/shard_map/all_to_all | solution.py:315
  50.8 0.0 copy-done
  50.8 0.0 copy-done.2
  50.8 0.0 copy-done.3
  50.8 0.0 copy-done.4
  50.8 1.1 shard_map.95
  51.9 18.0 %all_to_all.37.src_ref = bf16[128,2,384]{2,1,0:T(2,128)(2,1)S(1)} all-to-all(bf16[128,2,384]{2,1,0:T(2,128)(2,1)S(1)} %get-tuple-element.30), channel_id=1, replica_groups={{138,170,202,234,10,42,74,106,154,186,218,250,26,58,90,122,136,168,200,..., dimensions={0} | all-to-all | bytes 393216 | tf_op jit(solution)/shard_map/all_to_all | solution.py:315
  69.9 1.6 %collective-permute-start.1 = (bf16[128,2,384]{2,1,0:T(2,128)(2,1)S(1)}, bf16[128,2,384]{2,1,0:T(2,128)(2,1)S(1)}, u32[]{:S(2)}, u32[]{:S(2)}) collective-permute-start(bf16[128,2,384]{2,1,0:T(2,128)(2,1)S(1)} %all_to_all.37.src_ref), channel_id=1, source_target_pairs={{0,1},{1,0},{2,3},{3,2},{4,5},{5,4},{6,7},{7,6},{8,9},{9,8},{10,11... | collective-permute-start | bytes 589832 | tf_op jit(solution)/shard_map/ppermute | solution.py:356
  71.5 1.0 shard_map.96
  72.5 0.1 collective-permute-done.1.src_ref
  72.6 1.3 shard_map.97
  73.8 21.4 %all_to_all.38.recv_ref = bf16[128,2,640]{2,1,0:T(2,128)(2,1)S(1)} all-to-all(bf16[128,2,640]{2,1,0:T(2,128)(2,1)S(1)} %shard_map.97), channel_id=1, replica_groups={{138,170,202,234,10,42,74,106,154,186,218,250,26,58,90,122,136,168,200,..., dimensions={0} | all-to-all | bytes 655360 | tf_op jit(solution)/shard_map/all_to_all | solution.py:315
  95.2 0.0 copy-start.1
  95.2 0.9 shard_map.98
  96.2 1.0 collective-permute-start.2
  97.2 0.0 copy-done.1
  97.2 0.7 shard_map.99
  97.9 0.3 collective-permute-done.2.sib_ref
  98.2 9.9 %all_to_all.39.recv_ref = bf16[16,32,128]{2,1,0:T(8,128)(2,1)S(1)} all-to-all(bf16[16,32,128]{2,1,0:T(8,128)(2,1)S(1)} %shard_map.100), channel_id=1, replica_groups={{10,8,14,12,2,0,6,4,26,24,30,28,18,16,22,20},{11,9,15,13,3,1,7,5,27,25,..., dimensions={0} | all-to-all | bytes 262144 | tf_op jit(solution)/shard_map/all_to_all | solution.py:315
  108.1 9.3 %all_to_all.40.recv_ref = bf16[8,32,128]{2,1,0:T(8,128)(2,1)S(1)} all-to-all(bf16[8,32,128]{2,1,0:T(8,128)(2,1)S(1)} %shard_map.101), channel_id=1, replica_groups={{128,160,192,224,0,32,64,96},{129,161,193,225,1,33,65,97},{130,162,194,..., dimensions={0} | all-to-all | bytes 131072 | tf_op jit(solution)/shard_map/all_to_all | solution.py:315
  117.5 14.1 %all_to_all.41.full_ref = bf16[32,32,128]{2,1,0:T(8,128)(2,1)S(1)} all-to-all(bf16[32,32,128]{2,1,0:T(8,128)(2,1)S(1)} %shard_map.102), channel_id=1, replica_groups={{10,11,8,9,14,15,12,13,2,3,0,1,6,7,4,5,26,27,24,25,30,31,28,29,18,19,16..., dimensions={0} | all-to-all | bytes 524288 | tf_op jit(solution)/shard_map/all_to_all | solution.py:315
  131.6 0.9 shard_map.103
  (3 shorter events, 0.1 us)
Async XLA Ops:
  28.1 2.3 %collective-permute-start = (bf16[128,2,640]{2,1,0:T(2,128)(2,1)S(1)}, bf16[128,2,640]{2,1,0:T(2,128)(2,1)S(1)}, u32[]{:S(2)}, u32[]{:S(2)}) collective-permute-start(bf16[128,2,640]{2,1,0:T(2,128)(2,1)S(1)} %all_to_all.35.src_ref), channel_id=1, source_target_pairs={{0,1},{1,0},{2,3},{3,2},{4,5},{5,4},{6,7},{7,6},{8,9},{9,8},{10,11... | collective-permute-start | bytes 983048 | tf_op jit(solution)/shard_map/ppermute | solution.py:326
  31.8 19.0 %copy-start = (bf16[128,640]{1,0:T(8,128)(2,1)S(1)}, bf16[128,640]{1,0:T(8,128)(2,1)}, u32[]{:S(2)}) copy-start(bf16[128,640]{1,0:T(8,128)(2,1)} %w_ref.5) | copy-start | bytes 491524
  31.8 19.0 %copy-start.2 = (bf16[24,24,128]{2,1,0:T(8,128)(2,1)S(1)}, bf16[24,24,128]{2,1,0:T(8,128)(2,1)}, u32[]{:S(2)}) copy-start(bf16[24,24,128]{2,1,0:T(8,128)(2,1)} %cot_ref.1) | copy-start | bytes 442372
  31.8 19.0 %copy-start.3 = (bf16[128,128]{1,0:T(8,128)(2,1)S(1)}, bf16[128,128]{1,0:T(8,128)(2,1)}, u32[]{:S(2)}) copy-start(bf16[128,128]{1,0:T(8,128)(2,1)} %wo_ref.1) | copy-start | bytes 98308
  31.8 19.0 %copy-start.4 = (f32[4,128]{1,0:T(4,128)S(1)}, f32[4,128]{1,0:T(4,128)}, u32[]{:S(2)}) copy-start(f32[4,128]{1,0:T(4,128)} %norm_ref.3) | copy-start | bytes 6148
  69.9 2.7 %collective-permute-start.1 = (bf16[128,2,384]{2,1,0:T(2,128)(2,1)S(1)}, bf16[128,2,384]{2,1,0:T(2,128)(2,1)S(1)}, u32[]{:S(2)}, u32[]{:S(2)}) collective-permute-start(bf16[128,2,384]{2,1,0:T(2,128)(2,1)S(1)} %all_to_all.37.src_ref), channel_id=1, source_target_pairs={{0,1},{1,0},{2,3},{3,2},{4,5},{5,4},{6,7},{7,6},{8,9},{9,8},{10,11... | collective-permute-start | bytes 589832 | tf_op jit(solution)/shard_map/ppermute | solution.py:356
  95.2 2.0 %copy-start.1 = (bf16[24,24,128]{2,1,0:T(8,128)(2,1)S(1)}, bf16[24,24,128]{2,1,0:T(8,128)(2,1)}, u32[]{:S(2)}) copy-start(bf16[24,24,128]{2,1,0:T(8,128)(2,1)} %pair_ref.1) | copy-start | bytes 442372
  96.2 2.0 %collective-permute-start.2 = (bf16[384,128]{1,0:T(8,128)(2,1)S(1)}, bf16[384,128]{1,0:T(8,128)(2,1)S(1)}, u32[]{:S(2)}, u32[]{:S(2)}) collective-permute-start(bf16[384,128]{1,0:T(8,128)(2,1)S(1)} %get-tuple-element.40), channel_id=1, source_target_pairs={{0,1},{1,0},{2,3},{3,2},{4,5},{5,4},{6,7},{7,6},{8,9},{9,8},{10,11... | collective-permute-start | bytes 294920 | tf_op jit(solution)/shard_map/ppermute | solution.py:383

commit v10 on v8

--- a/solution.py
+++ b/solution.py
@@ -22,7 +22,7 @@
 PLANE = 32
 CHIP_AXES = ("x", "yh", "yl", "z")
 PLANE_AXES = ("yl", "x", "yh", "core")
-FLIPS = {"x": 2, "yh": 1, "z": 4}
+FLIPS = {"x": 2, "yh": 1, "z": 5}
 
 
 def dot(x, y, cx, cy):
@@ -123,11 +123,6 @@
                 scr[ROWS * (4 * g + u) : ROWS * (4 * g + u + 1), t * 128 : (t + 1) * 128] = o
 
 
-def swap_blocks(val):
-    pairs = val.reshape(-1, 2, WIDE, val.shape[1])
-    return jnp.concatenate([pairs[:, 1:], pairs[:, :1]], axis=1).reshape(val.shape)
-
-
 def gather_b(src, first, rows, bscr, b_dst):
     for n in range(2 * rows):
         bscr[pl.ds(n * WIDE + TILE, WIDE - TILE), :] = jnp.zeros((WIDE - TILE, 128), F32)
@@ -137,7 +132,7 @@
             parts = [block(src, 4 * g + u, 1, t, first, rows) for u in range(4)]
             for j, o in zip(rows_of(t), spread_turn(parts, wins, t)):
                 bscr[pl.ds(rows * WIDE * g + j, rows, stride=WIDE), :] = o
-        part = swap_blocks(bscr[rows * WIDE * g : rows * WIDE * (g + 1), :]).astype(BF16)
+        part = bscr[rows * WIDE * g : rows * WIDE * (g + 1), :].astype(BF16)
         b_dst[:, :, g * 128 : (g + 1) * 128] = part.reshape(rows // COLS, COLS * WIDE, 128)
 
 
@@ -200,7 +195,7 @@
     dx = d_ref[...]
     db = dot(dx, a_ref[...], 0, 0)
     for g in range(2):
-        dbscr[pl.ds(256 * g, 256), :] = swap_blocks(db[:, g * 128 : (g + 1) * 128])
+        dbscr[pl.ds(256 * g, 256), :] = db[:, g * 128 : (g + 1) * 128]
     wins = windows(COLS)
     for g in range(2):
         for t in range(TROWS):

time: 133 us -> 133 us (level)
  blocking collectives: 118 us -> 114 us
  starting transfers between devices: 3.56 us -> 6.2 us
    all_to_all x7, blocking collectives: 118 us -> 114 us  [turn(): lax.all_to_all(x, axes, split_axis=0, concat_axis=0, axis_index_groups=gr...]
    ppermute x2, starting transfers between devices: 2.53 us -> 4.61 us  [shards(): sib = lax.ppermute(own, 'core', swap)]
where the time goes in v10:
time: 133 us; the launch traced here: 132 us
  blocking collectives  114 us (86%)
  Pallas kernels  10.4 us (8%)
  starting transfers between devices  6.2 us (5%)
    all_to_all x7, blocking collectives, turn(): lax.all_to_all(x, axes, split_axis=0, concat_axis=0, axis_index_groups=gr...  114 us
    pallas_call x12, Pallas kernels, call(): pl.pallas_call(kernel, out_shape=[jax.ShapeDtypeStruct(s, t) for s, t in...  10.4 us
    ppermute x2, starting transfers between devices, shards(): sib = lax.ppermute(own, 'core', swap)  4.61 us
  transfers between devices with their start and end apart: 3, of which 2 were waited for; matrix products, arithmetic and copies ran while one was open for 0% of the time, Pallas kernels for 2%

profile of v10, /device:TPU:1, one launch (start us, length us, event | category | flops | bytes accessed | tf_op | source)
XLA Modules:
  0.0 132.3 jit_solution(13964568227094949090)
XLA Ops:
  0.6 1.7 %shard_map.92 = (bf16[128,2,640]{2,1,0:T(2,128)(2,1)S(1)}, bf16[640,128]{1,0:T(8,128)(2,1)S(1)}) custom-call(bf16[24,24,128]{2,1,0:T(8,128)(2,1)} %pair_ref.1, bf16[128,640]{1,0:T(8,128)(2,1)} %w_ref.5, f32[4,128]{1,0:T(4,128)} %norm_ref.3), custom_call_target="tpu_custom_call" | custom-call | tf_op jit(solution)/shard_map/pallas_call | solution.py:285
  2.4 24.5 %all_to_all.35.src_ref = bf16[128,2,640]{2,1,0:T(2,128)(2,1)S(1)} all-to-all(bf16[128,2,640]{2,1,0:T(2,128)(2,1)S(1)} %get-tuple-element.27), channel_id=1, replica_groups={{170,138,234,202,42,10,106,74,186,154,250,218,58,26,122,90,168,136,232,..., dimensions={0} | all-to-all | bytes 655360 | tf_op jit(solution)/shard_map/all_to_all | solution.py:307
  26.9 1.9 %collective-permute-start = (bf16[128,2,640]{2,1,0:T(2,128)(2,1)S(1)}, bf16[128,2,640]{2,1,0:T(2,128)(2,1)S(1)}, u32[]{:S(2)}, u32[]{:S(2)}) collective-permute-start(bf16[128,2,640]{2,1,0:T(2,128)(2,1)S(1)} %all_to_all.35.src_ref), channel_id=1, source_target_pairs={{0,1},{1,0},{2,3},{3,2},{4,5},{5,4},{6,7},{7,6},{8,9},{9,8},{10,11... | collective-permute-start | bytes 983048 | tf_op jit(solution)/shard_map/ppermute | solution.py:318
  28.8 1.3 shard_map.93
  30.1 0.0 collective-permute-done.src_ref
  30.1 1.4 %shard_map.94 = bf16[128,2,384]{2,1,0:T(2,128)(2,1)S(1)} custom-call(s32[1]{0:T(128)} %bitcast.core_ref, bf16[128,2,640]{2,1,0:T(2,128)(2,1)S(1)} %collective-permute-done.src_ref, f32[384,256]{1,0:T(8,128)S(1)} %get-tuple-element.28.part_ref), custom_call_target="tpu_custom_call" | custom-call | tf_op jit(solution)/shard_map/pallas_call | solution.py:285
  31.6 0.0 copy-start
  31.6 0.0 copy-start.2
  31.6 0.0 copy-start.3
  31.6 0.0 copy-start.4
  31.6 18.7 %all_to_all.36.recv_ref = bf16[128,2,384]{2,1,0:T(2,128)(2,1)S(1)} all-to-all(bf16[128,2,384]{2,1,0:T(2,128)(2,1)S(1)} %shard_map.94), channel_id=1, replica_groups={{170,138,234,202,42,10,106,74,186,154,250,218,58,26,122,90,168,136,232,..., dimensions={0} | all-to-all | bytes 393216 | tf_op jit(solution)/shard_map/all_to_all | solution.py:307
  50.3 0.0 copy-done
  50.3 0.0 copy-done.2
  50.3 0.0 copy-done.3
  50.3 0.0 copy-done.4
  50.4 1.1 shard_map.95
  51.5 17.1 %all_to_all.37.src_ref = bf16[128,2,384]{2,1,0:T(2,128)(2,1)S(1)} all-to-all(bf16[128,2,384]{2,1,0:T(2,128)(2,1)S(1)} %get-tuple-element.30), channel_id=1, replica_groups={{170,138,234,202,42,10,106,74,186,154,250,218,58,26,122,90,168,136,232,..., dimensions={0} | all-to-all | bytes 393216 | tf_op jit(solution)/shard_map/all_to_all | solution.py:307
  68.6 2.7 %collective-permute-start.1 = (bf16[128,2,384]{2,1,0:T(2,128)(2,1)S(1)}, bf16[128,2,384]{2,1,0:T(2,128)(2,1)S(1)}, u32[]{:S(2)}, u32[]{:S(2)}) collective-permute-start(bf16[128,2,384]{2,1,0:T(2,128)(2,1)S(1)} %all_to_all.37.src_ref), channel_id=1, source_target_pairs={{0,1},{1,0},{2,3},{3,2},{4,5},{5,4},{6,7},{7,6},{8,9},{9,8},{10,11... | collective-permute-start | bytes 589832 | tf_op jit(solution)/shard_map/ppermute | solution.py:348
  71.2 1.0 shard_map.96
  72.2 0.1 collective-permute-done.1.src_ref
  72.3 1.3 shard_map.97
  73.6 20.5 %all_to_all.38.recv_ref = bf16[128,2,640]{2,1,0:T(2,128)(2,1)S(1)} all-to-all(bf16[128,2,640]{2,1,0:T(2,128)(2,1)S(1)} %shard_map.97), channel_id=1, replica_groups={{170,138,234,202,42,10,106,74,186,154,250,218,58,26,122,90,168,136,232,..., dimensions={0} | all-to-all | bytes 655360 | tf_op jit(solution)/shard_map/all_to_all | solution.py:307
  94.0 0.0 copy-start.1
  94.0 0.9 shard_map.98
  95.0 1.6 %collective-permute-start.2 = (f32[384,128]{1,0:T(8,128)S(1)}, f32[384,128]{1,0:T(8,128)S(1)}, u32[]{:S(2)}, u32[]{:S(2)}) collective-permute-start(f32[384,128]{1,0:T(8,128)S(1)} %get-tuple-element.38), channel_id=1, source_target_pairs={{0,1},{1,0},{2,3},{3,2},{4,5},{5,4},{6,7},{7,6},{8,9},{9,8},{10,11... | collective-permute-start | bytes 589832 | tf_op jit(solution)/shard_map/ppermute | solution.py:376
  96.6 0.0 copy-done.1
  96.6 0.7 shard_map.99
  97.2 0.4 collective-permute-done.2.sib_ref
  97.7 10.0 %all_to_all.39.recv_ref = bf16[16,32,128]{2,1,0:T(8,128)(2,1)S(1)} all-to-all(bf16[16,32,128]{2,1,0:T(8,128)(2,1)S(1)} %shard_map.100), channel_id=1, replica_groups={{10,8,14,12,2,0,6,4,26,24,30,28,18,16,22,20},{11,9,15,13,3,1,7,5,27,25,..., dimensions={0} | all-to-all | bytes 262144 | tf_op jit(solution)/shard_map/all_to_all | solution.py:307
  107.7 9.5 %all_to_all.40.recv_ref = bf16[8,32,128]{2,1,0:T(8,128)(2,1)S(1)} all-to-all(bf16[8,32,128]{2,1,0:T(8,128)(2,1)S(1)} %shard_map.101), channel_id=1, replica_groups={{160,128,224,192,32,0,96,64},{161,129,225,193,33,1,97,65},{162,130,226,..., dimensions={0} | all-to-all | bytes 131072 | tf_op jit(solution)/shard_map/all_to_all | solution.py:307
  117.2 14.2 %all_to_all.41.full_ref = bf16[32,32,128]{2,1,0:T(8,128)(2,1)S(1)} all-to-all(bf16[32,32,128]{2,1,0:T(8,128)(2,1)S(1)} %shard_map.102), channel_id=1, replica_groups={{10,11,8,9,14,15,12,13,2,3,0,1,6,7,4,5,26,27,24,25,30,31,28,29,18,19,16..., dimensions={0} | all-to-all | bytes 524288 | tf_op jit(solution)/shard_map/all_to_all | solution.py:307
  131.4 0.9 shard_map.103
  (3 shorter events, 0.1 us)
Async XLA Ops:
  26.9 3.3 %collective-permute-start = (bf16[128,2,640]{2,1,0:T(2,128)(2,1)S(1)}, bf16[128,2,640]{2,1,0:T(2,128)(2,1)S(1)}, u32[]{:S(2)}, u32[]{:S(2)}) collective-permute-start(bf16[128,2,640]{2,1,0:T(2,128)(2,1)S(1)} %all_to_all.35.src_ref), channel_id=1, source_target_pairs={{0,1},{1,0},{2,3},{3,2},{4,5},{5,4},{6,7},{7,6},{8,9},{9,8},{10,11... | collective-permute-start | bytes 983048 | tf_op jit(solution)/shard_map/ppermute | solution.py:318
  31.6 18.8 %copy-start = (bf16[128,640]{1,0:T(8,128)(2,1)S(1)}, bf16[128,640]{1,0:T(8,128)(2,1)}, u32[]{:S(2)}) copy-start(bf16[128,640]{1,0:T(8,128)(2,1)} %w_ref.5) | copy-start | bytes 491524
  31.6 18.8 %copy-start.2 = (bf16[24,24,128]{2,1,0:T(8,128)(2,1)S(1)}, bf16[24,24,128]{2,1,0:T(8,128)(2,1)}, u32[]{:S(2)}) copy-start(bf16[24,24,128]{2,1,0:T(8,128)(2,1)} %cot_ref.1) | copy-start | bytes 442372
  31.6 18.8 %copy-start.3 = (bf16[128,128]{1,0:T(8,128)(2,1)S(1)}, bf16[128,128]{1,0:T(8,128)(2,1)}, u32[]{:S(2)}) copy-start(bf16[128,128]{1,0:T(8,128)(2,1)} %wo_ref.1) | copy-start | bytes 98308
  31.6 18.7 %copy-start.4 = (f32[4,128]{1,0:T(4,128)S(1)}, f32[4,128]{1,0:T(4,128)}, u32[]{:S(2)}) copy-start(f32[4,128]{1,0:T(4,128)} %norm_ref.3) | copy-start | bytes 6148
  68.6 3.7 %collective-permute-start.1 = (bf16[128,2,384]{2,1,0:T(2,128)(2,1)S(1)}, bf16[128,2,384]{2,1,0:T(2,128)(2,1)S(1)}, u32[]{:S(2)}, u32[]{:S(2)}) collective-permute-start(bf16[128,2,384]{2,1,0:T(2,128)(2,1)S(1)} %all_to_all.37.src_ref), channel_id=1, source_target_pairs={{0,1},{1,0},{2,3},{3,2},{4,5},{5,4},{6,7},{7,6},{8,9},{9,8},{10,11... | collective-permute-start | bytes 589832 | tf_op jit(solution)/shard_map/ppermute | solution.py:348
  94.0 2.5 %copy-start.1 = (bf16[24,24,128]{2,1,0:T(8,128)(2,1)S(1)}, bf16[24,24,128]{2,1,0:T(8,128)(2,1)}, u32[]{:S(2)}) copy-start(bf16[24,24,128]{2,1,0:T(8,128)(2,1)} %pair_ref.1) | copy-start | bytes 442372
  95.0 2.7 %collective-permute-start.2 = (f32[384,128]{1,0:T(8,128)S(1)}, f32[384,128]{1,0:T(8,128)S(1)}, u32[]{:S(2)}, u32[]{:S(2)}) collective-permute-start(f32[384,128]{1,0:T(8,128)S(1)} %get-tuple-element.38), channel_id=1, source_target_pairs={{0,1},{1,0},{2,3},{3,2},{4,5},{5,4},{6,7},{7,6},{8,9},{9,8},{10,11... | collective-permute-start | bytes 589832 | tf_op jit(solution)/shard_map/ppermute | solution.py:376
